TPU v7x, 32 devices: a whole 2x2x4 slice. The times are simulated.
32 devices in a mesh: dp: 16 (over z, x, core), fsdp: 2 (over y).
Axes of the slice: x: 2, y: 2, z: 4, core: 2. Of those that a mesh axis runs over, the one named last changes fastest.
Arguments:
- tokens: bfloat16 [32, 768, 768], P(('dp', 'fsdp')), may hold values from -6 to 6
- cond: bfloat16 [32, 768, 384], P(('dp', 'fsdp')), may hold values from -6 to 6
- pair: bfloat16 [2, 768, 768, 128], P(None, ('dp', 'fsdp')), may hold values from -6 to 6
- counts: int32 [2], replicated, may hold values from 385 to 768, as said below
- owner: int32 [32], replicated, may hold values from 0 to 1
- out_grad: bfloat16 [32, 768, 768], P(('dp', 'fsdp')), may hold values from -6 to 6
- cond_gain: float32 [384], replicated, may hold values from 0.1 to 1.9
- cond_weight: bfloat16 [384, 4608], P('fsdp'), may hold values from -0.3125 to 0.3125
- cond_bias: float32 [4608], replicated, may hold values from -3 to 3
- qkvg_weight: bfloat16 [768, 3072], P('fsdp'), may hold values from -0.21875 to 0.21875
- query_bias: float32 [768], replicated, may hold values from -3 to 3
- out_weight: bfloat16 [768, 768], P('fsdp'), may hold values from -4 to 4
- pair_gain: float32 [128], replicated, may hold values from 0.1 to 1.9
- pair_weight: bfloat16 [128, 16], replicated, may hold values from -0.5 to 0.5
- up_weight: bfloat16 [768, 3072], P('fsdp'), may hold values from -0.21875 to 0.21875
- down_weight: bfloat16 [1536, 768], P('fsdp'), may hold values from -0.15625 to 0.15625
Outputs:
- block_out: float32 [32, 768, 768], P(('dp', 'fsdp'))
- tokens_grad: float32 [32, 768, 768], P(('dp', 'fsdp'))
- cond_grad: float32 [32, 768, 384], P(('dp', 'fsdp'))
- pair_grad: float32 [2, 768, 768, 128], P(None, ('dp', 'fsdp'))
- cond_gain_grad: float32 [384], replicated
- cond_weight_grad: float32 [384, 4608], P('fsdp')
- cond_bias_grad: float32 [4608], replicated
- qkvg_weight_grad: float32 [768, 3072], P('fsdp')
- query_bias_grad: float32 [768], replicated
- out_weight_grad: float32 [768, 768], P('fsdp')
- pair_gain_grad: float32 [128], replicated
- pair_weight_grad: float32 [128, 16], replicated
- up_weight_grad: float32 [768, 3072], P('fsdp')
- down_weight_grad: float32 [1536, 768], P('fsdp')
Inputs may be any that keep to these rules, and one draw needn't show every extreme that they name: One of the two counts is exactly 768 in every draw, which one drawn from the seed; the other lies above 384.
All inputs are finite; a program needn't handle non-finite values.
Results may differ from a plain program's by a relative error of at most 0.017.
Values may be sent and summed in bfloat16 or wider, within the bound.
A program may use at most 320 MiB of HBM per device.

v0:
```python
import math

import jax
import jax.numpy as jnp
from jax import lax
from jax.sharding import PartitionSpec as P

norm_eps = 1e-05
mask_fill = -1000000000.0


def normalize(values):
    mean_value = jnp.mean(values, axis=-1, keepdims=True)
    centered = values - mean_value
    variance = jnp.mean(centered * centered, axis=-1, keepdims=True)
    return centered * lax.rsqrt(variance + norm_eps)


def scaled_norm(values, gain_vector):
    return normalize(values) * gain_vector


def modulate(modul, token_norm):
    scale_one, shift_one, gate_one, scale_two, shift_two, gate_two = jnp.split(modul, 6, axis=-1)
    first = jax.nn.sigmoid(scale_one) * token_norm + shift_one
    second = jax.nn.sigmoid(scale_two) * token_norm + shift_two
    return (first, second, jax.nn.sigmoid(gate_one), jax.nn.sigmoid(gate_two))


def swish_product(hidden):
    h_gate, h_up = jnp.split(hidden, 2, axis=-1)
    return jax.nn.silu(h_gate) * h_up


def left_product(left_side, right_side):
    return lax.dot_general(
        left_side, right_side, (((0,), (0,)), ((), ())), preferred_element_type=jnp.float32
    )


def right_product(left_side, right_side):
    return lax.dot_general(
        left_side, right_side, (((1,), (1,)), ((), ())), preferred_element_type=jnp.float32
    )


def sample_pass(token_rows, cond_rows, cotangent_rows, mask_rows, bias_rows, matrices, vectors):
    full_cond, full_qkvg, full_out, full_up, full_down = matrices
    cond_gain, cond_bias, query_bias = vectors
    seq_length, model_width = token_rows.shape
    head_count = bias_rows.shape[1]
    head_size = model_width // head_count
    inverse_root = 1.0 / math.sqrt(head_size)
    head_shape = (seq_length, head_count, head_size)
    cond_norm, cond_back = jax.vjp(scaled_norm, cond_rows.astype(jnp.float32), cond_gain)
    cond_low = cond_norm.astype(jnp.bfloat16)
    modul = jnp.dot(cond_low, full_cond, preferred_element_type=jnp.float32) + cond_bias
    token_norm, token_back = jax.vjp(normalize, token_rows.astype(jnp.float32))
    (first, second, gate_one, gate_two), modul_back = jax.vjp(modulate, modul, token_norm)
    first_low = first.astype(jnp.bfloat16)
    second_low = second.astype(jnp.bfloat16)
    projected = jnp.dot(first_low, full_qkvg, preferred_element_type=jnp.float32)
    part_q, part_k, part_v, part_g = jnp.split(projected, 4, axis=-1)
    queries = ((part_q + query_bias) * inverse_root).astype(jnp.bfloat16).reshape(head_shape)
    key_heads = part_k.astype(jnp.bfloat16).reshape(head_shape)
    value_heads = part_v.astype(jnp.bfloat16).reshape(head_shape)
    gate_sig = jax.nn.sigmoid(part_g)
    score_extra = bias_rows.astype(jnp.float32) + mask_rows[None, None, :]
    scores = (
        jnp.einsum("qhd,khd->qhk", queries, key_heads, preferred_element_type=jnp.float32)
        + score_extra
    )
    row_max = jnp.max(scores, axis=-1, keepdims=True)
    exponent = jnp.exp(scores - row_max)
    row_total = jnp.sum(exponent, axis=-1, keepdims=True)
    log_total = row_max + jnp.log(row_total)
    probs_low = (exponent / row_total).astype(jnp.bfloat16)
    mixed_heads = jnp.einsum(
        "qhk,khd->qhd", probs_low, value_heads, preferred_element_type=jnp.float32
    ).reshape(seq_length, model_width)
    gated_low = (gate_sig * mixed_heads).astype(jnp.bfloat16)
    attn_out = jnp.dot(gated_low, full_out, preferred_element_type=jnp.float32)
    hidden = jnp.dot(second_low, full_up, preferred_element_type=jnp.float32)
    activated, act_back = jax.vjp(swish_product, hidden)
    act_low = activated.astype(jnp.bfloat16)
    trans_out = jnp.dot(act_low, full_down, preferred_element_type=jnp.float32)
    result = token_rows.astype(jnp.float32) + gate_one * attn_out + gate_two * trans_out
    cotangent = cotangent_rows.astype(jnp.float32)
    grad_attn = (cotangent * gate_one).astype(jnp.bfloat16)
    grad_trans = (cotangent * gate_two).astype(jnp.bfloat16)
    grad_gate_one = cotangent * attn_out
    grad_gate_two = cotangent * trans_out
    down_grad = left_product(act_low, grad_trans)
    (grad_hidden,) = act_back(right_product(grad_trans, full_down))
    hidden_low = grad_hidden.astype(jnp.bfloat16)
    up_grad = left_product(second_low, hidden_low)
    grad_second = right_product(hidden_low, full_up)
    out_grad_rows = left_product(gated_low, grad_attn)
    grad_gated = right_product(grad_attn, full_out)
    grad_mixed = (grad_gated * gate_sig).astype(jnp.bfloat16).reshape(head_shape)
    grad_part_g = grad_gated * mixed_heads * gate_sig * (1.0 - gate_sig)
    scores = (
        jnp.einsum("qhd,khd->qhk", queries, key_heads, preferred_element_type=jnp.float32)
        + score_extra
    )
    probs_full = jnp.exp(scores - log_total)
    grad_probs = jnp.einsum(
        "qhd,khd->qhk", grad_mixed, value_heads, preferred_element_type=jnp.float32
    )
    inner_sum = jnp.sum(probs_full * grad_probs, axis=-1, keepdims=True)
    grad_scores = (probs_full * (grad_probs - inner_sum)).astype(jnp.bfloat16)
    grad_values = jnp.einsum(
        "qhk,qhd->khd", probs_low, grad_mixed, preferred_element_type=jnp.float32
    )
    grad_query = (
        jnp.einsum("qhk,khd->qhd", grad_scores, key_heads, preferred_element_type=jnp.float32)
        * inverse_root
    )
    grad_keys = jnp.einsum("qhk,qhd->khd", grad_scores, queries, preferred_element_type=jnp.float32)
    query_rows = grad_query.reshape(seq_length, model_width)
    query_bias_grad = jnp.sum(query_rows, axis=0)
    grad_proj = jnp.concatenate(
        [
            query_rows,
            grad_keys.reshape(seq_length, model_width),
            grad_values.reshape(seq_length, model_width),
            grad_part_g,
        ],
        axis=-1,
    ).astype(jnp.bfloat16)
    qkvg_grad = left_product(first_low, grad_proj)
    grad_first = right_product(grad_proj, full_qkvg)
    grad_modul, grad_token_norm = modul_back(
        (grad_first, grad_second, grad_gate_one, grad_gate_two)
    )
    cond_bias_grad = jnp.sum(grad_modul, axis=0)
    modul_low = grad_modul.astype(jnp.bfloat16)
    cond_grad_rows = left_product(cond_low, modul_low)
    grad_cond, cond_gain_grad = cond_back(right_product(modul_low, full_cond))
    (grad_tokens,) = token_back(grad_token_norm)
    matrix_grads = (cond_grad_rows, qkvg_grad, out_grad_rows, up_grad, down_grad)
    vector_grads = (cond_gain_grad, cond_bias_grad, query_bias_grad)
    return (result, cotangent + grad_tokens, grad_cond, grad_scores, matrix_grads, vector_grads)


def on_device(
    tokens,
    cond,
    pair,
    counts,
    owner,
    out_grad,
    cond_gain,
    cond_weight,
    cond_bias,
    qkvg_weight,
    query_bias,
    out_weight,
    pair_gain,
    pair_weight,
    up_weight,
    down_weight,
):
    matrices = (
        lax.all_gather(cond_weight, "fsdp", axis=0, tiled=True),
        lax.all_gather(qkvg_weight, "fsdp", axis=0, tiled=True),
        lax.all_gather(out_weight, "fsdp", axis=0, tiled=True),
        lax.all_gather(up_weight, "fsdp", axis=0, tiled=True),
        lax.all_gather(down_weight, "fsdp", axis=0, tiled=True),
    )
    pair_norm, pair_back = jax.vjp(scaled_norm, pair.astype(jnp.float32), pair_gain)
    pair_low = pair_norm.astype(jnp.bfloat16)
    bias_part = jnp.einsum(
        "crkz,zh->crhk", pair_low, pair_weight, preferred_element_type=jnp.float32
    ).astype(jnp.bfloat16)
    bias_all = lax.all_gather(bias_part, ("dp", "fsdp"), axis=1, tiled=True)
    sample_count = tokens.shape[0]
    seq_length = tokens.shape[1]
    head_count = bias_all.shape[2]
    first_sample = lax.axis_index(("dp", "fsdp")) * sample_count
    owner_rows = lax.dynamic_slice_in_dim(owner, first_sample, sample_count)
    positions = jnp.arange(seq_length, dtype=jnp.int32)
    vectors = (cond_gain, cond_bias, query_bias)
    results, token_grads, cond_grads, score_grads = ([], [], [], [])
    owner_index = owner_rows[0]
    key_limit = counts[owner_index]
    mask_rows = jnp.where(positions < key_limit, 0.0, mask_fill).astype(jnp.float32)
    bias_rows = lax.dynamic_index_in_dim(bias_all, owner_index, 0, keepdims=False)
    result, grad_tokens, grad_cond, grad_scores, matrix_grads, vector_grads = sample_pass(
        tokens[0], cond[0], out_grad[0], mask_rows, bias_rows, matrices, vectors
    )
    results.append(result)
    token_grads.append(grad_tokens)
    cond_grads.append(grad_cond)
    score_grads.append(grad_scores)
    stacked = jnp.stack(score_grads, axis=1)
    received = lax.all_to_all(
        lax.all_to_all(stacked, "dp", split_axis=0, concat_axis=1, tiled=True),
        "fsdp",
        split_axis=0,
        concat_axis=1,
        tiled=True,
    )
    dp_count = lax.axis_size("dp")
    fsdp_count = lax.axis_size("fsdp")
    received = received.reshape(
        received.shape[0], fsdp_count, dp_count, sample_count, head_count, seq_length
    )
    sources = owner.reshape(dp_count, fsdp_count, sample_count).transpose(1, 0, 2)
    onehot = (sources[..., None] == jnp.arange(2, dtype=jnp.int32)).astype(jnp.bfloat16)
    bias_sum = jnp.einsum("rfpshk,fpsc->crhk", received, onehot, preferred_element_type=jnp.float32)
    bias_grad = bias_sum.astype(jnp.bfloat16)
    pair_weight_grad = jnp.einsum(
        "crkz,crhk->zh", pair_low, bias_grad, preferred_element_type=jnp.float32
    )
    grad_pair_norm = jnp.einsum(
        "crhk,zh->crkz", bias_grad, pair_weight, preferred_element_type=jnp.float32
    )
    pair_grad, pair_gain_grad = pair_back(grad_pair_norm)
    cond_sum, qkvg_sum, out_sum, up_sum, down_sum = matrix_grads
    shards = (
        lax.psum_scatter(
            cond_sum.astype(jnp.bfloat16), "fsdp", scatter_dimension=0, tiled=True
        ).astype(jnp.float32),
        lax.psum_scatter(
            qkvg_sum.astype(jnp.bfloat16), "fsdp", scatter_dimension=0, tiled=True
        ).astype(jnp.float32),
        lax.psum_scatter(
            out_sum.astype(jnp.bfloat16), "fsdp", scatter_dimension=0, tiled=True
        ).astype(jnp.float32),
        lax.psum_scatter(
            up_sum.astype(jnp.bfloat16), "fsdp", scatter_dimension=0, tiled=True
        ).astype(jnp.float32),
        lax.psum_scatter(
            down_sum.astype(jnp.bfloat16), "fsdp", scatter_dimension=0, tiled=True
        ).astype(jnp.float32),
    )
    totals = (
        lax.psum(shards[0].astype(jnp.bfloat16), "dp").astype(jnp.float32),
        lax.psum(shards[1].astype(jnp.bfloat16), "dp").astype(jnp.float32),
        lax.psum(shards[2].astype(jnp.bfloat16), "dp").astype(jnp.float32),
        lax.psum(shards[3].astype(jnp.bfloat16), "dp").astype(jnp.float32),
        lax.psum(shards[4].astype(jnp.bfloat16), "dp").astype(jnp.float32),
    )
    cond_gain_sum, cond_bias_sum, query_bias_sum = vector_grads
    small = lax.psum(
        (cond_gain_sum, cond_bias_sum, query_bias_sum, pair_gain_grad, pair_weight_grad),
        ("dp", "fsdp"),
    )
    return (
        jnp.stack(results),
        jnp.stack(token_grads),
        jnp.stack(cond_grads),
        pair_grad,
        small[0],
        totals[0],
        small[1],
        totals[1],
        small[2],
        totals[2],
        small[3],
        small[4],
        totals[3],
        totals[4],
    )


def solution(mesh):
    in_specs = (
        P(("dp", "fsdp"), None, None),
        P(("dp", "fsdp"), None, None),
        P(None, ("dp", "fsdp"), None, None),
        P(),
        P(),
        P(("dp", "fsdp"), None, None),
        P(),
        P("fsdp", None),
        P(),
        P("fsdp", None),
        P(),
        P("fsdp", None),
        P(),
        P(),
        P("fsdp", None),
        P("fsdp", None),
    )
    out_specs = (
        P(("dp", "fsdp"), None, None),
        P(("dp", "fsdp"), None, None),
        P(("dp", "fsdp"), None, None),
        P(None, ("dp", "fsdp"), None, None),
        P(),
        P("fsdp", None),
        P(),
        P("fsdp", None),
        P(),
        P("fsdp", None),
        P(),
        P(),
        P("fsdp", None),
        P("fsdp", None),
    )
    return jax.shard_map(
        on_device, mesh=mesh, in_specs=in_specs, out_specs=out_specs, check_vma=False
    )
```

profile of v0, /device:TPU:0, one launch (start us, length us, event | category | flops | bytes accessed | tf_op | source)
XLA Modules:
  0.0 1312.0 jit_solution(13882968473659724289)
XLA Ops:
  9.5 12.9 copy.110
  43.6 18.0 %all-gather.7.cloned.1.call-done = bf16[384,4608]{1,0:T(8,128)(2,1)} async-done(((bf16[192,4608]{1,0:T(8,128)(2,1)}), bf16[384,4608]{1,0:T(8,128)(2,1)}) %all-gather.7.cloned.1.call-update) | async-done | bytes 3538960 | tf_op jit(solution)/shard_map/all_gather | solution.py:165
  75.0 50.9 %all-gather.9.cloned.1.call-done = bf16[768,3072]{1,0:T(8,128)(2,1)} async-done(((bf16[384,3072]{1,0:T(8,128)(2,1)}), bf16[768,3072]{1,0:T(8,128)(2,1)}) %all-gather.9.cloned.1.call-update) | async-done | bytes 4718608 | tf_op jit(solution)/shard_map/all_gather | solution.py:166
  125.9 8.8 fusion.128
  136.2 14.1 %all-gather.13.cloned.1.call-done = bf16[768,768]{1,0:T(8,128)(2,1)} async-done(((bf16[384,768]{1,0:T(8,128)(2,1)}), bf16[768,768]{1,0:T(8,128)(2,1)}) %all-gather.13.cloned.1.call-update) | async-done | bytes 1179664 | tf_op jit(solution)/shard_map/all_gather | solution.py:167
  160.6 208.0 %all-gather.11.cloned.1.call-done = bf16[2,768,16,768]{3,2,0,1:T(8,128)(2,1)} async-done(((bf16[2,24,16,768]{3,2,0,1:T(8,128)(2,1)}), bf16[2,768,16,768]{3,2,0,1:T(8,128)(2,1)}) %all-gather.11.cloned.1.call-update) | async-done | bytes 37748752 | tf_op jit(solution)/shard_map/all_gather | solution.py:176
  368.6 17.1 %constant_dynamic-slice_fusion = bf16[1,768,16,768]{3,2,0,1:T(8,128)(2,1)} fusion(bf16[2,768,16,768]{3,2,0,1:T(8,128)(2,1)} %all-gather.11.cloned.1.call-done, s32[]{:T(128)S(6)} %select_n.17), kind=kLoop, calls=%fused_computation.172 | loop fusion | bytes 37748740 | tf_op jit(solution)/shard_map/jit(dynamic_index_in_dim)/dynamic_slice | solution.py:188
  385.7 24.5 %copy.160 = bf16[1,768,16,768]{1,3,2,0:T(8,128)(2,1)} copy(bf16[1,768,16,768]{3,2,0,1:T(8,128)(2,1)} %constant_dynamic-slice_fusion) | data formatting | bytes 37748736
  410.2 21.2 %fusion.129 = (f32[768,16]{0,1:T(8,128)}, f32[768,16,768]{0,2,1:T(8,128)}) fusion(f32[768]{0:T(1024)S(1)} %fusion.105, bf16[1,768,16,768]{1,3,2,0:T(8,128)(2,1)} %copy.160, bf16[768,16,48]{0,2,1:T(8,128)(2,1)S(1)} %bitcast.210, bf16[768,16,48]{0,2,1:T(8,128)(2,1)} %bitcast.214), kind=kOutput, calls=%fused_computation.182 | convolution fusion | flops 943706112 | bytes 59034624 | tf_op jit(solution)/shard_map/qhd,khd->qhk/dot_general | solution.py:70
  431.4 15.6 %fusion.4 = f32[768,16]{0,1:T(8,128)S(1)} fusion(f32[768,16,768]{0,2,1:T(8,128)} %get-tuple-element.93, f32[768,16]{0,1:T(8,128)} %get-tuple-element.92), kind=kLoop, calls=%fused_computation.10 | loop fusion | flops 18862080 | bytes 37847040 | tf_op jit(solution)/shard_map/reduce_sum | solution.py:75
  447.7 28.5 %fusion.1 = (f32[768,16]{0,1:T(8,128)}, f32[16,768,768]{2,1,0:T(8,128)}) fusion(f32[768,16,768]{0,2,1:T(8,128)} %get-tuple-element.93, f32[768,16]{0,1:T(8,128)} %log_add_fusion, bf16[768,16,48]{0,2,1:T(8,128)(2,1)S(1)} %bitcast.208, bf16[768,16,48]{0,2,1:T(8,128)(2,1)S(1)} %bitcast.212), kind=kOutput, calls=%fused_computation.4 | convolution fusion | flops 934268928 | bytes 77955072 | tf_op jit(solution)/shard_map/qhd,khd->qhk/dot_general | solution.py:107
  476.1 33.5 %fusion.3 = (bf16[768,16,768]{0,2,1:T(8,128)(2,1)}, bf16[768,16,768]{0,2,1:T(8,128)(2,1)S(1)}) fusion(f32[16,768,768]{2,1,0:T(8,128)} %get-tuple-element.95, f32[768,16,768]{0,2,1:T(8,128)} %get-tuple-element.93, f32[768,16]{0,1:T(8,128)} %get-tuple-element.94, f32[768,16]{0,1:T(8,128)} %log_add_fusion, f32[768,16]{0,1:T(8,128)} %copy-done.39, ...), kind=kLoop, calls=%fused_computation.6 | loop fusion | flops 66060288 | bytes 113442816 | tf_op jit(solution)/shard_map/convert_element_type | solution.py:111
  519.9 24.9 %copy.137 = bf16[768,1,16,768]{3,2,1,0:T(8,128)(2,1)} copy(bf16[768,1,16,768]{0,3,2,1:T(8,128)(2,1)} %bitcast.207) | data formatting | bytes 37748736 | tf_op jit(solution)/shard_map/stack | solution.py:196
  550.1 13.0 convolution_convert_fusion.6
  565.9 11.9 convolution_convert_fusion.7
  579.3 11.2 bitcast_convert_fusion.1
  602.3 10.7 fusion.42
  613.0 11.1 fusion.131
  624.2 9.2 fusion.20
  658.6 9.2 fusion.52
  667.8 9.7 convolution_convert_fusion
  696.3 187.0 %all-to-all-done = bf16[768,1,16,768]{3,2,1,0:T(8,128)(2,1)} async-done(((bf16[768,1,16,768]{3,2,1,0:T(8,128)(2,1)}), bf16[768,1,16,768]{3,2,1,0:T(8,128)(2,1)}, u32[]{:S(2)}, u32[]{:S(2)}) %all-to-all-start) | async-done | bytes 18874400 | tf_op jit(solution)/shard_map/all_to_all | solution.py:198
  883.3 17.0 %copy.138 = bf16[48,16,16,768]{3,2,1,0:T(8,128)(2,1)} copy(bf16[48,16,16,768]{3,2,0,1:T(8,128)(2,1)} %bitcast.35) | data formatting | bytes 37748736 | tf_op jit(solution)/shard_map/all_to_all | solution.py:198
  900.3 10.5 all-to-all-start.1
  912.5 9.0 fusion.91
  938.6 221.0 %all-reduce.4.cloned.1.call-done = (bf16[192,4608]{1,0:T(8,128)(2,1)}, bf16[384,3072]{1,0:T(8,128)(2,1)}, bf16[384,768]{1,0:T(8,128)(2,1)}, bf16[384,3072]{1,0:T(8,128)(2,1)}, bf16[768,768]{1,0:T(8,128)(2,1)}) async-done(((bf16[192,4608]{1,0:T(8,128)(2,1)}, bf16[384,3072]{1,0:T(8,128)(2,1)}, bf16[384,768]{1,0:T(8,128)(2,1)}, bf16[384,3072]{1,0:T(8,128)(2,1)}, bf16[768,768]{1,0:T(8,128)(2,1)}), ...) | async-done | bytes 8257552 | tf_op jit(solution)/shard_map/psum | solution.py:239
  1171.6 11.4 bitcast_convert_fusion
  1183.1 11.5 fusion.14
  1197.7 13.3 %fusion.12 = (f32[128]{0:T(128)S(1)}, f32[2,24,768]{2,1,0:T(8,128)S(1)}) fusion(f32[2,24,768,128]{2,3,1,0:T(8,128)} %get-tuple-element.106, bf16[2,24,768,128]{2,3,1,0:T(8,128)(2,1)S(1)} %bitcast.206, f32[2,24,768]{2,1,0:T(8,128)S(1)} %copy-done.19, f32[2,24,768]{2,1,0:T(8,128)S(1)} %copy-done.13, f32[2,24,768]{2,1,0:T(8,128)S(1)} %multiply_multiply_fusion, ...), kind=kLoop, calls=%fused_computation.21 | loop fusion | flops 51867520 | bytes 28902400 | tf_op jit(solution)/shard_map/transpose(jvp())/reduce_sum | solution.py:20
  1211.0 16.5 %broadcast_add_fusion = f32[2,24,768,128]{2,3,1,0:T(8,128)} fusion(f32[2,24,768]{2,1,0:T(8,128)S(1)} %negate_multiply_fusion, f32[2,24,768]{2,1,0:T(8,128)S(1)} %multiply_multiply_fusion, f32[2,24,768]{2,1,0:T(8,128)S(1)} %copy-done.13, bf16[2,24,768,128]{2,3,1,0:T(8,128)(2,1)S(1)} %bitcast.206, f32[2,24,768]{2,1,0:T(8,128)S(1)} %copy-done.19, ...), kind=kLoop, calls=%fused_computation.28 | loop fusion | flops 37748736 | bytes 47776256 | tf_op jit(solution)/shard_map/transpose(jvp())/add_any | solution.py:13
  1227.5 18.6 %copy.144 = f32[2,24,768,128]{3,2,1,0:T(8,128)} copy(f32[2,24,768,128]{2,3,1,0:T(8,128)} %broadcast_add_fusion) | data formatting | bytes 37748736
  1246.2 58.7 %all-reduce = (f32[384]{0:T(512)}, f32[4608]{0:T(1024)}, f32[768]{0:T(1024)}, f32[128]{0:T(128)}, f32[128,16]{0,1:T(8,128)}) all-reduce(f32[384]{0:T(512)S(1)} %copy-done.54, f32[4608]{0:T(1024)S(1)} %copy-done.44, f32[768]{0:T(1024)S(1)} %copy-done.51, ...), channel_id=1, replica_groups=mesh['dp'=16,'fsdp'=2] {'dp','fsdp'}, use_global_device_ids=true, to_apply=%region_16.17 | all-reduce | flops 7936 | bytes 63488 | tf_op jit(solution)/shard_map/psum | solution.py:246
  (240 shorter events, 156.3 us)
Async XLA Ops:
  7.2 25.9 %copy-start = (bf16[128,16]{0,1:T(8,128)(2,1)S(1)}, bf16[128,16]{0,1:T(8,128)(2,1)}, u32[]{:S(2)}) copy-start(bf16[128,16]{0,1:T(8,128)(2,1)} %param.29) | copy-start | bytes 12292
  7.2 54.5 %all-gather.7.cloned.1.call-start = ((), (), s32[]{:S(2)}) async-start(), calls=%async_computation.7 | async-start | bytes 5308416 | tf_op jit(solution)/shard_map/all_gather | solution.py:165
  7.9 118.0 %all-gather.9.cloned.1.call-start = ((), (), s32[]{:S(2)}) async-start(), calls=%async_computation.8 | async-start | bytes 7077888 | tf_op jit(solution)/shard_map/all_gather | solution.py:166
  8.7 141.6 %all-gather.13.cloned.1.call-start = ((), (), s32[]{:S(2)}) async-start(), calls=%async_computation.10 | async-start | bytes 1769472 | tf_op jit(solution)/shard_map/all_gather | solution.py:167
  9.4 359.2 %all-gather.11.cloned.1.call-start = ((), (), s32[]{:S(2)}) async-start(), calls=%async_computation.9 | async-start | bytes 38928384 | tf_op jit(solution)/shard_map/all_gather | solution.py:176
  37.2 575.8 %all-gather.15.cloned.1.call-start = ((), (), s32[]{:S(2)}) async-start(), calls=%async_computation.11 | async-start | bytes 7077888 | tf_op jit(solution)/shard_map/all_gather | solution.py:168
  37.8 586.4 %all-gather.17.cloned.1.call-start = ((), (), s32[]{:S(2)}) async-start(), calls=%async_computation.12 | async-start | bytes 3538944 | tf_op jit(solution)/shard_map/all_gather | solution.py:169
  40.3 21.4 %copy-start.32 = (f32[4608]{0:T(1024)S(1)}, f32[4608]{0:T(1024)}, u32[]{:S(2)}) copy-start(f32[4608]{0:T(1024)} %param.24) | copy-start | bytes 55300
  40.3 21.4 %copy-start.40 = (f32[384]{0:T(512)S(1)}, f32[384]{0:T(512)}, u32[]{:S(2)}) copy-start(f32[384]{0:T(512)} %param.22) | copy-start | bytes 4612
  40.6 27.1 %copy-start.42 = (f32[768]{0:T(1024)}, f32[768]{0:T(1024)S(1)}, u32[]{:S(2)}) copy-start(f32[768]{0:T(1024)S(1)} %broadcast_multiply_fusion.1) | copy-start | bytes 9220
  41.1 20.6 %copy-start.47 = (f32[768]{0:T(1024)}, f32[768]{0:T(1024)S(1)}, u32[]{:S(2)}) copy-start(f32[768]{0:T(1024)S(1)} %fusion.45) | copy-start | bytes 9220
  41.1 26.6 %copy-start.45 = (f32[768]{0:T(1024)}, f32[768]{0:T(1024)S(1)}, u32[]{:S(2)}) copy-start(f32[768]{0:T(1024)S(1)} %fusion.109) | copy-start | bytes 9220
  41.4 26.3 %copy-start.5 = (bf16[1,768,384]{1,2,0:T(8,128)(2,1)}, bf16[1,768,384]{1,2,0:T(8,128)(2,1)S(1)}, u32[]{:S(2)}) copy-start(bf16[1,768,384]{1,2,0:T(8,128)(2,1)S(1)} %copy.106) | copy-start | bytes 1769476
  41.5 20.2 %copy-start.33 = (f32[768]{0:T(1024)}, f32[768]{0:T(1024)S(1)}, u32[]{:S(2)}) copy-start(f32[768]{0:T(1024)S(1)} %broadcast_multiply_fusion.2) | copy-start | bytes 9220
  41.7 20.0 %copy-start.49 = (f32[768]{0:T(1024)}, f32[768]{0:T(1024)S(1)}, u32[]{:S(2)}) copy-start(f32[768]{0:T(1024)S(1)} %fusion.90) | copy-start | bytes 9220
  41.7 19.9 %copy-start.35 = (f32[768]{0:T(1024)}, f32[768]{0:T(1024)S(1)}, u32[]{:S(2)}) copy-start(f32[768]{0:T(1024)S(1)} %fusion.108) | copy-start | bytes 9220
  75.0 59.7 %copy-start.30 = (bf16[768,768]{1,0:T(8,128)(2,1)}, bf16[768,768]{1,0:T(8,128)(2,1)S(1)}, u32[]{:S(2)}) copy-start(bf16[768,768]{1,0:T(8,128)(2,1)S(1)} %fusion.38) | copy-start | bytes 3538948
  431.4 15.6 %copy-start.31 = (f32[768,16]{0,1:T(8,128)S(1)}, f32[768,16]{0,1:T(8,128)}, u32[]{:S(2)}) copy-start(f32[768,16]{0,1:T(8,128)} %get-tuple-element.92) | copy-start | bytes 147460
  544.8 338.5 %all-to-all-start = ((bf16[768,1,16,768]{3,2,1,0:T(8,128)(2,1)}), bf16[768,1,16,768]{3,2,1,0:T(8,128)(2,1)}, u32[]{:S(2)}, u32[]{:S(2)}) async-start(bf16[768,1,16,768]{3,2,1,0:T(8,128)(2,1)} %copy.137), calls=%async_computation | async-start | bytes 37748736 | tf_op jit(solution)/shard_map/all_to_all | solution.py:198
  550.1 360.9 %reduce-scatter.10.cloned.1.call-start = ((), (), s32[]{:S(2)}) async-start(), calls=%async_computation.15 | async-start | bytes 1769472 | tf_op jit(solution)/shard_map/reduce_scatter | solution.py:228
  602.2 308.9 %reduce-scatter.14.cloned.1.call-start = ((), (), s32[]{:S(2)}) async-start(), calls=%async_computation.17 | async-start | bytes 3538944 | tf_op jit(solution)/shard_map/reduce_scatter | solution.py:234
  613.0 27.2 %copy-start.16 = (f32[768,768]{1,0:T(8,128)}, f32[768,768]{1,0:T(8,128)S(1)}, u32[]{:S(2)}) copy-start(f32[768,768]{1,0:T(8,128)S(1)} %get-tuple-element.98) | copy-start | bytes 7077892
  640.1 271.0 %reduce-scatter.6.cloned.1.call-start = ((), (), s32[]{:S(2)}) async-start(), calls=%async_computation.13 | async-start | bytes 5308416 | tf_op jit(solution)/shard_map/reduce_scatter | solution.py:222
  677.5 233.6 %reduce-scatter.8.cloned.1.call-start = ((), (), s32[]{:S(2)}) async-start(), calls=%async_computation.14 | async-start | bytes 7077888 | tf_op jit(solution)/shard_map/reduce_scatter | solution.py:225
  687.2 224.0 %reduce-scatter.12.cloned.1.call-start = ((), (), s32[]{:S(2)}) async-start(), calls=%async_computation.16 | async-start | bytes 7077888 | tf_op jit(solution)/shard_map/reduce_scatter | solution.py:231
  900.3 271.3 %all-to-all-start.1 = ((bf16[48,16,16,768]{3,2,1,0:T(8,128)(2,1)}), bf16[48,16,16,768]{3,2,1,0:T(8,128)(2,1)}, u32[]{:S(2)}, u32[]{:S(2)}) async-start(bf16[48,16,16,768]{3,2,1,0:T(8,128)(2,1)} %copy.138), calls=%async_computation.1 | async-start | bytes 37748736 | tf_op jit(solution)/shard_map/all_to_all | solution.py:197
  910.8 248.8 %all-reduce.4.cloned.1.call-start = ((), (), s32[]{:S(2)}) async-start(), calls=%async_computation.18 | async-start | bytes 16515072 | tf_op jit(solution)/shard_map/psum | solution.py:239
  1171.6 22.9 %slice-start = ((s8[9437184]{0:T(1024)(128)(4,1)}), s8[4194304]{0:T(1024)(128)(4,1)S(1)}, s32[]{:S(2)}) async-start(s8[9437184]{0:T(1024)(128)(4,1)} %bitcast.205), calls=%async_computation.19 | async-start | bytes 8388608
  1171.6 22.9 %slice-start.1 = ((s8[9437184]{0:T(1024)(128)(4,1)}), s8[1048576]{0:T(1024)(128)(4,1)S(1)}, s32[]{:S(2)}) async-start(s8[9437184]{0:T(1024)(128)(4,1)} %bitcast.205), calls=%async_computation.20 | async-start | bytes 2097152
  1227.5 18.6 %copy-start.44 = (f32[4608]{0:T(1024)S(1)}, f32[4608]{0:T(1024)}, u32[]{:S(2)}) copy-start(f32[4608]{0:T(1024)} %reduce_sum.211) | copy-start | bytes 55300
  1227.5 18.6 %copy-start.51 = (f32[768]{0:T(1024)S(1)}, f32[768]{0:T(1024)}, u32[]{:S(2)}) copy-start(f32[768]{0:T(1024)} %reduce_sum.213) | copy-start | bytes 9220
  1227.5 18.6 %copy-start.54 = (f32[384]{0:T(512)S(1)}, f32[384]{0:T(512)}, u32[]{:S(2)}) copy-start(f32[384]{0:T(512)} %get-tuple-element.58) | copy-start | bytes 4612
  (53 other events, 267.5 us)
Sparse Core Ops, SparseCore 0:
  9.6 52.0 all-gather.6
  63.2 62.6 all-gather.8
  127.4 22.7 all-gather.12
  153.6 214.9 all-gather.10
  370.0 60.8 all-gather.14
  432.3 36.0 all-gather.16
  602.3 22.8 reduce-scatter.9
  640.2 35.7 reduce-scatter.13
  678.8 47.6 reduce-scatter.5
  729.3 59.9 reduce-scatter.7
  792.2 59.9 reduce-scatter.11
  916.2 243.3 all-reduce.3
where the time goes:
time: 1320 us; the launch traced here: 1310 us
  waiting for transfers between devices  702 us (53%)
  matrix products  239 us (18%)
  local copies, waits for them, and re-layouts  155 us (12%)
  other arithmetic  123 us (9%)
  blocking collectives  58.7 us (4%)
  between operations  17.2 us (1%)
  starting transfers between devices  16.6 us (1%)
    psum x1, waiting for transfers between devices, on_device(): lax.psum(shards[0].astype(jnp.bfloat16), 'dp').astype(jnp.float32)  221 us
    all_gather x1, waiting for transfers between devices, on_device(): bias_all = lax.all_gather(bias_part, ('dp', 'fsdp'), axis=1, tiled=True)  208 us
    all_to_all x1, waiting for transfers between devices, on_device(): lax.all_to_all(stacked, 'dp', split_axis=0, concat_axis=1, tiled=True)  187 us
    unnamed x149, local copies, waits for them, and re-layouts  78.2 us
    psum x1, blocking collectives, on_device(): lax.psum((cond_gain_sum, cond_bias_sum, query_bias_sum, pair_gain_grad, p...  58.7 us
    all_gather x1, waiting for transfers between devices, on_device(): lax.all_gather(qkvg_weight, 'fsdp', axis=0, tiled=True)  50.9 us
    dot_general x5, matrix products, right_product(): lax.dot_general(left_side, right_side, (((1,), (1,)), ((), ())), preferre...  43.7 us
    dot_general x5, matrix products, left_product(): lax.dot_general(left_side, right_side, (((0,), (0,)), ((), ())), preferre...  35.3 us
  transfers between devices with their start and end apart: 14, of which 6 were waited for; matrix products, arithmetic and copies ran while one was open for 32% of the time, Pallas kernels for 0%

commit v1 on v0

v1 whole, which is shorter than its diff:
```python
import functools

import jax
import jax.numpy as jnp
from jax import lax
from jax.experimental import pallas as pl
from jax.experimental.pallas import tpu as pltpu
from jax.sharding import Mesh, PartitionSpec as P

f32, bf16 = jnp.float32, jnp.bfloat16
norm_eps = 1e-05
mask_fill = -1000000000.0
log2e = 1.4426950408889634
ln2 = 0.6931471805599453
head_count = 16
group_size = 8
vmem_bytes = 58 << 20
nt_dims = (((1,), (1,)), ((), ()))


def dot(a, b):
    return jnp.dot(a, b, preferred_element_type=f32)


def dot_nt(a, b):
    return lax.dot_general(a, b, nt_dims, preferred_element_type=f32)


def dot_tn(a, b):
    return lax.dot_general(a, b, (((0,), (0,)), ((), ())), preferred_element_type=f32)


def norm_parts(values):
    centered = values - jnp.mean(values, axis=-1, keepdims=True)
    variance = jnp.mean(centered * centered, axis=-1, keepdims=True)
    scale = lax.rsqrt(variance + norm_eps)
    return centered * scale, scale


def norm_back(x, u, scale):
    mean_u = jnp.mean(u, axis=-1, keepdims=True)
    mean_ux = jnp.mean(u * x, axis=-1, keepdims=True)
    return (u - mean_u - x * mean_ux) * scale


def params(**kw):
    return pltpu.CompilerParams(vmem_limit_bytes=vmem_bytes, **kw)


def whole(a):
    zero = (0,) * a.ndim
    return pl.BlockSpec(a.shape, lambda *_: zero)


def lane_means(values):
    width = values.shape[-1]
    return dot(values, jnp.full((width, width), 1.0 / width, bf16))


def pair_norm(x):
    values = x.astype(f32)
    centered = values - lane_means(x)
    variance = lane_means((centered * centered).astype(bf16))
    scale = lax.rsqrt(variance + norm_eps)
    return centered * scale, scale


def pair_fwd_kernel(rows, counts_ref, x_ref, pw_ref, gain_ref, out_ref, scr_ref):
    step = pl.program_id(0)
    steps_each = pl.num_programs(0) // 2
    limit = counts_ref[step // steps_each]
    heads, length = scr_ref.shape[0], scr_ref.shape[2]
    valid = lax.broadcasted_iota(jnp.int32, (heads, length), 1) < limit
    pw = pw_ref[...]
    gain = gain_ref[...]
    for r in range(rows):
        x_hat, _ = pair_norm(x_ref[0, r])
        low = (x_hat * gain).astype(bf16)
        bias = dot_nt(pw, low)
        scr_ref[:, r, :] = jnp.where(valid, bias * log2e, mask_fill)
    out_ref[:, 0] = scr_ref[...].astype(bf16)


def pair_fwd(counts, pair, pw_t, gain):
    _, total, length, width = pair.shape
    rows = 8 if total % 8 == 0 else total
    steps = total // rows
    heads = pw_t.shape[0]
    return pl.pallas_call(
        functools.partial(pair_fwd_kernel, rows),
        grid_spec=pltpu.PrefetchScalarGridSpec(
            num_scalar_prefetch=1,
            grid=(2 * steps,),
            in_specs=[
                pl.BlockSpec((1, rows, length, width), lambda i, _: (i // steps, i % steps, 0, 0)),
                whole(pw_t),
                whole(gain),
            ],
            out_specs=pl.BlockSpec((heads, 1, rows, length), lambda i, _: (0, i // steps, i % steps, 0)),
            scratch_shapes=[pltpu.VMEM((heads, rows, length), f32)],
        ),
        out_shape=jax.ShapeDtypeStruct((heads, 2, total, length), bf16),
        compiler_params=params(),
        cost_estimate=pl.CostEstimate(flops=2 * pair.size * 300, bytes_accessed=pair.size * 2, transcendentals=pair.size),
        name="pair_fwd",
    )(counts, pair, pw_t, gain)


def pair_bwd_kernel(rows, x_ref, bg_ref, a_ref, out_ref, q_ref, scr_ref):
    @pl.when(pl.program_id(0) == 0)
    def _():
        q_ref[...] = jnp.zeros_like(q_ref)

    scr_ref[...] = bg_ref[:, 0].astype(f32)
    weights = a_ref[...]
    total = q_ref[...]
    width = out_ref.shape[-1]
    for r in range(rows):
        x_hat, scale = pair_norm(x_ref[0, r])
        grads = scr_ref[:, r, :].astype(bf16)
        total += dot(grads, x_hat.astype(bf16))
        u = dot_tn(jnp.concatenate([grads, grads], axis=0), weights)
        mean_ux = lane_means((u * x_hat).astype(bf16))
        out_ref[0, r] = (u - x_hat * mean_ux) * scale
    q_ref[...] = total


def pair_bwd(pair, bias_grad, centered_weights):
    _, total, length, width = pair.shape
    rows = 8 if total % 8 == 0 else total
    steps = total // rows
    heads = bias_grad.shape[0]
    return pl.pallas_call(
        functools.partial(pair_bwd_kernel, rows),
        grid=(2 * steps,),
        in_specs=[
            pl.BlockSpec((1, rows, length, width), lambda i: (i // steps, i % steps, 0, 0)),
            pl.BlockSpec((heads, 1, rows, length), lambda i: (0, i // steps, i % steps, 0)),
            whole(centered_weights),
        ],
        out_specs=[
            pl.BlockSpec((1, rows, length, width), lambda i: (i // steps, i % steps, 0, 0)),
            pl.BlockSpec((heads, width), lambda i: (0, 0)),
        ],
        out_shape=[
            jax.ShapeDtypeStruct(pair.shape, f32),
            jax.ShapeDtypeStruct((heads, width), f32),
        ],
        scratch_shapes=[pltpu.VMEM((heads, rows, length), f32)],
        compiler_params=params(),
        cost_estimate=pl.CostEstimate(flops=2 * pair.size * 500, bytes_accessed=pair.size * 6, transcendentals=pair.size),
        name="pair_bwd",
    )(pair, bias_grad, centered_weights)


def attn_kernel(rb, owner_ref, x_ref, bias_ref, y_ref, bg_ref, acc_ref):
    n = pl.program_id(0)
    c = owner_ref[n]
    length, hd = x_ref.shape[-1], x_ref.shape[-2]
    up, bz = bias_ref.shape[0], bias_ref.shape[2]

    @pl.when(n == 0)
    def _():
        acc_ref[...] = jnp.zeros_like(acc_ref)

    k_t, v_t = x_ref[0, 1], x_ref[0, 2]
    v_ext = jnp.concatenate([v_t, jnp.ones((16, length), bf16)], axis=0)
    dv = dk = 0.0
    for r in range(length // rb):
        sl = slice(r * rb, (r + 1) * rb)
        q_t = x_ref[0, 0, :, sl]
        q = q_t.T
        dm = x_ref[0, 3, :, sl].astype(f32).T
        z0 = r * rb // bz
        bias = jnp.concatenate([bias_ref[z0 + t, c].astype(f32) for t in range(rb // bz)], axis=0)
        s = dot(q, k_t) + bias
        e = jnp.exp2(s - jnp.max(s, axis=-1, keepdims=True))
        eb = e.astype(bf16)
        mx = dot_nt(eb, v_ext)
        inv = 1.0 / mx[:, hd : hd + 1]
        mixed = mx[:, :hd] * inv
        d = jnp.sum(mixed * dm, axis=-1, keepdims=True) * inv
        dms = (dm * inv).astype(bf16)
        ds = e * (dot(dms, v_t) - d)
        dsb = ds.astype(bf16)
        acc_ref[c, sl, :] += ds
        dq = dot_nt(dsb, k_t)
        dv = dv + dot(dms.T, eb)
        dk = dk + dot(q_t, dsb)
        y_ref[0, 0, :, sl] = mixed.T.astype(bf16)
        y_ref[0, 1, :, sl] = (dq * hd**-0.5).T.astype(bf16)
    y_ref[0, 2] = (dk * ln2).astype(bf16)
    y_ref[0, 3] = dv.astype(bf16)

    @pl.when(n == pl.num_programs(0) - 1)
    def _():
        for z in range(up):
            for cc in range(2):
                bg_ref[z, cc] = acc_ref[cc, z * bz : (z + 1) * bz, :].astype(bf16)


def attention(owner, x, bias):
    n, four, hd, length = x.shape
    return pl.pallas_call(
        functools.partial(attn_kernel, length // 2),
        grid_spec=pltpu.PrefetchScalarGridSpec(
            num_scalar_prefetch=1,
            grid=(n,),
            in_specs=[
                pl.BlockSpec((1, four, hd, length), lambda i, _: (i, 0, 0, 0)),
                pl.BlockSpec(bias.shape, lambda i, _: (0, 0, 0, 0)),
            ],
            out_specs=[
                pl.BlockSpec((1, four, hd, length), lambda i, _: (i, 0, 0, 0)),
                pl.BlockSpec(bias.shape, lambda i, _: (0, 0, 0, 0)),
            ],
            scratch_shapes=[pltpu.VMEM((2, length, length), f32)],
        ),
        out_shape=[jax.ShapeDtypeStruct(x.shape, bf16), jax.ShapeDtypeStruct(bias.shape, bf16)],
        compiler_params=params(),
        cost_estimate=pl.CostEstimate(
            flops=12 * n * length * length * 256, bytes_accessed=x.size * 4 + bias.size * 4, transcendentals=n * length * length
        ),
        name="attention",
    )(owner, x, bias)


def pick(flag, a, b):
    return jnp.where(flag == 0, a, b)


def split_dot(flag, x, own, other):
    half = own.shape[0]
    first, second = x[:, :half], x[:, half:]
    return dot(pick(flag, first, second), own[...]) + dot(pick(flag, second, first), other[...])


def split_dot_nt(flag, x, own, other):
    a, b = dot_nt(x, own[...]), dot_nt(x, other[...])
    return jnp.concatenate([pick(flag, a, b), pick(flag, b, a)], axis=-1)


def front_kernel(
    flag_ref, tok, cond, og, cgain, wc0, wc1, cb, wq0, wq1, qb, wo0, wo1,
    *outs,
):
    *xs, sg_o, gg_o, s1_o, g1_o, first_o = outs
    flag = flag_ref[0]
    width = tok.shape[-1]
    hd = width // head_count
    slots = len(xs)
    peers = head_count // slots
    cond_low = (norm_parts(cond[...].astype(f32))[0] * cgain[...]).astype(bf16)
    modul = split_dot(flag, cond_low, wc0, wc1) + cb[...]
    s1 = jax.nn.sigmoid(modul[:, :width])
    g1 = jax.nn.sigmoid(modul[:, 2 * width :])
    tn, _ = norm_parts(tok[...].astype(f32))
    first = (s1 * tn + modul[:, width : 2 * width]).astype(bf16)
    proj = split_dot(flag, first, wq0, wq1)
    q = (proj[:, :width] + qb[...]) * (hd**-0.5 * log2e)
    sg = jax.nn.sigmoid(proj[:, 3 * width :])
    ga = (og[...].astype(f32) * g1).astype(bf16)
    gg = split_dot_nt(flag, ga, wo0, wo1)
    dm = sg * gg
    sg_o[...] = sg.astype(bf16)
    gg_o[...] = gg.astype(bf16)
    s1_o[...] = s1.astype(bf16)
    g1_o[...] = g1.astype(bf16)
    first_o[...] = first
    for i, part in enumerate((q, proj[:, width : 2 * width], proj[:, 2 * width : 3 * width], dm)):
        turned = part.T.astype(bf16).reshape(peers, slots, hd, part.shape[0])
        for t in range(slots):
            xs[t][:, i] = turned[:, t]


def row_spec(a, rb):
    return pl.BlockSpec((rb, a.shape[1]), lambda i, *_: (i, 0))


def front(flag, tok, cond, og, cgain, wc, cb, wq, qb, wo, slots):
    length, width = tok.shape
    rb = 256
    peers, hd = head_count // slots, width // head_count
    small = jax.ShapeDtypeStruct((length, width), bf16)
    payload = jax.ShapeDtypeStruct((peers, 4, hd, length), bf16)
    return pl.pallas_call(
        front_kernel,
        grid_spec=pltpu.PrefetchScalarGridSpec(
            num_scalar_prefetch=1,
            grid=(length // rb,),
            in_specs=[row_spec(tok, rb), row_spec(cond, rb), row_spec(og, rb)]
            + [whole(a) for a in (cgain, *wc, cb, *wq, qb, *wo)],
            out_specs=[pl.BlockSpec((peers, 4, hd, rb), lambda i, _: (0, 0, 0, i))] * slots + [row_spec(tok, rb)] * 5,
        ),
        out_shape=[payload] * slots + [small] * 5,
        compiler_params=params(),
        cost_estimate=pl.CostEstimate(flops=2 * length * width * width * 7, bytes_accessed=20 << 20, transcendentals=length * width * 4),
        name="front",
    )(flag, tok, cond, og, cgain, *wc, cb, *wq, qb, *wo)


def trans_kernel(
    flag_ref, tok, cond, og, cgain, wc0, wc1, cb, wu0, wu1, wd0, wd1,
    part_o, u2_o, dcond_o, ml_o, cn_o, second_o, hid_o, act_o, gt_o, cbg_o,
):
    flag = flag_ref[0]
    width = tok.shape[-1]
    cond_low = (norm_parts(cond[...].astype(f32))[0] * cgain[...]).astype(bf16)
    cn_o[...] = cond_low
    modul = split_dot(flag, cond_low, wc0, wc1) + cb[...]
    s2 = jax.nn.sigmoid(modul[:, :width])
    g2 = jax.nn.sigmoid(modul[:, 2 * width :])
    tokens = tok[...].astype(f32)
    tn, _ = norm_parts(tokens)
    second = (s2 * tn + modul[:, width : 2 * width]).astype(bf16)
    second_o[...] = second
    hidden = split_dot(flag, second, wu0, wu1)
    ff = hidden.shape[1] // 2
    h_gate, h_up = hidden[:, :ff], hidden[:, ff:]
    sig = jax.nn.sigmoid(h_gate)
    silu = h_gate * sig
    act = (silu * h_up).astype(bf16)
    act_o[...] = act
    trans_out = split_dot(flag, act, wd0, wd1)
    part_o[...] = tokens + g2 * trans_out
    g = og[...].astype(f32)
    gt = (g * g2).astype(bf16)
    gt_o[...] = gt
    grad_act = split_dot_nt(flag, gt, wd0, wd1)
    hid = jnp.concatenate(
        [(grad_act * h_up * (sig * (1.0 + h_gate * (1.0 - sig)))).astype(bf16), (grad_act * silu).astype(bf16)], axis=-1
    )
    hid_o[...] = hid
    grad_second = split_dot_nt(flag, hid, wu0, wu1)
    u2_o[...] = (grad_second * s2).astype(bf16)
    grads = jnp.concatenate(
        [grad_second * tn * (s2 * (1.0 - s2)), grad_second, g * trans_out * (g2 * (1.0 - g2))], axis=-1
    )
    low = grads.astype(bf16)
    ml_o[...] = low

    @pl.when(pl.program_id(0) == 0)
    def _():
        cbg_o[...] = jnp.zeros_like(cbg_o)

    cbg_o[...] += jnp.sum(grads, axis=0, keepdims=True)
    dcond_o[...] = split_dot_nt(flag, low, wc0, wc1)


def transition(flag, tok, cond, og, cgain, wc, cb, wu, wd):
    length, width = tok.shape
    rb = 256
    cs, mw = cond.shape[1], cb.shape[1]
    ff2 = wu[0].shape[1]

    def out(w, dtype):
        return jax.ShapeDtypeStruct((length, w), dtype)

    shapes = [
        out(width, f32), out(width, bf16), out(cs, f32), out(mw, bf16), out(cs, bf16), out(width, bf16),
        out(ff2, bf16), out(ff2 // 2, bf16), out(width, bf16),
    ]
    return pl.pallas_call(
        trans_kernel,
        grid_spec=pltpu.PrefetchScalarGridSpec(
            num_scalar_prefetch=1,
            grid=(length // rb,),
            in_specs=[row_spec(tok, rb), row_spec(cond, rb), row_spec(og, rb)]
            + [whole(a) for a in (cgain, *wc, cb, *wu, *wd)],
            out_specs=[row_spec(s, rb) for s in shapes] + [pl.BlockSpec((1, mw), lambda i, _: (0, 0))],
        ),
        out_shape=shapes + [jax.ShapeDtypeStruct((1, mw), f32)],
        compiler_params=params(),
        cost_estimate=pl.CostEstimate(flops=2 * length * width * width * 15, bytes_accessed=40 << 20, transcendentals=length * width * 6),
        name="transition",
    )(flag, tok, cond, og, cgain, *wc, cb, *wu, *wd)


def back_kernel(slots, flag_ref, *refs):
    ys = refs[:slots]
    (
        sg, gg, s1, g1, part, u2, dcond2, tok, cond, og, cgain, wc0, wc1, wq0, wq1, wo0, wo1,
        out_o, tg_o, cg_o, gated_o, ga_o, gp_o, ml_o, qbg_o, cbg_o, cgg_o,
    ) = refs[slots:]
    flag = flag_ref[0]
    rb, width = tok.shape
    hd = width // head_count
    peers = head_count // slots

    def heads(i):
        stacked = jnp.stack([y[:, i] for y in ys], axis=1)
        return stacked.reshape(width, rb).astype(f32).T

    mixed = heads(0)
    sgv = sg[...].astype(f32)
    g1v = g1[...].astype(f32)
    gated = (sgv * mixed).astype(bf16)
    gated_o[...] = gated
    attn_out = split_dot(flag, gated, wo0, wo1)
    out_o[...] = part[...] + g1v * attn_out
    g = og[...].astype(f32)
    ga_o[...] = (g * g1v).astype(bf16)
    dg = gg[...].astype(f32) * mixed * (sgv * (1.0 - sgv))
    dq = heads(1)
    grad_proj = jnp.concatenate([dq.astype(bf16), heads(2).astype(bf16), heads(3).astype(bf16), dg.astype(bf16)], axis=-1)
    gp_o[...] = grad_proj
    grad_first = split_dot_nt(flag, grad_proj, wq0, wq1)
    s1v = s1[...].astype(f32)
    tn, tscale = norm_parts(tok[...].astype(f32))
    grads = jnp.concatenate(
        [grad_first * tn * (s1v * (1.0 - s1v)), grad_first, g * attn_out * (g1v * (1.0 - g1v))], axis=-1
    )
    low = grads.astype(bf16)
    ml_o[...] = low
    tg_o[...] = g + norm_back(tn, grad_first * s1v + u2[...].astype(f32), tscale)
    dcond = split_dot_nt(flag, low, wc0, wc1) + dcond2[...]
    cx, cscale = norm_parts(cond[...].astype(f32))
    cg_o[...] = norm_back(cx, dcond * cgain[...], cscale)

    @pl.when(pl.program_id(0) == 0)
    def _():
        qbg_o[...] = jnp.zeros_like(qbg_o)
        cbg_o[...] = jnp.zeros_like(cbg_o)
        cgg_o[...] = jnp.zeros_like(cgg_o)

    qbg_o[...] += jnp.sum(dq, axis=0, keepdims=True)
    cbg_o[...] += jnp.sum(grads, axis=0, keepdims=True)
    cgg_o[...] += jnp.sum(dcond * cx, axis=0, keepdims=True)


def back(flag, ys, sg, gg, s1, g1, part, u2, dcond2, tok, cond, og, cgain, wc, wq, wo):
    length, width = tok.shape
    rb = 256
    cs, mw = cond.shape[1], wc[0].shape[1]
    rows = (sg, gg, s1, g1, part, u2, dcond2, tok, cond, og)
    consts = (cgain, *wc, *wq, *wo)

    def out(w, dtype):
        return jax.ShapeDtypeStruct((length, w), dtype)

    shapes = [
        out(width, f32), out(width, f32), out(cs, f32), out(width, bf16), out(width, bf16), out(wq[0].shape[1], bf16), out(mw, bf16),
    ]
    small = [jax.ShapeDtypeStruct((1, w), f32) for w in (width, mw, cs)]
    return pl.pallas_call(
        functools.partial(back_kernel, len(ys)),
        grid_spec=pltpu.PrefetchScalarGridSpec(
            num_scalar_prefetch=1,
            grid=(length // rb,),
            in_specs=[pl.BlockSpec(y.shape[:3] + (rb,), lambda i, _: (0, 0, 0, i)) for y in ys]
            + [row_spec(a, rb) for a in rows]
            + [whole(a) for a in consts],
            out_specs=[row_spec(s, rb) for s in shapes] + [pl.BlockSpec(s.shape, lambda i, _: (0, 0)) for s in small],
        ),
        out_shape=shapes + small,
        compiler_params=params(),
        cost_estimate=pl.CostEstimate(flops=2 * length * width * width * 7, bytes_accessed=40 << 20, transcendentals=length * width),
        name="back",
    )(flag, *ys, *rows, *consts)


def on_device(
    tokens, cond, pair, counts, owner, out_grad, cond_gain, cond_weight, cond_bias, qkvg_weight, query_bias,
    out_weight, pair_gain, pair_weight, up_weight, down_weight,
):
    ups, los, ffs = lax.axis_size("up"), lax.axis_size("lo"), lax.axis_size("fsdp")
    plane = ("lo", "fsdp")
    members = los * ffs
    slots = head_count // members
    length, width = tokens.shape[1:]
    rows = pair.shape[1]
    fs = lax.axis_index("fsdp")

    def halves(w):
        if ffs == 2:
            quarter = w.shape[0] // los
            piece = lax.dynamic_slice_in_dim(w, lax.axis_index("lo") * quarter, quarter)
            got = lax.ppermute(piece, "fsdp", [(0, 1), (1, 0)])
            return w, lax.all_gather(got, "lo", tiled=True)
        full = lax.all_gather(w, "fsdp", axis=0, tiled=True)
        half = full.shape[0] // 2
        return full[:half], full[half:]

    flag = (fs if ffs == 2 else jnp.zeros((), jnp.int32)).astype(jnp.int32).reshape(1)
    wide = 3 * width

    bias = pair_fwd(counts, pair, pair_weight.T, pair_gain[None])
    bias = bias.reshape(members, slots, 2, rows, length)

    def spread(part):
        got = lax.all_to_all(part, plane, 0, 0, tiled=True)
        mine = got.transpose(1, 0, 2, 3).reshape(2, members * rows, length)
        return lax.all_gather(mine, "up", axis=0, tiled=False)

    def summed_up(blocks):
        size, bit = ups, 1
        me = lax.axis_index("up")
        while bit < size:
            pairs = blocks.reshape((blocks.shape[0] // 2, 2) + blocks.shape[1:])
            mine = lax.rem(me // bit, 2)
            sent = lax.dynamic_index_in_dim(pairs, 1 - mine, 1, keepdims=False)
            kept = lax.dynamic_index_in_dim(pairs, mine, 1, keepdims=False)
            got = lax.ppermute(sent, "up", [(i, i ^ bit) for i in range(size)])
            blocks = (kept.astype(f32) + got.astype(f32)).astype(bf16)
            bit *= 2
        return blocks[0]

    wc1 = halves(cond_weight[:, :wide])
    wq = halves(qkvg_weight)
    wo = halves(out_weight)
    biases = [spread(bias[:, t]) for t in range(slots)]
    wc2 = halves(cond_weight[:, wide:])
    wu = halves(up_weight)
    wd = halves(down_weight)

    tok, cnd, og = tokens[0], cond[0], out_grad[0]
    cgain = cond_gain[None]
    *xs, sg, gg, s1, g1, first = front(
        flag, tok, cnd, og, cgain, wc1, cond_bias[None, :wide], wq, query_bias[None], wo, slots
    )
    xs = [lax.all_to_all(x, plane, 0, 0, tiled=True) for x in xs]
    part, u2, dcond2, ml2, cn, second, hid, act, gt, cbg2 = transition(
        flag, tok, cnd, og, cgain, wc2, cond_bias[None, wide:], wu, wd
    )

    def fold(g):
        k, n = g.shape
        if k == width:
            return g
        if k > width:
            times = k // width
            parts = g.reshape(ffs, times, width // ffs, n)
            return jnp.concatenate([parts[:, t] for t in range(times)], axis=-1).reshape(width, n * times)
        times = width // k
        parts = g.reshape(ffs, k // ffs, times, n // times)
        return jnp.concatenate([parts[:, :, t] for t in range(times)], axis=1).reshape(width, n // times)

    def unfold(h, k, n):
        rows_each = width // ffs
        if k == width:
            return h
        if k > width:
            times = k // width
            return jnp.concatenate([h[:, t * n : (t + 1) * n] for t in range(times)], axis=0)
        times = width // k
        step = rows_each // times
        return jnp.concatenate([h[t * step : (t + 1) * step] for t in range(times)], axis=1)

    def reduced(grads):
        folded = [fold(g) for g in grads]
        mine = lax.psum_scatter(
            jnp.concatenate(folded, axis=1), ("fsdp", "up", "lo"), scatter_dimension=0, tiled=True
        )
        full = lax.all_gather(mine, ("up", "lo"), axis=0, tiled=True)
        outs, at = [], 0
        for g, h in zip(grads, folded):
            outs.append(unfold(full[:, at : at + h.shape[1]], *g.shape).astype(f32))
            at += h.shape[1]
        return outs

    up_total, down_total, cond_total2 = reduced(
        [dot_tn(second, hid).astype(bf16), dot_tn(act, gt).astype(bf16), dot_tn(cn, ml2).astype(bf16)]
    )

    owners = lax.dynamic_slice_in_dim(owner, lax.axis_index("up") * members, members)
    ys, bias_grads = [], []
    for t in range(slots):
        y, bg = attention(owners, xs[t], biases[t])
        ys.append(lax.all_to_all(y, plane, 0, 0, tiled=True))
        mine = summed_up(bg)
        mine = mine.reshape(2, members, rows, length).transpose(1, 0, 2, 3)
        bias_grads.append(lax.all_to_all(mine, plane, 0, 0, tiled=True))

    block_out, tokens_grad, cond_grad, gated, ga, gp, ml1, qbg, cbg1, cgg = back(
        flag, ys, sg, gg, s1, g1, part, u2, dcond2, tok, cnd, og, cgain, wc1, wq, wo
    )
    qkvg_total, out_total, cond_total1 = reduced(
        [dot_tn(first, gp).astype(bf16), dot_tn(gated, ga).astype(bf16), dot_tn(cn, ml1).astype(bf16)]
    )

    bias_grad = jnp.stack(bias_grads, axis=1).reshape(head_count, 2, rows, length)
    pw = pair_weight.astype(f32).T
    scaled = pw * pair_gain
    centered = scaled - jnp.mean(scaled, axis=-1, keepdims=True)
    high = centered.astype(bf16)
    low = (centered - high.astype(f32)).astype(bf16)
    pair_grad, moments = pair_bwd(pair, bias_grad, jnp.concatenate([high, low], axis=0))
    pieces = [cgg, cbg1, cbg2, qbg, moments.reshape(1, -1)]
    small = lax.psum(jnp.concatenate([p.reshape(-1, 128) for p in pieces], axis=0), ("up", "lo", "fsdp")).reshape(-1)
    ends = [0]
    for p in pieces:
        ends.append(ends[-1] + p.size)
    small = [small[a:b] for a, b in zip(ends[:-1], ends[1:])]
    moments = small[4].reshape(moments.shape)
    return (
        block_out[None],
        tokens_grad[None],
        cond_grad[None],
        pair_grad,
        small[0],
        jnp.concatenate([cond_total1, cond_total2], axis=1),
        jnp.concatenate([small[1], small[2]]),
        qkvg_total,
        small[3],
        out_total,
        jnp.sum(pw * moments, axis=0),
        (moments * pair_gain).T,
        up_total,
        down_total,
    )


def solution(mesh):
    dp, fsdp = mesh.shape["dp"], mesh.shape["fsdp"]
    lo = max(1, group_size // fsdp)
    fine = Mesh(mesh.devices.reshape(dp // lo, lo, fsdp), ("up", "lo", "fsdp"))
    every = ("up", "lo", "fsdp")
    in_specs = (
        P(every, None, None),
        P(every, None, None),
        P(None, every, None, None),
        P(),
        P(),
        P(every, None, None),
        P(),
        P("fsdp", None),
        P(),
        P("fsdp", None),
        P(),
        P("fsdp", None),
        P(),
        P(),
        P("fsdp", None),
        P("fsdp", None),
    )
    out_specs = (
        P(every, None, None),
        P(every, None, None),
        P(every, None, None),
        P(None, every, None, None),
        P(),
        P("fsdp", None),
        P(),
        P("fsdp", None),
        P(),
        P("fsdp", None),
        P(),
        P(),
        P("fsdp", None),
        P("fsdp", None),
    )
    return jax.shard_map(on_device, mesh=fine, in_specs=in_specs, out_specs=out_specs, check_vma=False)
```

time: 1320 us -> 745 us (0.56)
  waiting for transfers between devices: 702 us -> 300 us
  matrix products: 239 us -> 24.1 us
  Pallas kernels: 0 us -> 171 us
  local copies, waits for them, and re-layouts: 155 us -> 42.8 us
  other arithmetic: 123 us -> 25.3 us
  blocking collectives: 58.7 us -> 125 us
  starting transfers between devices: 16.6 us -> 35.7 us
    all_gather x6 -> x7, waiting for transfers between devices: 291 us -> 0.06 us  [the longest x3 0.04 us: halves(): return (w, lax.all_gather(got, 'lo', tiled=True))]
    psum x1 -> x0, waiting for transfers between devices: 221 us -> none  [on_device(): lax.psum(shards[0].astype(jnp.bfloat16), 'dp').astype(jnp.float32)]
    dot_general x25 -> x6, matrix products: 239 us -> 24.1 us  [dot_tn(): lax.dot_general(a, b, (((0,), (0,)), ((), ())), preferred_element_type=f32)]
    pallas_call x0 -> x7, Pallas kernels: none -> 171 us  [the longest x2 59.2 us: attention(): pl.pallas_call(functools.partial(attn_kernel, length // 2), grid_spec=plt...]
    all_to_all x2 -> x6, waiting for transfers between devices: 187 us -> 29.2 us  [the longest x2 13.3 us: on_device(): xs = [lax.all_to_all(x, plane, 0, 0, tiled=True) for x in xs]]
    ppermute x0 -> x10, waiting for transfers between devices: none -> 156 us  [the longest x4 115 us: summed_up(): got = lax.ppermute(sent, 'up', [(i, i ^ bit) for i in range(size)])]
    unnamed x12 -> x11, waiting for transfers between devices: 3.25 us -> 115 us
    unnamed x149 -> x62, local copies, waits for them, and re-layouts: 78.2 us -> 9.36 us
  transfers between devices with their start and end apart: 14 -> 25, of which waited for: 6 -> 11; matrix products, arithmetic and copies ran while one was open for 32% -> 10% of each run, Pallas kernels for 0% -> 23%
where the time goes in v1:
time: 745 us; the launch traced here: 740 us
  waiting for transfers between devices  300 us (40%)
  Pallas kernels  171 us (23%)
  blocking collectives  125 us (17%)
  local copies, waits for them, and re-layouts  42.8 us (6%)
  starting transfers between devices  35.7 us (5%)
  other arithmetic  25.3 us (3%)
  matrix products  24.1 us (3%)
  between operations  14.7 us (2%)
    unnamed x11, waiting for transfers between devices  115 us
    ppermute x4, waiting for transfers between devices, summed_up(): got = lax.ppermute(sent, 'up', [(i, i ^ bit) for i in range(size)])  115 us
    pallas_call x2, Pallas kernels, attention(): pl.pallas_call(functools.partial(attn_kernel, length // 2), grid_spec=plt...  59.2 us
    ppermute x6, waiting for transfers between devices, halves(): got = lax.ppermute(piece, 'fsdp', [(0, 1), (1, 0)])  40.8 us
    all_to_all x1, blocking collectives, on_device(): ys.append(lax.all_to_all(y, plane, 0, 0, tiled=True))  40.4 us
    psum x1, blocking collectives, on_device(): lax.psum(jnp.concatenate([p.reshape(-1, 128) for p in pieces], axis=0), (...  39.1 us
    pallas_call x1, Pallas kernels, transition(): pl.pallas_call(trans_kernel, grid_spec=pltpu.PrefetchScalarGridSpec(num_s...  28.8 us
    all_gather x3, blocking collectives, halves(): return (w, lax.all_gather(got, 'lo', tiled=True))  26.7 us
  transfers between devices with their start and end apart: 25, of which 11 were waited for; matrix products, arithmetic and copies ran while one was open for 10% of the time, Pallas kernels for 23%

profile of v1, /device:TPU:0, one launch (start us, length us, event | category | flops | bytes accessed | tf_op | source)
XLA Modules:
  0.0 739.6 jit_solution(2728041249806764810)
XLA Ops:
  11.3 7.0 collective-permute-done.5
  22.0 12.8 %collective-permute-done.4 = bf16[96,3072]{1,0:T(8,128)(2,1)S(1)} collective-permute-done((bf16[96,3072]{1,0:T(8,128)(2,1)S(1)}, bf16[96,3072]{1,0:T(8,128)(2,1)S(1)}, u32[]{:S(2)}, u32[]{:S(2)}) %collective-permute-start.4) | collective-permute-done | bytes 589856 | tf_op jit(solution)/shard_map/ppermute | solution.py:478
  38.2 12.3 %collective-permute-done.1 = bf16[96,3072]{1,0:T(8,128)(2,1)S(1)} collective-permute-done((bf16[96,3072]{1,0:T(8,128)(2,1)S(1)}, bf16[96,3072]{1,0:T(8,128)(2,1)S(1)}, u32[]{:S(2)}, u32[]{:S(2)}) %collective-permute-start.1) | collective-permute-done | bytes 589856 | tf_op jit(solution)/shard_map/ppermute | solution.py:478
  51.4 21.2 %pair_fwd.1 = bf16[16,2,24,768]{3,2,1,0:T(8,128)(2,1)} custom-call(s32[2]{0:T(128)} %counts_ref.1, bf16[2,24,768,128]{3,2,1,0:T(8,128)(2,1)} %x_ref.3, bf16[16,128]{1,0:T(8,128)(2,1)} %bitcast.125, f32[1,128]{1,0:T(1,128)} %bitcast.129), custom_call_target="tpu_custom_call" | custom-call | flops 2831155200 | bytes 9437184 | tf_op jit(solution)/shard_map/pair_fwd/pallas_call | solution.py:89
  74.9 19.2 %all_to_all.40 = bf16[8,2,24,768]{3,2,1,0:T(8,128)(2,1)S(1)} all-to-all(bf16[8,2,24,768]{3,2,1,0:T(8,128)(2,1)S(1)} %get-tuple-element.94), channel_id=1, replica_groups=mesh['up'=4,'lo'=4,'fsdp'=2] {'lo','fsdp'}, dimensions={0} | all-to-all | bytes 1179648 | tf_op jit(solution)/shard_map/all_to_all | solution.py:491
  105.9 8.8 %collective-permute-done.2 = bf16[96,768]{1,0:T(8,128)(2,1)S(1)} collective-permute-done((bf16[96,768]{1,0:T(8,128)(2,1)S(1)}, bf16[96,768]{1,0:T(8,128)(2,1)S(1)}, u32[]{:S(2)}, u32[]{:S(2)}) %collective-permute-start.2) | collective-permute-done | bytes 147488 | tf_op jit(solution)/shard_map/ppermute | solution.py:478
  114.6 7.1 all_gather.32.wo1.refs_18_
  121.8 9.7 %all_gather.35.wc1 = bf16[192,2304]{1,0:T(8,128)(2,1)} all-gather(bf16[48,2304]{1,0:T(8,128)(2,1)S(1)} %collective-permute-done.3), channel_id=1, replica_groups=mesh['up'=4,'lo'=4,'fsdp'=2] {'lo'}, dimensions={0}, use_global_device_ids=true | all-gather | bytes 1105920 | tf_op jit(solution)/shard_map/all_gather | solution.py:479
  131.5 9.9 %all_gather.30.wc1.refs_14_ = bf16[192,2304]{1,0:T(8,128)(2,1)} all-gather(bf16[48,2304]{1,0:T(8,128)(2,1)S(1)} %collective-permute-done), channel_id=1, replica_groups=mesh['up'=4,'lo'=4,'fsdp'=2] {'lo'}, dimensions={0}, use_global_device_ids=true | all-gather | bytes 1105920 | tf_op jit(solution)/shard_map/all_gather | solution.py:479
  142.3 28.8 %transition.1 = (f32[768,768]{1,0:T(8,128)}, bf16[768,768]{1,0:T(8,128)(2,1)}, f32[768,384]{1,0:T(8,128)}, bf16[768,2304]{1,0:T(8,128)(2,1)}, bf16[768,384]{1,0:...) custom-call(s32[1]{0:T(128)} %bitcast.flag_ref, ...), custom_call_target="tpu_custom_call" | custom-call | flops 13589544960 | bytes 41943040 | tf_op jit(solution)/shard_map/transition/pallas_call | solution.py:363
  171.1 5.0 convolution_convert_fusion.2
  176.1 3.8 reshape.118
  184.8 16.1 %front.1 = (bf16[8,4,48,768]{3,2,1,0:T(8,128)(2,1)}, bf16[8,4,48,768]{3,2,1,0:T(8,128)(2,1)}, bf16[768,768]{1,0:T(8,128)(2,1)}, bf16[768,768]{1,0:T(8,128)(2,1)}...) custom-call(s32[1]{0:T(128)} %bitcast.flag_ref, bf16[768,768]{1,0:T(8,128)(2,1)} %bitcast.116, ...), custom_call_target="tpu_custom_call" | custom-call | flops 6341787648 | bytes 20971520 | tf_op jit(solution)/shard_map/front/pallas_call | solution.py:286
  200.9 4.4 all-to-all-start.3
  209.1 6.5 convolution_convert_fusion
  216.8 3.7 pad_maximum_fusion
  220.6 13.3 %all-to-all-done.3.x_ref = bf16[8,4,48,768]{3,2,1,0:T(8,128)(2,1)} async-done(((bf16[8,4,48,768]{3,2,1,0:T(8,128)(2,1)}), bf16[8,4,48,768]{3,2,1,0:T(8,128)(2,1)}, u32[]{:S(2)}, u32[]{:S(2)}) %all-to-all-start.3) | async-done | bytes 2359328 | tf_op jit(solution)/shard_map/all_to_all | solution.py:521
  233.9 3.8 all-to-all-start
  238.3 29.6 %attention.3 = (bf16[8,4,48,768]{3,2,1,0:T(8,128)(2,1)}, bf16[4,2,192,768]{3,2,1,0:T(8,128)(2,1)}) custom-call(s32[8]{0:T(128)} %dynamic_slice.39.owner_ref, bf16[8,4,48,768]{3,2,1,0:T(8,128)(2,1)} %all-to-all-done.3.x_ref, bf16[4,2,192,768]{3,2,1,0:T(8,128)(2,1)} %all-gather.12.cloned.1.call-done.bias_ref), custom_call_target="tpu_custom_call" | custom-call | flops 14495514624 | bytes 9437184 | tf_op jit(solution)/shard_map/attention/pallas_call | solution.py:204
  269.3 4.1 all-to-all-start.5
  273.4 29.6 %attention.2 = (bf16[8,4,48,768]{3,2,1,0:T(8,128)(2,1)}, bf16[4,2,192,768]{3,2,1,0:T(8,128)(2,1)}) custom-call(s32[8]{0:T(128)} %dynamic_slice.39.owner_ref, bf16[8,4,48,768]{3,2,1,0:T(8,128)(2,1)} %copy-done.7, bf16[4,2,192,768]{3,2,1,0:T(8,128)(2,1)} %all-gather.10.cloned.1.call-done.bias_ref), custom_call_target="tpu_custom_call" | custom-call | flops 14495514624 | bytes 9437184 | tf_op jit(solution)/shard_map/attention/pallas_call | solution.py:204
  303.0 7.2 all-to-all-done.5.refs_1_
  310.2 40.4 %all_to_all.41.refs_0_ = bf16[8,4,48,768]{3,2,1,0:T(8,128)(2,1)} all-to-all(bf16[8,4,48,768]{3,2,1,0:T(8,128)(2,1)} %get-tuple-element.48), channel_id=1, replica_groups=mesh['up'=4,'lo'=4,'fsdp'=2] {'lo','fsdp'}, dimensions={0} | all-to-all | bytes 4718592 | tf_op jit(solution)/shard_map/all_to_all | solution.py:569
  350.6 20.6 %back.1 = (f32[768,768]{1,0:T(8,128)}, f32[768,768]{1,0:T(8,128)}, f32[768,384]{1,0:T(8,128)}, bf16[768,768]{1,0:T(8,128)(2,1)}, bf16[768,768]{1,0:T(8,128)(2,1)...) custom-call(s32[1]{0:T(128)} %bitcast.flag_ref, ...), custom_call_target="tpu_custom_call" | custom-call | flops 6341787648 | bytes 41943040 | tf_op jit(solution)/shard_map/back/pallas_call | solution.py:445
  381.6 4.1 convolution_convert_fusion.1
  390.2 114.4 %reduce-scatter.7.cloned.1.call-done = bf16[24,4992]{1,0:T(8,128)(2,1)} async-done(((bf16[768,4992]{1,0:T(8,128)(2,1)}), bf16[24,4992]{1,0:T(8,128)(2,1)}) %reduce-scatter.7.cloned.1.call-update) | async-done | bytes 239632
  509.1 50.6 %collective-permute-done.6 = bf16[2,2,192,768]{3,2,1,0:T(8,128)(2,1)} collective-permute-done((bf16[2,2,192,768]{3,2,1,0:T(8,128)(2,1)}, bf16[2,2,192,768]{3,2,1,0:T(8,128)(2,1)}, u32[]{:S(2)}, u32[]{:S(2)}) %collective-permute-start.6) | collective-permute-done | bytes 1179680 | tf_op jit(solution)/shard_map/ppermute | solution.py:503
  562.5 35.0 %collective-permute-done.8 = bf16[2,2,192,768]{3,2,1,0:T(8,128)(2,1)} collective-permute-done((bf16[2,2,192,768]{3,2,1,0:T(8,128)(2,1)S(1)}, bf16[2,2,192,768]{3,2,1,0:T(8,128)(2,1)}, u32[]{:S(2)}, u32[]{:S(2)}) %collective-permute-start.8) | collective-permute-done | bytes 1179680 | tf_op jit(solution)/shard_map/ppermute | solution.py:503
  605.2 29.2 %collective-permute-done.9 = bf16[1,2,192,768]{3,2,1,0:T(8,128)(2,1)S(1)} collective-permute-done((bf16[1,2,192,768]{3,2,1,0:T(8,128)(2,1)S(1)}, bf16[1,2,192,768]{3,2,1,0:T(8,128)(2,1)S(1)}, u32[]{:S(2)}, u32[]{:S(2)}) %collective-permute-start.9) | collective-permute-done | bytes 589856 | tf_op jit(solution)/shard_map/ppermute | solution.py:503
  639.8 8.7 %all-to-all-done.7 = bf16[8,2,24,768]{3,2,1,0:T(8,128)(2,1)S(1)} async-done(((bf16[8,2,24,768]{3,2,1,0:T(8,128)(2,1)}), bf16[8,2,24,768]{3,2,1,0:T(8,128)(2,1)S(1)}, u32[]{:S(2)}, u32[]{:S(2)}) %all-to-all-start.7) | async-done | bytes 589856 | tf_op jit(solution)/shard_map/all_to_all | solution.py:572
  649.7 25.6 %pair_bwd.1 = (f32[2,24,768,128]{3,2,1,0:T(8,128)}, f32[16,128]{1,0:T(8,128)}) custom-call(bf16[2,24,768,128]{3,2,1,0:T(8,128)(2,1)} %x_ref.3, bf16[16,2,24,768]{3,2,1,0:T(8,128)(2,1)} %bitcast.121, bf16[32,128]{1,0:T(8,128)(2,1)} %pad_maximum_fusion.6.a_ref), custom_call_target="tpu_custom_call" | custom-call | flops 4718592000 | bytes 28311552 | tf_op jit(solution)/shard_map/pair_bwd/pallas_call | solution.py:133
  676.5 39.1 %psum.7 = f32[61,128]{1,0:T(8,128)S(1)} all-reduce(f32[61,128]{1,0:T(8,128)S(1)} %concatenate.41), channel_id=1, replica_groups=mesh['up'=4,'lo'=4,'fsdp'=2] {'up','lo','fsdp'}, use_global_device_ids=true, to_apply=%region_1.2 | all-reduce | flops 7808 | bytes 62464 | tf_op jit(solution)/shard_map/psum | solution.py:589
  (170 shorter events, 93.4 us)
Async XLA Ops:
  7.2 135.1 %all-gather.16.cloned.1.call-start = ((), (), s32[]{:S(2)}) async-start(), calls=%async_computation.14 | async-start | bytes 1474560 | tf_op jit(solution)/shard_map/all_gather | solution.py:479
  8.2 10.0 %collective-permute-start.5 = (bf16[192,768]{1,0:T(8,128)(2,1)S(1)}, bf16[192,768]{1,0:T(8,128)(2,1)S(1)}, u32[]{:S(2)}, u32[]{:S(2)}) collective-permute-start(bf16[192,768]{1,0:T(8,128)(2,1)S(1)} %constant_dynamic-slice_fusion.2), channel_id=1, source_target_pairs={{0,1},{1,0},{2,3},{3,2},{4,5},{5,4},{6,7},{7,6},{8,9},{9,8},{10,11... | collective-permute-start | bytes 884744 | tf_op jit(solution)/shard_map/ppermute | solution.py:478
  19.0 123.3 %all-gather.14.cloned.1.call-start = ((), (), s32[]{:S(2)}) async-start(), calls=%async_computation.13 | async-start | bytes 2949120 | tf_op jit(solution)/shard_map/all_gather | solution.py:479
  20.2 14.6 %collective-permute-start.4 = (bf16[96,3072]{1,0:T(8,128)(2,1)S(1)}, bf16[96,3072]{1,0:T(8,128)(2,1)S(1)}, u32[]{:S(2)}, u32[]{:S(2)}) collective-permute-start(bf16[96,3072]{1,0:T(8,128)(2,1)S(1)} %constant_dynamic-slice_fusion.3), channel_id=1, source_target_pairs={{0,1},{1,0},{2,3},{3,2},{4,5},{5,4},{6,7},{7,6},{8,9},{9,8},{10,11... | collective-permute-start | bytes 1769480 | tf_op jit(solution)/shard_map/ppermute | solution.py:478
  35.6 149.2 %all-gather.8.cloned.1.call-start = ((), (), s32[]{:S(2)}) async-start(), calls=%async_computation.10 | async-start | bytes 2949120 | tf_op jit(solution)/shard_map/all_gather | solution.py:479
  36.8 13.8 %collective-permute-start.1 = (bf16[96,3072]{1,0:T(8,128)(2,1)S(1)}, bf16[96,3072]{1,0:T(8,128)(2,1)S(1)}, u32[]{:S(2)}, u32[]{:S(2)}) collective-permute-start(bf16[96,3072]{1,0:T(8,128)(2,1)S(1)} %constant_dynamic-slice_fusion.6), channel_id=1, source_target_pairs={{0,1},{1,0},{2,3},{3,2},{4,5},{5,4},{6,7},{7,6},{8,9},{9,8},{10,11... | collective-permute-start | bytes 1769480 | tf_op jit(solution)/shard_map/ppermute | solution.py:478
  51.4 186.9 %all-gather.12.cloned.1.call-start = ((), (), s32[]{:S(2)}) async-start(), calls=%async_computation.12 | async-start | bytes 2949120 | tf_op jit(solution)/shard_map/all_gather | solution.py:493
  95.2 46.1 %copy-start.9 = (bf16[192,2304]{1,0:T(8,128)(2,1)}, bf16[192,2304]{1,0:T(8,128)(2,1)S(1)}, u32[]{:S(2)}) copy-start(bf16[192,2304]{1,0:T(8,128)(2,1)S(1)} %get-tuple-element.92.wc0) | copy-start | bytes 2654212
  95.3 26.5 %collective-permute-start.3 = (bf16[48,2304]{1,0:T(8,128)(2,1)S(1)}, bf16[48,2304]{1,0:T(8,128)(2,1)S(1)}, u32[]{:S(2)}, u32[]{:S(2)}) collective-permute-start(bf16[48,2304]{1,0:T(8,128)(2,1)S(1)} %constant_dynamic-slice_fusion.4), channel_id=1, source_target_pairs={{0,1},{1,0},{2,3},{3,2},{4,5},{5,4},{6,7},{7,6},{8,9},{9,8},{10,11... | collective-permute-start | bytes 663560 | tf_op jit(solution)/shard_map/ppermute | solution.py:478
  96.8 34.7 %collective-permute-start = (bf16[48,2304]{1,0:T(8,128)(2,1)S(1)}, bf16[48,2304]{1,0:T(8,128)(2,1)S(1)}, u32[]{:S(2)}, u32[]{:S(2)}) collective-permute-start(bf16[48,2304]{1,0:T(8,128)(2,1)S(1)} %constant_dynamic-slice_fusion.7), channel_id=1, source_target_pairs={{0,1},{1,0},{2,3},{3,2},{4,5},{5,4},{6,7},{7,6},{8,9},{9,8},{10,11... | collective-permute-start | bytes 663560 | tf_op jit(solution)/shard_map/ppermute | solution.py:478
  98.6 16.1 %collective-permute-start.2 = (bf16[96,768]{1,0:T(8,128)(2,1)S(1)}, bf16[96,768]{1,0:T(8,128)(2,1)S(1)}, u32[]{:S(2)}, u32[]{:S(2)}) collective-permute-start(bf16[96,768]{1,0:T(8,128)(2,1)S(1)} %constant_dynamic-slice_fusion.5), channel_id=1, source_target_pairs={{0,1},{1,0},{2,3},{3,2},{4,5},{5,4},{6,7},{7,6},{8,9},{9,8},{10,11... | collective-permute-start | bytes 442376 | tf_op jit(solution)/shard_map/ppermute | solution.py:478
  99.9 41.4 %all-to-all-start.1 = ((bf16[8,2,24,768]{3,2,1,0:T(8,128)(2,1)}), bf16[8,2,24,768]{3,2,1,0:T(8,128)(2,1)S(1)}, u32[]{:S(2)}, u32[]{:S(2)}) async-start(bf16[8,2,24,768]{3,2,1,0:T(8,128)(2,1)} %get-tuple-element.95), calls=%async_computation.1 | async-start | bytes 1179648 | tf_op jit(solution)/shard_map/all_to_all | solution.py:491
  103.4 170.0 %all-gather.10.cloned.1.call-start = ((), (), s32[]{:S(2)}) async-start(), calls=%async_computation.11 | async-start | bytes 2949120 | tf_op jit(solution)/shard_map/all_gather | solution.py:493
  200.9 33.0 %all-to-all-start.3 = ((bf16[8,4,48,768]{3,2,1,0:T(8,128)(2,1)}), bf16[8,4,48,768]{3,2,1,0:T(8,128)(2,1)}, u32[]{:S(2)}, u32[]{:S(2)}) async-start(bf16[8,4,48,768]{3,2,1,0:T(8,128)(2,1)} %get-tuple-element.49), calls=%async_computation.3 | async-start | bytes 4718592 | tf_op jit(solution)/shard_map/all_to_all | solution.py:521
  205.3 183.9 %reduce-scatter.9.cloned.1.call-start = ((), (), s32[]{:S(2)}) async-start(), calls=%async_computation.18 | async-start | bytes 9123840
  233.9 34.0 %all-to-all-start = ((bf16[8,4,48,768]{3,2,1,0:T(8,128)(2,1)}), bf16[8,4,48,768]{3,2,1,0:T(8,128)(2,1)S(1)}, u32[]{:S(2)}, u32[]{:S(2)}) async-start(bf16[8,4,48,768]{3,2,1,0:T(8,128)(2,1)} %get-tuple-element.47), calls=%async_computation | async-start | bytes 4718592 | tf_op jit(solution)/shard_map/all_to_all | solution.py:521
  269.3 40.9 %all-to-all-start.5 = ((bf16[8,4,48,768]{3,2,1,0:T(8,128)(2,1)}), bf16[8,4,48,768]{3,2,1,0:T(8,128)(2,1)S(1)}, u32[]{:S(2)}, u32[]{:S(2)}) async-start(bf16[8,4,48,768]{3,2,1,0:T(8,128)(2,1)} %get-tuple-element.50), calls=%async_computation.5 | async-start | bytes 4718592 | tf_op jit(solution)/shard_map/all_to_all | solution.py:569
  273.3 231.2 %reduce-scatter.7.cloned.1.call-start = ((), (), s32[]{:S(2)}) async-start(), calls=%async_computation.17 | async-start | bytes 7907328
  310.2 40.4 %copy-start = (bf16[8,4,48,768]{3,2,1,0:T(8,128)(2,1)}, bf16[8,4,48,768]{3,2,1,0:T(8,128)(2,1)S(1)}, u32[]{:S(2)}) copy-start(bf16[8,4,48,768]{3,2,1,0:T(8,128)(2,1)S(1)} %all-to-all-done.5.refs_1_) | copy-start | bytes 7077892
  389.1 118.9 %copy-start.5 = (bf16[4,2,192,768]{3,2,1,0:T(8,128)(2,1)S(1)}, bf16[4,2,192,768]{3,2,1,0:T(8,128)(2,1)}, u32[]{:S(2)}) copy-start(bf16[4,2,192,768]{3,2,1,0:T(8,128)(2,1)} %get-tuple-element.62) | copy-start | bytes 7077892
  389.2 329.3 %all-gather.20.cloned.1.call-start = ((), (), s32[]{:S(2)}) async-start(), calls=%async_computation.16 | async-start | bytes 4700160 | tf_op jit(solution)/shard_map/all_gather | solution.py:554
  389.9 334.5 %all-gather.18.cloned.1.call-start = ((), (), s32[]{:S(2)}) async-start(), calls=%async_computation.15 | async-start | bytes 4073472 | tf_op jit(solution)/shard_map/all_gather | solution.py:554
  507.0 52.8 %collective-permute-start.6 = (bf16[2,2,192,768]{3,2,1,0:T(8,128)(2,1)}, bf16[2,2,192,768]{3,2,1,0:T(8,128)(2,1)}, u32[]{:S(2)}, u32[]{:S(2)}) collective-permute-start(bf16[2,2,192,768]{3,2,1,0:T(8,128)(2,1)} %dynamic-slice_bitcast_fusion.1), channel_id=1, source_target_pairs={{0,8},{8,0},{16,24},{24,16},{1,9},{9,1},{17,25},{25,17},{2,10},{10... | collective-permute-start | bytes 3538952 | tf_op jit(solution)/shard_map/ppermute | solution.py:503
  508.2 89.4 %collective-permute-start.8 = (bf16[2,2,192,768]{3,2,1,0:T(8,128)(2,1)S(1)}, bf16[2,2,192,768]{3,2,1,0:T(8,128)(2,1)}, u32[]{:S(2)}, u32[]{:S(2)}) collective-permute-start(bf16[2,2,192,768]{3,2,1,0:T(8,128)(2,1)S(1)} %dynamic-slice_bitcast_fusion), channel_id=1, source_target_pairs={{0,8},{8,0},{16,24},{24,16},{1,9},{9,1},{17,25},{25,17},{2,10},{10... | collective-permute-start | bytes 3538952 | tf_op jit(solution)/shard_map/ppermute | solution.py:503
  509.1 88.4 %copy-start.6 = (bf16[4,2,192,768]{3,2,1,0:T(8,128)(2,1)S(1)}, bf16[4,2,192,768]{3,2,1,0:T(8,128)(2,1)}, u32[]{:S(2)}) copy-start(bf16[4,2,192,768]{3,2,1,0:T(8,128)(2,1)} %get-tuple-element.62) | copy-start | bytes 7077892
  562.5 36.9 %collective-permute-start.7 = (bf16[1,2,192,768]{3,2,1,0:T(8,128)(2,1)}, bf16[1,2,192,768]{3,2,1,0:T(8,128)(2,1)}, u32[]{:S(2)}, u32[]{:S(2)}) collective-permute-start(bf16[1,2,192,768]{3,2,1,0:T(8,128)(2,1)} %constant_dynamic-slice_fusion.1), channel_id=1, source_target_pairs={{0,16},{8,24},{16,0},{24,8},{1,17},{9,25},{17,1},{25,9},{2,18},{10... | collective-permute-start | bytes 1769480 | tf_op jit(solution)/shard_map/ppermute | solution.py:503
  599.2 35.2 %collective-permute-start.9 = (bf16[1,2,192,768]{3,2,1,0:T(8,128)(2,1)S(1)}, bf16[1,2,192,768]{3,2,1,0:T(8,128)(2,1)S(1)}, u32[]{:S(2)}, u32[]{:S(2)}) collective-permute-start(bf16[1,2,192,768]{3,2,1,0:T(8,128)(2,1)S(1)} %constant_dynamic-slice_fusion), channel_id=1, source_target_pairs={{0,16},{8,24},{16,0},{24,8},{1,17},{9,25},{17,1},{25,9},{2,18},{10... | collective-permute-start | bytes 1769480 | tf_op jit(solution)/shard_map/ppermute | solution.py:503
  601.5 34.0 %all-to-all-start.6 = ((bf16[8,2,24,768]{3,2,1,0:T(8,128)(2,1)}), bf16[8,2,24,768]{3,2,1,0:T(8,128)(2,1)S(1)}, u32[]{:S(2)}, u32[]{:S(2)}) async-start(bf16[8,2,24,768]{3,2,1,0:T(8,128)(2,1)} %copy.70), calls=%async_computation.6 | async-start | bytes 1179648 | tf_op jit(solution)/shard_map/all_to_all | solution.py:572
  605.1 34.7 %copy-start.16 = (f32[1,2304]{1,0:T(1,128)S(1)}, f32[1,2304]{1,0:T(1,128)}, u32[]{:S(2)}) copy-start(f32[1,2304]{1,0:T(1,128)} %get-tuple-element.65) | copy-start | bytes 27652
  605.1 34.7 %copy-start.19 = (f32[1,768]{1,0:T(1,128)S(1)}, f32[1,768]{1,0:T(1,128)}, u32[]{:S(2)}) copy-start(f32[1,768]{1,0:T(1,128)} %get-tuple-element.67) | copy-start | bytes 9220
  605.1 34.7 %copy-start.21 = (f32[1,384]{1,0:T(1,128)S(1)}, f32[1,384]{1,0:T(1,128)}, u32[]{:S(2)}) copy-start(f32[1,384]{1,0:T(1,128)} %get-tuple-element.64) | copy-start | bytes 4612
  635.5 13.1 %all-to-all-start.7 = ((bf16[8,2,24,768]{3,2,1,0:T(8,128)(2,1)}), bf16[8,2,24,768]{3,2,1,0:T(8,128)(2,1)S(1)}, u32[]{:S(2)}, u32[]{:S(2)}) async-start(bf16[8,2,24,768]{3,2,1,0:T(8,128)(2,1)} %copy.72), calls=%async_computation.7 | async-start | bytes 1179648 | tf_op jit(solution)/shard_map/all_to_all | solution.py:572
  (24 other events, 148.2 us)
Sparse Core Ops, SparseCore 0:
  19.1 18.9 all-gather.15
  40.2 24.0 all-gather.13
  66.5 30.3 all-gather.7
  98.3 50.4 all-gather.11
  150.3 49.2 all-gather.9
  220.7 156.5 reduce-scatter.8
  389.3 115.2 reduce-scatter.6
  507.0 76.6 all-gather.19
  586.0 66.2 all-gather.17

commit v2 on v1

--- a/solution.py
+++ b/solution.py
@@ -52,14 +52,61 @@
     return pl.BlockSpec(a.shape, lambda *_: zero)
 
 
+MESH = pl.DeviceIdType.MESH
+BITS = {"c": ("lo", 1), "x": ("lo", 2), "y": ("fsdp", 1), "z0": ("up", 1), "z1": ("up", 2)}
+PEERS = (("c",), ("x",), ("y",), ("c", "x"), ("c", "y"), ("x", "y"), ("c", "x", "y"))
+ORDERS = (("c", "x", "y", "z0", "z1"), ("c", "y", "z0", "z1", "x"))
+
+
+def coords():
+    return {a: lax.axis_index(a) for a in ("up", "lo", "fsdp")}
+
+
+def bit_of(where, name):
+    axis, value = BITS[name]
+    return lax.rem(where[axis] // value, 2)
+
+
+def across(where, *names):
+    other = dict(where)
+    for name in names:
+        axis, value = BITS[name]
+        other[axis] = other[axis] + value * (1 - 2 * bit_of(where, name))
+    return other
+
+
+def device(where):
+    return (where["up"], where["lo"], where["fsdp"])
+
+
+def place(where):
+    return where["lo"] * 2 + where["fsdp"]
+
+
+def greet(devices):
+    barrier = pltpu.get_barrier_semaphore()
+    for other in devices:
+        pl.semaphore_signal(barrier, inc=1, device_id=device(other), device_id_type=MESH)
+    pl.semaphore_wait(barrier, len(devices))
+
+
+def remote(src, dst, send_sem, recv_sem, other):
+    copy = pltpu.make_async_remote_copy(
+        src_ref=src, dst_ref=dst, send_sem=send_sem, recv_sem=recv_sem, device_id=device(other), device_id_type=MESH
+    )
+    copy.start()
+    return copy
+
+
 def lane_means(values):
-    width = values.shape[-1]
-    return dot(values, jnp.full((width, width), 1.0 / width, bf16))
-
-
-def pair_norm(x):
-    values = x.astype(f32)
-    centered = values - lane_means(x)
+    total = values.shape[-1]
+    group = lax.broadcasted_iota(jnp.int32, (total, total), 0) // 128 == lax.broadcasted_iota(jnp.int32, (total, total), 1) // 128
+    return dot(values, jnp.where(group, 1.0 / 128, 0.0).astype(bf16))
+
+
+def pair_norm(*blocks):
+    x = jnp.concatenate(blocks, axis=-1)
+    centered = x.astype(f32) - lane_means(x)
     variance = lane_means((centered * centered).astype(bf16))
     scale = lax.rsqrt(variance + norm_eps)
     return centered * scale, scale
@@ -74,8 +121,7 @@
     pw = pw_ref[...]
     gain = gain_ref[...]
     for r in range(rows):
-        x_hat, _ = pair_norm(x_ref[0, r])
-        low = (x_hat * gain).astype(bf16)
+        low = (pair_norm(x_ref[0, r])[0] * gain).astype(bf16)
         bias = dot_nt(pw, low)
         scr_ref[:, r, :] = jnp.where(valid, bias * log2e, mask_fill)
     out_ref[:, 0] = scr_ref[...].astype(bf16)
@@ -106,51 +152,194 @@
     )(counts, pair, pw_t, gain)
 
 
-def pair_bwd_kernel(rows, x_ref, bg_ref, a_ref, out_ref, q_ref, scr_ref):
+def pair_bwd_kernel(rows, x_ref, bg_ref, a_ref, out_ref, q_ref, low_buf):
     @pl.when(pl.program_id(0) == 0)
     def _():
         q_ref[...] = jnp.zeros_like(q_ref)
 
-    scr_ref[...] = bg_ref[:, 0].astype(f32)
-    weights = a_ref[...]
-    total = q_ref[...]
     width = out_ref.shape[-1]
-    for r in range(rows):
-        x_hat, scale = pair_norm(x_ref[0, r])
-        grads = scr_ref[:, r, :].astype(bf16)
-        total += dot(grads, x_hat.astype(bf16))
-        u = dot_tn(jnp.concatenate([grads, grads], axis=0), weights)
-        mean_ux = lane_means((u * x_hat).astype(bf16))
-        out_ref[0, r] = (u - x_hat * mean_ux) * scale
-    q_ref[...] = total
-
-
-def pair_bwd(pair, bias_grad, centered_weights):
+    heads, _, _, length = bg_ref.shape
+    grads = bg_ref[:, 0].astype(f32).reshape(heads * rows, length)
+    turned = grads.T.astype(bf16)
+    u_all = dot(jnp.concatenate([turned, turned], axis=1), a_ref[...])
+    step = 2 - rows % 2
+    for r in range(0, rows, step):
+        x_hat, scale = pair_norm(*(x_ref[0, r + t] for t in range(step)))
+        low_buf[:, r * width : (r + step) * width] = x_hat.astype(bf16)
+        u = u_all[:, r * width : (r + step) * width]
+        grad = (u - x_hat * lane_means((u * x_hat).astype(bf16))) * scale
+        for t in range(step):
+            out_ref[0, r + t] = grad[:, t * width : (t + 1) * width]
+    q_ref[...] += dot(grads.astype(bf16), low_buf[...])
+
+
+def pair_bwd(pair, bias_grad, high, low):
     _, total, length, width = pair.shape
     rows = 8 if total % 8 == 0 else total
     steps = total // rows
     heads = bias_grad.shape[0]
-    return pl.pallas_call(
+    eye = jnp.eye(rows, dtype=bf16)
+    both = jnp.stack([high, low])
+    weights = (both[:, :, None, None, :] * eye[None, None, :, :, None]).reshape(2 * heads * rows, rows * width)
+    grad, moments = pl.pallas_call(
         functools.partial(pair_bwd_kernel, rows),
         grid=(2 * steps,),
         in_specs=[
             pl.BlockSpec((1, rows, length, width), lambda i: (i // steps, i % steps, 0, 0)),
             pl.BlockSpec((heads, 1, rows, length), lambda i: (0, i // steps, i % steps, 0)),
-            whole(centered_weights),
+            whole(weights),
         ],
         out_specs=[
             pl.BlockSpec((1, rows, length, width), lambda i: (i // steps, i % steps, 0, 0)),
-            pl.BlockSpec((heads, width), lambda i: (0, 0)),
+            pl.BlockSpec((heads * rows, rows * width), lambda i: (0, 0)),
         ],
         out_shape=[
             jax.ShapeDtypeStruct(pair.shape, f32),
-            jax.ShapeDtypeStruct((heads, width), f32),
+            jax.ShapeDtypeStruct((heads * rows, rows * width), f32),
         ],
-        scratch_shapes=[pltpu.VMEM((heads, rows, length), f32)],
+        scratch_shapes=[pltpu.VMEM((length, rows * width), bf16)],
         compiler_params=params(),
         cost_estimate=pl.CostEstimate(flops=2 * pair.size * 500, bytes_accessed=pair.size * 6, transcendentals=pair.size),
         name="pair_bwd",
-    )(pair, bias_grad, centered_weights)
+    )(pair, bias_grad, weights)
+    moments = moments.reshape(heads, rows, rows, width)
+    return grad, sum(moments[:, r, r] for r in range(rows))
+
+
+class Mover:
+    def __init__(self, where, own, other, send, recv):
+        self.where, self.own, self.other, self.send, self.recv = where, own, other, send, recv
+        self.quarter = own.shape[0] // 4
+        self.copies = []
+
+    def go(self, k, name, src, at):
+        rows = pl.ds(at * self.quarter, self.quarter)
+        self.copies.append(
+            remote(src.at[rows], self.other.at[rows], self.send.at[k], self.recv.at[k], across(self.where, name))
+        )
+
+    def first(self):
+        self.go(0, "y", self.own, self.where["lo"])
+
+    def second(self):
+        self.go(1, "x", self.other, self.where["lo"])
+        self.go(2, "c", self.other, self.where["lo"])
+
+    def third(self):
+        self.copies[1].wait_recv()
+        self.go(3, "c", self.other, across(self.where, "x")["lo"])
+
+    def last(self):
+        self.copies[2].wait_recv()
+        self.copies[3].wait_recv()
+        for copy in self.copies:
+            copy.wait_send()
+
+
+def start_kernel(n_w, counts, pw, gain, pair, *refs):
+    owns, others, spread = refs[:n_w], refs[n_w : 2 * n_w], refs[2 * n_w]
+    x_buf, low_buf, bias_f, bias_v, x_sems, w_send, w_recv, b_send, b_recv, b_sem = refs[2 * n_w + 1 :]
+    where = coords()
+    peers = [across(where, *names) for names in PEERS]
+    total = pair.shape[1]
+    length, width = pair.shape[2:]
+    heads = bias_f.shape[0]
+    groups = 2 * total // 8
+
+    def fetch(g, slot):
+        return pltpu.make_async_copy(
+            pair.at[(g * 8) // total, pl.ds(lax.rem(g * 8, total), 8)], x_buf.at[slot], x_sems.at[slot]
+        )
+
+    fetch(0, 0).start()
+    greet(peers)
+    movers = [Mover(where, owns[i], others[i], w_send.at[i], w_recv.at[i]) for i in range(n_w)]
+    if movers:
+        movers[0].first()
+
+    def group(g, _):
+        slot = lax.rem(g, 2)
+
+        @pl.when(g + 1 < groups)
+        def _():
+            fetch(g + 1, 1 - slot).start()
+
+        fetch(g, slot).wait()
+        for r in range(0, 8, 2):
+            x_hat, _ = pair_norm(x_buf[slot, r], x_buf[slot, r + 1])
+            low_buf[:, r * width : (r + 2) * width] = (x_hat * gain[...]).astype(bf16)
+        bias = dot(low_buf[...], pw[...]).T
+        limit = counts[(g * 8) // total]
+        valid = lax.broadcasted_iota(jnp.int32, bias.shape, 1) < limit
+        bias = jnp.where(valid, bias * log2e, mask_fill)
+        bias_f[:, pl.ds(pl.multiple_of(g * 8, 8), 8), :] = bias.reshape(heads, 8, length)
+        return 0
+
+    lax.fori_loop(0, groups, group, 0)
+    each = heads // (len(PEERS) + 1)
+    bias_v[...] = bias_f[...].astype(bf16).reshape(bias_v.shape)
+
+    keep = pltpu.make_async_copy(bias_v.at[place(where)], spread.at[place(where)], b_sem)
+    keep.start()
+    sent = []
+
+    def send_bias():
+        for k, peer in enumerate(peers):
+            sent.append(remote(bias_v.at[place(peer)], spread.at[place(where)], b_send.at[k], b_recv.at[k], peer))
+
+    for i in range(n_w):
+        movers[i].copies[0].wait_recv()
+        if i + 1 < n_w:
+            movers[i + 1].first()
+        movers[i].second()
+        if i == 0:
+            send_bias()
+        if i:
+            movers[i - 1].third()
+    if not sent:
+        send_bias()
+    if n_w:
+        movers[-1].third()
+    keep.wait()
+    for copy in sent:
+        copy.wait()
+    for m in movers:
+        m.last()
+
+
+def start(counts, pair, pw_big, gain, owns):
+    heads, length, width = 16, pair.shape[2], pair.shape[3]
+    rows = 2 * pair.shape[1]
+    n = len(owns)
+    any_spec = pl.BlockSpec(memory_space=pl.ANY)
+    vm = pl.BlockSpec(memory_space=pltpu.VMEM)
+    return pl.pallas_call(
+        functools.partial(start_kernel, n),
+        in_specs=[pl.BlockSpec(memory_space=pltpu.SMEM), vm, vm, any_spec] + [any_spec] * n,
+        out_specs=[any_spec] * (n + 1),
+        out_shape=[jax.ShapeDtypeStruct(w.shape, bf16) for w in owns]
+        + [jax.ShapeDtypeStruct((8, heads // 8, rows, length), bf16)],
+        scratch_shapes=[
+            pltpu.VMEM((2, 8, length, width), bf16),
+            pltpu.VMEM((length, 8 * width), bf16),
+            pltpu.VMEM((heads, rows, length), f32),
+            pltpu.VMEM((8, heads // 8, rows, length), bf16),
+            pltpu.SemaphoreType.DMA((2,)),
+            pltpu.SemaphoreType.DMA((n, 4)),
+            pltpu.SemaphoreType.DMA((n, 4)),
+            pltpu.SemaphoreType.DMA((7,)),
+            pltpu.SemaphoreType.DMA((7,)),
+            pltpu.SemaphoreType.DMA,
+        ],
+        compiler_params=pltpu.CompilerParams(vmem_limit_bytes=vmem_bytes, collective_id=2, has_side_effects=True),
+        name="start",
+    )(counts, pw_big, gain, pair, *owns)
+
+
+def big_weights(pw):
+    width, heads = pw.shape
+    eye = jnp.eye(8, dtype=pw.dtype)
+    return (eye[:, None, None, :] * pw[None, :, :, None]).reshape(8 * width, heads * 8)
 
 
 def attn_kernel(rb, owner_ref, x_ref, bias_ref, y_ref, bg_ref, acc_ref):
@@ -273,6 +462,10 @@
             xs[t][:, i] = turned[:, t]
 
 
+def half_spec(a, h):
+    return pl.BlockSpec((a.shape[0], a.shape[1] // 2), lambda *_: (0, h))
+
+
 def row_spec(a, rb):
     return pl.BlockSpec((rb, a.shape[1]), lambda i, *_: (i, 0))
 
@@ -289,7 +482,9 @@
             num_scalar_prefetch=1,
             grid=(length // rb,),
             in_specs=[row_spec(tok, rb), row_spec(cond, rb), row_spec(og, rb)]
-            + [whole(a) for a in (cgain, *wc, cb, *wq, qb, *wo)],
+            + [whole(cgain)]
+            + [half_spec(a, 0) for a in wc]
+            + [whole(a) for a in (cb, *wq, qb, *wo)],
             out_specs=[pl.BlockSpec((peers, 4, hd, rb), lambda i, _: (0, 0, 0, i))] * slots + [row_spec(tok, rb)] * 5,
         ),
         out_shape=[payload] * slots + [small] * 5,
@@ -366,7 +561,9 @@
             num_scalar_prefetch=1,
             grid=(length // rb,),
             in_specs=[row_spec(tok, rb), row_spec(cond, rb), row_spec(og, rb)]
-            + [whole(a) for a in (cgain, *wc, cb, *wu, *wd)],
+            + [whole(cgain)]
+            + [half_spec(a, 1) for a in wc]
+            + [whole(a) for a in (cb, *wu, *wd)],
             out_specs=[row_spec(s, rb) for s in shapes] + [pl.BlockSpec((1, mw), lambda i, _: (0, 0))],
         ),
         out_shape=shapes + [jax.ShapeDtypeStruct((1, mw), f32)],
@@ -431,9 +628,9 @@
 def back(flag, ys, sg, gg, s1, g1, part, u2, dcond2, tok, cond, og, cgain, wc, wq, wo):
     length, width = tok.shape
     rb = 256
-    cs, mw = cond.shape[1], wc[0].shape[1]
+    cs, mw = cond.shape[1], wc[0].shape[1] // 2
     rows = (sg, gg, s1, g1, part, u2, dcond2, tok, cond, og)
-    consts = (cgain, *wc, *wq, *wo)
+    consts = (*wq, *wo)
 
     def out(w, dtype):
         return jax.ShapeDtypeStruct((length, w), dtype)
@@ -449,6 +646,8 @@
             grid=(length // rb,),
             in_specs=[pl.BlockSpec(y.shape[:3] + (rb,), lambda i, _: (0, 0, 0, i)) for y in ys]
             + [row_spec(a, rb) for a in rows]
+            + [whole(cgain)]
+            + [half_spec(a, 0) for a in wc]
             + [whole(a) for a in consts],
             out_specs=[row_spec(s, rb) for s in shapes] + [pl.BlockSpec(s.shape, lambda i, _: (0, 0)) for s in small],
         ),
@@ -456,7 +655,208 @@
         compiler_params=params(),
         cost_estimate=pl.CostEstimate(flops=2 * length * width * width * 7, bytes_accessed=40 << 20, transcendentals=length * width),
         name="back",
-    )(flag, *ys, *rows, *consts)
+    )(flag, *ys, *rows, cgain, *wc, *consts)
+
+
+def wgrad_kernel(shape, lhs, rhs, out_ref, turned):
+    @pl.when(pl.program_id(0) == 0)
+    def _():
+        turned[...] = lhs[...].T
+
+    out_ref[...] = dot(turned[...], rhs[...]).astype(bf16).reshape(out_ref.shape)
+
+
+def wgrad(lhs, rhs):
+    length, k = lhs.shape
+    n = rhs.shape[1]
+    row_groups = k // 96
+    col_groups = 16 // row_groups
+    piece = n // col_groups
+    cols = piece if piece <= 1536 else piece // 2
+    steps = n // cols
+    per = piece // cols
+    return pl.pallas_call(
+        functools.partial(wgrad_kernel, None),
+        grid=(steps,),
+        in_specs=[whole(lhs), pl.BlockSpec((length, cols), lambda i: (0, i))],
+        out_specs=pl.BlockSpec((2, row_groups, 48, cols), lambda i: (0, i // per, 0, i % per)),
+        out_shape=jax.ShapeDtypeStruct((2, 16, 48, piece), bf16),
+        scratch_shapes=[pltpu.VMEM((k, length), bf16)],
+        compiler_params=params(),
+        cost_estimate=pl.CostEstimate(flops=2 * length * k * n, bytes_accessed=2 * (length * (k + n) + k * n), transcendentals=0),
+        name="wgrad",
+    )(lhs, rhs)
+
+
+def laid_out(pieces, rows):
+    _, _, cols = pieces.shape
+    row_groups = rows // 48
+    blocks = pieces.reshape(16 // row_groups, rows, cols).astype(f32)
+    return jnp.concatenate([blocks[t] for t in range(blocks.shape[0])], axis=1)
+
+
+def reduce_kernel(plan, n_in, *refs):
+    ins, (small, *outs), scratch = refs[:n_in], refs[n_in : 2 * n_in + 2], refs[2 * n_in + 2 :]
+    small_o, outs = outs[0], outs[1:]
+    n = len(plan)
+    xs, rs = scratch[:n], scratch[n : 2 * n]
+    sbuf, load_sems, send_sems, recv_sems, keep_sems, s_send, s_recv = scratch[2 * n :]
+    where = coords()
+
+    loads = []
+    for i, (a, c0, w, order) in enumerate(plan):
+        src = ins[a]
+        at = ORDERS[order].index("y")
+        before = 1 << at
+        run = 32 >> (at + 1)
+        mine = []
+        for b in range(before):
+            for f in range(2):
+                mine.append(
+                    pltpu.make_async_copy(
+                        src.at[f, pl.ds(b * run, run), :, pl.ds(c0, w)],
+                        xs[i].at[pl.ds((b * 2 + f) * run, run)],
+                        load_sems.at[i, b * 2 + f],
+                    )
+                )
+        for cp in mine:
+            cp.start()
+        loads.append(mine)
+    sbuf[0] = small[...]
+    greet([across(where, name) for name in BITS])
+
+    base = [0] * n
+    size = [32] * n
+    roff = [0] * n
+    pend = [None] * n
+    sends = []
+
+    def rs_start(i, k):
+        name = ORDERS[plan[i][3]][k]
+        half = size[i] // 2
+        b = bit_of(where, name)
+        copy = remote(
+            xs[i].at[pl.ds(base[i] + (1 - b) * half, half)],
+            rs[i].at[pl.ds(roff[i], half)],
+            send_sems.at[i, k],
+            recv_sems.at[i, k],
+            across(where, name),
+        )
+        sends.append(copy)
+        pend[i] = copy
+        base[i] = base[i] + b * half
+        size[i] = half
+
+    def rs_finish(i, k):
+        pend[i].wait_recv()
+        half, b0, r0 = size[i], base[i], roff[i]
+
+        def body(j, _):
+            xs[i][b0 + j] = (xs[i][b0 + j].astype(f32) + rs[i][r0 + j].astype(f32)).astype(bf16)
+            return 0
+
+        lax.fori_loop(0, half, body, 0)
+        roff[i] = r0 + half
+
+    place = [None] * n
+
+    def ag_begin(i):
+        a, c0, w, order = plan[i]
+        p = 0
+        for name in ORDERS[order]:
+            if name != "y":
+                p = p * 2 + bit_of(where, name)
+        place[i] = p
+        copy = pltpu.make_async_copy(
+            xs[i].at[pl.ds(base[i], 1)], outs[a].at[pl.ds(p, 1), :, pl.ds(c0, w)], keep_sems.at[i]
+        )
+        copy.start()
+        copy.wait()
+
+    def ag_start(i, j):
+        a, c0, w, order = plan[i]
+        name = [m for m in ORDERS[order] if m != "y"][3 - j]
+        block = 1 << j
+        start = place[i] - lax.rem(place[i], block)
+        ref = outs[a].at[pl.ds(start, block), :, pl.ds(c0, w)]
+        copy = remote(ref, ref, send_sems.at[i, 5 + j], recv_sems.at[i, 5 + j], across(where, name))
+        sends.append(copy)
+        pend[i] = copy
+
+    def advance(i, k):
+        if k == 0:
+            for cp in loads[i]:
+                cp.wait()
+            rs_start(i, 0)
+        elif k < 5:
+            rs_finish(i, k - 1)
+            rs_start(i, k)
+        elif k == 5:
+            rs_finish(i, 4)
+            ag_begin(i)
+            ag_start(i, 0)
+        elif k < 9:
+            pend[i].wait_recv()
+            ag_start(i, k - 5)
+        else:
+            pend[i].wait_recv()
+
+    def small_step(k):
+        if k > 0:
+            scopy[k - 1].wait_recv()
+            sbuf[2 * k] = sbuf[2 * k - 2] + sbuf[2 * k - 1]
+        if k < 5:
+            name = list(BITS)[k]
+            copy = remote(sbuf.at[2 * k], sbuf.at[2 * k + 1], s_send.at[k], s_recv.at[k], across(where, name))
+            sends.append(copy)
+            scopy.append(copy)
+
+    scopy = []
+    for t in range(10):
+        for i in range(n):
+            advance(i, t)
+            if i == 0 and t < 6:
+                small_step(t)
+    small_o[...] = sbuf[10]
+    for copy in sends:
+        copy.wait_send()
+
+
+def reduce_all(arrays, small, plan):
+    n = len(plan)
+    shapes = [jax.ShapeDtypeStruct(a.shape[1:], bf16) for a in arrays]
+    return pl.pallas_call(
+        functools.partial(reduce_kernel, plan, len(arrays)),
+        out_shape=[jax.ShapeDtypeStruct(small.shape, f32)] + shapes,
+        in_specs=[pl.BlockSpec(memory_space=pl.ANY)] * len(arrays) + [pl.BlockSpec(memory_space=pltpu.VMEM)],
+        out_specs=[pl.BlockSpec(memory_space=pltpu.VMEM)] + [pl.BlockSpec(memory_space=pl.ANY)] * len(arrays),
+        scratch_shapes=[pltpu.VMEM((32, 48, w), bf16) for _, _, w, _ in plan]
+        + [pltpu.VMEM((31, 48, w), bf16) for _, _, w, _ in plan]
+        + [
+            pltpu.VMEM((11,) + small.shape, f32),
+            pltpu.SemaphoreType.DMA((n, 8)),
+            pltpu.SemaphoreType.DMA((n, 9)),
+            pltpu.SemaphoreType.DMA((n, 9)),
+            pltpu.SemaphoreType.DMA((n,)),
+            pltpu.SemaphoreType.DMA((5,)),
+            pltpu.SemaphoreType.DMA((5,)),
+        ],
+        compiler_params=pltpu.CompilerParams(vmem_limit_bytes=vmem_bytes, collective_id=1, has_side_effects=True),
+        name="reduce_grads",
+    )(*arrays, small)
+
+
+reduce_plan = (
+    (0, 0, 768, 0),
+    (0, 768, 768, 1),
+    (1, 0, 640, 0),
+    (1, 640, 512, 1),
+    (2, 0, 384, 1),
+    (3, 0, 768, 0),
+    (3, 768, 768, 1),
+    (4, 0, 384, 0),
+    (4, 384, 384, 1),
+)
 
 
 def on_device(
@@ -470,58 +870,42 @@
     length, width = tokens.shape[1:]
     rows = pair.shape[1]
     fs = lax.axis_index("fsdp")
+    direct = ffs == 2 and los == 4 and ups == 4
 
     def halves(w):
-        if ffs == 2:
-            quarter = w.shape[0] // los
-            piece = lax.dynamic_slice_in_dim(w, lax.axis_index("lo") * quarter, quarter)
-            got = lax.ppermute(piece, "fsdp", [(0, 1), (1, 0)])
-            return w, lax.all_gather(got, "lo", tiled=True)
         full = lax.all_gather(w, "fsdp", axis=0, tiled=True)
         half = full.shape[0] // 2
         return full[:half], full[half:]
 
-    flag = (fs if ffs == 2 else jnp.zeros((), jnp.int32)).astype(jnp.int32).reshape(1)
+    flag = (fs if direct else jnp.zeros((), jnp.int32)).astype(jnp.int32).reshape(1)
     wide = 3 * width
 
-    bias = pair_fwd(counts, pair, pair_weight.T, pair_gain[None])
-    bias = bias.reshape(members, slots, 2, rows, length)
-
-    def spread(part):
-        got = lax.all_to_all(part, plane, 0, 0, tiled=True)
-        mine = got.transpose(1, 0, 2, 3).reshape(2, members * rows, length)
+    def spread(got):
+        mine = got.reshape(members, 2, rows, length).transpose(1, 0, 2, 3).reshape(2, members * rows, length)
         return lax.all_gather(mine, "up", axis=0, tiled=False)
 
-    def summed_up(blocks):
-        size, bit = ups, 1
-        me = lax.axis_index("up")
-        while bit < size:
-            pairs = blocks.reshape((blocks.shape[0] // 2, 2) + blocks.shape[1:])
-            mine = lax.rem(me // bit, 2)
-            sent = lax.dynamic_index_in_dim(pairs, 1 - mine, 1, keepdims=False)
-            kept = lax.dynamic_index_in_dim(pairs, mine, 1, keepdims=False)
-            got = lax.ppermute(sent, "up", [(i, i ^ bit) for i in range(size)])
-            blocks = (kept.astype(f32) + got.astype(f32)).astype(bf16)
-            bit *= 2
-        return blocks[0]
-
-    wc1 = halves(cond_weight[:, :wide])
-    wq = halves(qkvg_weight)
-    wo = halves(out_weight)
-    biases = [spread(bias[:, t]) for t in range(slots)]
-    wc2 = halves(cond_weight[:, wide:])
-    wu = halves(up_weight)
-    wd = halves(down_weight)
+    matrices = (cond_weight, qkvg_weight, out_weight, up_weight, down_weight)
+    if direct:
+        *others, spreads = start(counts, pair, big_weights(pair_weight), jnp.tile(pair_gain, 2)[None], matrices)
+        wc, wq, wo, wu, wd = zip(matrices, others)
+    else:
+        bias = pair_fwd(counts, pair, pair_weight.T, pair_gain[None])
+        bias = bias.reshape(members, slots, 2 * rows, length)
+        spreads = lax.all_to_all(bias, plane, 0, 0, tiled=True)
+        wc, wq, wo, wu, wd = [halves(w) for w in matrices]
+    biases = [spread(spreads[:, t]) for t in range(slots)]
 
     tok, cnd, og = tokens[0], cond[0], out_grad[0]
     cgain = cond_gain[None]
     *xs, sg, gg, s1, g1, first = front(
-        flag, tok, cnd, og, cgain, wc1, cond_bias[None, :wide], wq, query_bias[None], wo, slots
+        flag, tok, cnd, og, cgain, wc, cond_bias[None, :wide], wq, query_bias[None], wo, slots
     )
-    xs = [lax.all_to_all(x, plane, 0, 0, tiled=True) for x in xs]
+    xs[0] = lax.all_to_all(xs[0], plane, 0, 0, tiled=True)
     part, u2, dcond2, ml2, cn, second, hid, act, gt, cbg2 = transition(
-        flag, tok, cnd, og, cgain, wc2, cond_bias[None, wide:], wu, wd
+        flag, tok, cnd, og, cgain, wc, cond_bias[None, wide:], wu, wd
     )
+    *xs, hid = lax.optimization_barrier((*xs, hid))
+    xs = [xs[0]] + [lax.all_to_all(x, plane, 0, 0, tiled=True) for x in xs[1:]]
 
     def fold(g):
         k, n = g.shape
@@ -558,25 +942,29 @@
             at += h.shape[1]
         return outs
 
-    up_total, down_total, cond_total2 = reduced(
-        [dot_tn(second, hid).astype(bf16), dot_tn(act, gt).astype(bf16), dot_tn(cn, ml2).astype(bf16)]
-    )
+    if direct:
+        early = [wgrad(second, hid), wgrad(act, gt)]
+        xs[0], *early = lax.optimization_barrier((xs[0], *early))
+    else:
+        up_total, down_total = reduced([dot_tn(second, hid).astype(bf16), dot_tn(act, gt).astype(bf16)])
 
     owners = lax.dynamic_slice_in_dim(owner, lax.axis_index("up") * members, members)
     ys, bias_grads = [], []
     for t in range(slots):
         y, bg = attention(owners, xs[t], biases[t])
         ys.append(lax.all_to_all(y, plane, 0, 0, tiled=True))
-        mine = summed_up(bg)
+        mine = lax.psum_scatter(bg, "up", scatter_dimension=0, tiled=True)
         mine = mine.reshape(2, members, rows, length).transpose(1, 0, 2, 3)
         bias_grads.append(lax.all_to_all(mine, plane, 0, 0, tiled=True))
 
     block_out, tokens_grad, cond_grad, gated, ga, gp, ml1, qbg, cbg1, cgg = back(
-        flag, ys, sg, gg, s1, g1, part, u2, dcond2, tok, cnd, og, cgain, wc1, wq, wo
+        flag, ys, sg, gg, s1, g1, part, u2, dcond2, tok, cnd, og, cgain, wc, wq, wo
     )
-    qkvg_total, out_total, cond_total1 = reduced(
-        [dot_tn(first, gp).astype(bf16), dot_tn(gated, ga).astype(bf16), dot_tn(cn, ml1).astype(bf16)]
-    )
+    ml = jnp.concatenate([ml1, ml2], axis=1)
+    if not direct:
+        qkvg_total, out_total, cond_total = reduced(
+            [dot_tn(first, gp).astype(bf16), dot_tn(gated, ga).astype(bf16), dot_tn(cn, ml).astype(bf16)]
+        )
 
     bias_grad = jnp.stack(bias_grads, axis=1).reshape(head_count, 2, rows, length)
     pw = pair_weight.astype(f32).T
@@ -584,9 +972,20 @@
     centered = scaled - jnp.mean(scaled, axis=-1, keepdims=True)
     high = centered.astype(bf16)
     low = (centered - high.astype(f32)).astype(bf16)
-    pair_grad, moments = pair_bwd(pair, bias_grad, jnp.concatenate([high, low], axis=0))
+    pair_grad, moments = pair_bwd(pair, bias_grad, high, low)
     pieces = [cgg, cbg1, cbg2, qbg, moments.reshape(1, -1)]
-    small = lax.psum(jnp.concatenate([p.reshape(-1, 128) for p in pieces], axis=0), ("up", "lo", "fsdp")).reshape(-1)
+    stacked = jnp.concatenate([p.reshape(-1, 128) for p in pieces], axis=0)
+    if direct:
+        height = -(-stacked.shape[0] // 8) * 8
+        stacked = jnp.pad(stacked, ((0, height - stacked.shape[0]), (0, 0)))
+        late = [wgrad(first, gp), wgrad(cn, ml), wgrad(gated, ga)]
+        stacked, *totals = reduce_all(late + early, stacked, reduce_plan)
+        qkvg_total, cond_total, out_total, up_total, down_total = [
+            laid_out(p, w.shape[0]) for p, w in zip(totals, (qkvg_weight, cond_weight, out_weight, up_weight, down_weight))
+        ]
+    else:
+        stacked = lax.psum(stacked, ("up", "lo", "fsdp"))
+    small = stacked.reshape(-1)
     ends = [0]
     for p in pieces:
         ends.append(ends[-1] + p.size)
@@ -598,7 +997,7 @@
         cond_grad[None],
         pair_grad,
         small[0],
-        jnp.concatenate([cond_total1, cond_total2], axis=1),
+        cond_total,
         jnp.concatenate([small[1], small[2]]),
         qkvg_total,
         small[3],

time: 745 us -> 571 us (0.77)
  waiting for transfers between devices: 300 us -> 29.7 us
  Pallas kernels: 171 us -> 417 us
  blocking collectives: 125 us -> 32.6 us
  matrix products: 24.1 us -> 0 us
  local copies, waits for them, and re-layouts: 42.8 us -> 24.5 us
  starting transfers between devices: 35.7 us -> 20.1 us
    pallas_call x1 -> x7, Pallas kernels: 21.2 us -> 275 us  [the longest x1 160 us: reduce_all(): pl.pallas_call(functools.partial(reduce_kernel, plan, len(arrays)), out_s...]
    ppermute x10 -> x0, waiting for transfers between devices: 156 us -> none  [the longest x4 115 us: summed_up(): got = lax.ppermute(sent, 'up', [(i, i ^ bit) for i in range(size)])]
    unnamed x11 -> x4, waiting for transfers between devices: 115 us -> 0.07 us
    psum x1 -> x0, blocking collectives: 39.1 us -> none  [on_device(): lax.psum(jnp.concatenate([p.reshape(-1, 128) for p in pieces], axis=0), (...]
    all_to_all x2 -> x1, blocking collectives: 59.7 us -> 32.6 us  [on_device(): xs = [xs[0]] + [lax.all_to_all(x, plane, 0, 0, tiled=True) for x in xs[1:]]]
    all_gather x3 -> x0, blocking collectives: 26.7 us -> none  [halves(): return (w, lax.all_gather(got, 'lo', tiled=True))]
    dot_general x6 -> x0, matrix products: 24.1 us -> none  [dot_tn(): lax.dot_general(a, b, (((0,), (0,)), ((), ())), preferred_element_type=f32)]
    all_to_all x1 -> x2, waiting for transfers between devices: 7.16 us -> 27.4 us  [on_device(): ys.append(lax.all_to_all(y, plane, 0, 0, tiled=True))]
  transfers between devices with their start and end apart: 25 -> 9, of which waited for: 11 -> 2; matrix products, arithmetic and copies ran while one was open for 10% -> 3% of each run, Pallas kernels for 23% -> 28%
where the time goes in v2:
time: 571 us; the launch traced here: 565 us
  Pallas kernels  417 us (73%)
  blocking collectives  32.6 us (6%)
  waiting for transfers between devices  29.7 us (5%)
  other arithmetic  26.1 us (5%)
  local copies, waits for them, and re-layouts  24.5 us (4%)
  starting transfers between devices  20.1 us (4%)
  between operations  14.6 us (3%)
    pallas_call x1, Pallas kernels, reduce_all(): pl.pallas_call(functools.partial(reduce_kernel, plan, len(arrays)), out_s...  160 us
    pallas_call x1, Pallas kernels, start(): pl.pallas_call(functools.partial(start_kernel, n), in_specs=[pl.BlockSpec...  81.5 us
    pallas_call x2, Pallas kernels, attention(): pl.pallas_call(functools.partial(attn_kernel, length // 2), grid_spec=plt...  59.1 us
    pallas_call x5, Pallas kernels, wgrad(): pl.pallas_call(functools.partial(wgrad_kernel, None), grid=(steps,), in_s...  33.9 us
    all_to_all x1, blocking collectives, on_device(): xs = [xs[0]] + [lax.all_to_all(x, plane, 0, 0, tiled=True) for x in xs[1:]]  32.6 us
    pallas_call x1, Pallas kernels, transition(): pl.pallas_call(trans_kernel, grid_spec=pltpu.PrefetchScalarGridSpec(num_s...  29.2 us
    all_to_all x2, waiting for transfers between devices, on_device(): ys.append(lax.all_to_all(y, plane, 0, 0, tiled=True))  27.4 us
    pallas_call x1, Pallas kernels, back(): pl.pallas_call(functools.partial(back_kernel, len(ys)), grid_spec=pltpu.P...  20.3 us
  transfers between devices with their start and end apart: 9, of which 2 were waited for; matrix products, arithmetic and copies ran while one was open for 3% of the time, Pallas kernels for 28%

profile of v2, /device:TPU:0, one launch (start us, length us, event | category | flops | bytes accessed | tf_op | source)
XLA Modules:
  0.0 564.9 jit_solution(16712533409000963742)
XLA Ops:
  10.1 81.5 %start.1 = (bf16[192,4608]{1,0:T(8,128)(2,1)}, bf16[384,3072]{1,0:T(8,128)(2,1)}, bf16[384,768]{1,0:T(8,128)(2,1)}, bf16[384,3072]{1,0:T(8,128)(2,1)}, bf16[768,...) custom-call(s32[2]{0:T(128)} %counts.1, bf16[1024,128]{1,0:T(8,128)(2,1)} %copy.49.pw, f32[1,256]{1,0:T(1,128)} %bitcast.146, ...), custom_call_target="tpu_custom_call" | custom-call | tf_op jit(solution)/shard_map/start/pallas_call | solution.py:316
  95.7 15.8 %front.1 = (bf16[8,4,48,768]{3,2,1,0:T(8,128)(2,1)}, bf16[8,4,48,768]{3,2,1,0:T(8,128)(2,1)}, bf16[768,768]{1,0:T(8,128)(2,1)}, bf16[768,768]{1,0:T(8,128)(2,1)}...) custom-call(s32[1]{0:T(128)} %bitcast.flag_ref, bf16[768,768]{1,0:T(8,128)(2,1)} %bitcast.120, ...), custom_call_target="tpu_custom_call" | custom-call | flops 6341787648 | bytes 20971520 | tf_op jit(solution)/shard_map/front/pallas_call | solution.py:479
  111.5 3.7 all-to-all-start
  117.6 29.2 %transition.1 = (f32[768,768]{1,0:T(8,128)}, bf16[768,768]{1,0:T(8,128)(2,1)}, f32[768,384]{1,0:T(8,128)}, bf16[768,2304]{1,0:T(8,128)(2,1)}, bf16[768,384]{1,0:...) custom-call(s32[1]{0:T(128)} %bitcast.flag_ref, ...), custom_call_target="tpu_custom_call" | custom-call | flops 13589544960 | bytes 41943040 | tf_op jit(solution)/shard_map/transition/pallas_call | solution.py:558
  146.8 5.5 wgrad.6.refs_4_
  152.3 8.7 %wgrad.5.refs_3_ = bf16[2,16,48,1536]{3,2,1,0:T(8,128)(2,1)} custom-call(bf16[768,768]{1,0:T(8,128)(2,1)} %get-tuple-element.74.lhs, bf16[768,3072]{1,0:T(8,128)(2,1)} %get-tuple-element.75.rhs), custom_call_target="tpu_custom_call" | custom-call | flops 3623878656 | bytes 10616832 | tf_op jit(solution)/shard_map/wgrad/pallas_call | solution.py:678
  161.0 29.6 %attention.2 = (bf16[8,4,48,768]{3,2,1,0:T(8,128)(2,1)}, bf16[4,2,192,768]{3,2,1,0:T(8,128)(2,1)}) custom-call(s32[8]{0:T(128)} %dynamic_slice.3.owner_ref, bf16[8,4,48,768]{3,2,1,0:T(8,128)(2,1)} %copy-done.6, bf16[4,2,192,768]{3,2,1,0:T(8,128)(2,1)} %all-gather.3.cloned.1.call-done.bias_ref), custom_call_target="tpu_custom_call" | custom-call | flops 14495514624 | bytes 9437184 | tf_op jit(solution)/shard_map/attention/pallas_call | solution.py:393
  190.7 1.6 copy-done.5
  192.3 32.6 %all_to_all.30.x_ref = bf16[8,4,48,768]{3,2,1,0:T(8,128)(2,1)} all-to-all(bf16[8,4,48,768]{3,2,1,0:T(8,128)(2,1)S(1)} %copy-done.5), channel_id=1, replica_groups=mesh['up'=4,'lo'=4,'fsdp'=2] {'lo','fsdp'}, dimensions={0} | all-to-all | bytes 4718592 | tf_op jit(solution)/shard_map/all_to_all | solution.py:908
  224.9 3.6 all-to-all-start.1
  228.6 29.4 %attention.3 = (bf16[8,4,48,768]{3,2,1,0:T(8,128)(2,1)}, bf16[4,2,192,768]{3,2,1,0:T(8,128)(2,1)}) custom-call(s32[8]{0:T(128)} %dynamic_slice.3.owner_ref, bf16[8,4,48,768]{3,2,1,0:T(8,128)(2,1)} %all_to_all.30.x_ref, bf16[4,2,192,768]{3,2,1,0:T(8,128)(2,1)} %all-gather.5.cloned.1.call-done.bias_ref), custom_call_target="tpu_custom_call" | custom-call | flops 14495514624 | bytes 9437184 | tf_op jit(solution)/shard_map/attention/pallas_call | solution.py:393
  259.5 4.4 all-to-all-start.3
  265.1 27.4 %all-to-all-done.3.refs_1_ = bf16[8,4,48,768]{3,2,1,0:T(8,128)(2,1)} async-done(((bf16[8,4,48,768]{3,2,1,0:T(8,128)(2,1)}), bf16[8,4,48,768]{3,2,1,0:T(8,128)(2,1)}, u32[]{:S(2)}, u32[]{:S(2)}) %all-to-all-start.3) | async-done | bytes 2359328 | tf_op jit(solution)/shard_map/all_to_all | solution.py:955
  292.5 20.3 %back.1 = (f32[768,768]{1,0:T(8,128)}, f32[768,768]{1,0:T(8,128)}, f32[768,384]{1,0:T(8,128)}, bf16[768,768]{1,0:T(8,128)(2,1)}, bf16[768,768]{1,0:T(8,128)(2,1)...) custom-call(s32[1]{0:T(128)} %bitcast.flag_ref, ...), custom_call_target="tpu_custom_call" | custom-call | flops 6341787648 | bytes 41943040 | tf_op jit(solution)/shard_map/back/pallas_call | solution.py:642
  316.7 4.4 wgrad.9.refs_2_
  321.0 1.9 copy.77
  322.9 4.4 all-to-all-start.4
  327.4 5.5 pad_maximum_fusion.rhs
  332.9 1.9 copy.76
  334.8 2.2 all-to-all-done.4
  337.0 3.5 all-to-all-start.5
  340.5 7.5 %wgrad.8.refs_1_ = bf16[2,16,48,1152]{3,2,1,0:T(8,128)(2,1)} custom-call(bf16[768,384]{1,0:T(8,128)(2,1)} %get-tuple-element.98.lhs, bf16[768,4608]{1,0:T(8,128)(2,1)} %pad_maximum_fusion.rhs), custom_call_target="tpu_custom_call" | custom-call | flops 2717908992 | bytes 11206656 | tf_op jit(solution)/shard_map/wgrad/pallas_call | solution.py:678
  348.1 7.8 %wgrad.7.refs_0_ = bf16[2,16,48,1536]{3,2,1,0:T(8,128)(2,1)} custom-call(bf16[768,768]{1,0:T(8,128)(2,1)} %get-tuple-element.96.lhs, bf16[768,3072]{1,0:T(8,128)(2,1)} %get-tuple-element.97.rhs), custom_call_target="tpu_custom_call" | custom-call | flops 3623878656 | bytes 10616832 | tf_op jit(solution)/shard_map/wgrad/pallas_call | solution.py:678
  355.8 2.2 pad_maximum_fusion.4
  358.0 17.8 %pair_bwd.1 = (f32[2,24,768,128]{3,2,1,0:T(8,128)}, f32[128,1024]{1,0:T(8,128)}) custom-call(bf16[2,24,768,128]{3,2,1,0:T(8,128)(2,1)} %x_ref.1, bf16[16,2,24,768]{3,2,1,0:T(8,128)(2,1)} %bitcast.119, bf16[256,1024]{1,0:T(8,128)(2,1)} %bitcast.132), custom_call_target="tpu_custom_call" | custom-call | flops 4718592000 | bytes 28311552 | tf_op jit(solution)/shard_map/pair_bwd/pallas_call | solution.py:184
  378.2 159.9 %reduce_grads.1 = (f32[64,128]{1,0:T(8,128)}, bf16[16,48,1536]{2,1,0:T(8,128)(2,1)}, bf16[16,48,1152]{2,1,0:T(8,128)(2,1)}, bf16[16,48,384]{2,1,0:T(8,128)(2,1)}...) custom-call(bf16[2,16,48,1536]{3,2,1,0:T(8,128)(2,1)} %wgrad.7.refs_0_, ...), custom_call_target="tpu_custom_call" | custom-call | tf_op jit(solution)/shard_map/reduce_grads/pallas_call | solution.py:828
  538.1 1.4 slice_bitcast_fusion.3
  540.8 1.8 multiply_bitcast_fusion.1
  545.8 1.7 bitcast_convert_fusion
  550.5 2.6 pad_maximum_fusion.2
  553.1 2.6 pad_maximum_fusion.1
  555.7 2.2 pad_maximum_fusion.3
  (87 shorter events, 25.6 us)
Async XLA Ops:
  7.2 153.9 %all-gather.3.cloned.1.call-start = ((), (), s32[]{:S(2)}) async-start(), calls=%async_computation.8 | async-start | bytes 2949120 | tf_op jit(solution)/shard_map/all_gather | solution.py:885
  91.6 2.3 copy-start.17
  91.7 2.8 copy-start.16
  91.7 3.4 copy-start.10
  111.5 5.5 copy-start.18
  111.5 40.8 %all-to-all-start = ((bf16[8,4,48,768]{3,2,1,0:T(8,128)(2,1)}), bf16[8,4,48,768]{3,2,1,0:T(8,128)(2,1)S(1)}, u32[]{:S(2)}, u32[]{:S(2)}) async-start(bf16[8,4,48,768]{3,2,1,0:T(8,128)(2,1)} %get-tuple-element.68), calls=%async_computation | async-start | bytes 4718592 | tf_op jit(solution)/shard_map/all_to_all | solution.py:903
  115.2 113.4 %all-gather.5.cloned.1.call-start = ((), (), s32[]{:S(2)}) async-start(), calls=%async_computation.9 | async-start | bytes 2949120 | tf_op jit(solution)/shard_map/all_gather | solution.py:885
  116.2 204.9 %reduce-scatter.3.cloned.1.call-start = ((), (), s32[]{:S(2)}) async-start(), calls=%async_computation.10 | async-start | bytes 2949120 | tf_op jit(solution)/shard_map/reduce_scatter | solution.py:956
  152.3 8.8 %copy-start.6 = (bf16[8,4,48,768]{3,2,1,0:T(8,128)(2,1)}, bf16[8,4,48,768]{3,2,1,0:T(8,128)(2,1)S(1)}, u32[]{:S(2)}) copy-start(bf16[8,4,48,768]{3,2,1,0:T(8,128)(2,1)S(1)} %all-to-all-done.x_ref) | copy-start | bytes 7077892
  190.7 1.7 copy-start.5
  224.9 33.2 %all-to-all-start.1 = ((bf16[8,4,48,768]{3,2,1,0:T(8,128)(2,1)}), bf16[8,4,48,768]{3,2,1,0:T(8,128)(2,1)S(1)}, u32[]{:S(2)}, u32[]{:S(2)}) async-start(bf16[8,4,48,768]{3,2,1,0:T(8,128)(2,1)} %get-tuple-element.80), calls=%async_computation.1 | async-start | bytes 4718592 | tf_op jit(solution)/shard_map/all_to_all | solution.py:955
  228.5 104.4 %reduce-scatter.5.cloned.1.call-start = ((), (), s32[]{:S(2)}) async-start(), calls=%async_computation.11 | async-start | bytes 2949120 | tf_op jit(solution)/shard_map/reduce_scatter | solution.py:956
  258.1 1.4 copy-start
  258.1 5.8 %copy-start.12 = (f32[1,2304]{1,0:T(1,128)S(1)}, f32[1,2304]{1,0:T(1,128)}, u32[]{:S(2)}) copy-start(f32[1,2304]{1,0:T(1,128)} %get-tuple-element.107) | copy-start | bytes 27652
  258.1 5.8 %copy-start.8 = (bf16[128,16]{0,1:T(8,128)(2,1)S(1)}, bf16[128,16]{0,1:T(8,128)(2,1)}, u32[]{:S(2)}) copy-start(bf16[128,16]{0,1:T(8,128)(2,1)} %param.29) | copy-start | bytes 12292
  258.1 5.8 %copy-start.14 = (f32[128]{0:T(128)S(1)}, f32[128]{0:T(128)}, u32[]{:S(2)}) copy-start(f32[128]{0:T(128)} %param.28) | copy-start | bytes 1540
  259.5 33.0 %all-to-all-start.3 = ((bf16[8,4,48,768]{3,2,1,0:T(8,128)(2,1)}), bf16[8,4,48,768]{3,2,1,0:T(8,128)(2,1)}, u32[]{:S(2)}, u32[]{:S(2)}) async-start(bf16[8,4,48,768]{3,2,1,0:T(8,128)(2,1)} %get-tuple-element.82), calls=%async_computation.3 | async-start | bytes 4718592 | tf_op jit(solution)/shard_map/all_to_all | solution.py:955
  316.7 10.7 %copy-start.4 = (bf16[768,2304]{1,0:T(8,128)(2,1)S(1)}, bf16[768,2304]{1,0:T(8,128)(2,1)}, u32[]{:S(2)}) copy-start(bf16[768,2304]{1,0:T(8,128)(2,1)} %get-tuple-element.100) | copy-start | bytes 10616836
  322.9 14.0 %all-to-all-start.4 = ((bf16[8,2,24,768]{3,2,1,0:T(8,128)(2,1)}), bf16[8,2,24,768]{3,2,1,0:T(8,128)(2,1)}, u32[]{:S(2)}, u32[]{:S(2)}) async-start(bf16[8,2,24,768]{3,2,1,0:T(8,128)(2,1)} %bitcast.113), calls=%async_computation.5 | async-start | bytes 1179648 | tf_op jit(solution)/shard_map/all_to_all | solution.py:958
  337.0 18.8 %all-to-all-start.5 = ((bf16[8,2,24,768]{3,2,1,0:T(8,128)(2,1)}), bf16[8,2,24,768]{3,2,1,0:T(8,128)(2,1)S(1)}, u32[]{:S(2)}, u32[]{:S(2)}) async-start(bf16[8,2,24,768]{3,2,1,0:T(8,128)(2,1)} %bitcast.99), calls=%async_computation.7 | async-start | bytes 1179648 | tf_op jit(solution)/shard_map/all_to_all | solution.py:958
  358.0 19.0 %copy-start.9 = (f32[2304]{0:T(1024)S(1)}, f32[2304]{0:T(1024)}, u32[]{:S(2)}) copy-start(f32[2304]{0:T(1024)} %reduce.1) | copy-start | bytes 27652
  358.0 19.0 %copy-start.11 = (f32[768]{0:T(1024)S(1)}, f32[768]{0:T(1024)}, u32[]{:S(2)}) copy-start(f32[768]{0:T(1024)} %reduce.3) | copy-start | bytes 9220
  358.0 19.0 %copy-start.13 = (f32[384]{0:T(512)S(1)}, f32[384]{0:T(512)}, u32[]{:S(2)}) copy-start(f32[384]{0:T(512)} %reduce) | copy-start | bytes 4612
  378.2 162.6 %copy-start.15 = (f32[128]{0:T(128)S(1)}, f32[128]{0:T(128)}, u32[]{:S(2)}) copy-start(f32[128]{0:T(128)} %param.28) | copy-start | bytes 1540
  538.1 6.4 %copy-start.3 = (bf16[16,48,1152]{2,1,0:T(8,128)(2,1)S(1)}, bf16[16,48,1152]{2,1,0:T(8,128)(2,1)}, u32[]{:S(2)}) copy-start(bf16[16,48,1152]{2,1,0:T(8,128)(2,1)} %get-tuple-element.111) | copy-start | bytes 5308420
  544.6 1.3 copy-start.7
  545.8 3.4 copy-start.1
  545.8 3.4 copy-start.2
Sparse Core Ops, SparseCore 0:
  94.0 51.7 all-gather.2
  147.4 49.2 all-gather.4
  199.6 46.8 reduce-scatter.2
  258.2 49.7 reduce-scatter.4

commit v3 on v2

v3 whole, which is shorter than its diff:
```python
import functools

import jax
import jax.numpy as jnp
from jax import lax
from jax.experimental import pallas as pl
from jax.experimental.pallas import tpu as pltpu
from jax.sharding import Mesh, PartitionSpec as P

f32, bf16 = jnp.float32, jnp.bfloat16
norm_eps = 1e-05
mask_fill = -1000000000.0
log2e = 1.4426950408889634
ln2 = 0.6931471805599453
head_count = 16
group_size = 8
vmem_bytes = 58 << 20
nt_dims = (((1,), (1,)), ((), ()))


def dot(a, b):
    return jnp.dot(a, b, preferred_element_type=f32)


def dot_nt(a, b):
    return lax.dot_general(a, b, nt_dims, preferred_element_type=f32)


def dot_tn(a, b):
    return lax.dot_general(a, b, (((0,), (0,)), ((), ())), preferred_element_type=f32)


def norm_parts(values):
    centered = values - jnp.mean(values, axis=-1, keepdims=True)
    variance = jnp.mean(centered * centered, axis=-1, keepdims=True)
    scale = lax.rsqrt(variance + norm_eps)
    return centered * scale, scale


def norm_back(x, u, scale):
    mean_u = jnp.mean(u, axis=-1, keepdims=True)
    mean_ux = jnp.mean(u * x, axis=-1, keepdims=True)
    return (u - mean_u - x * mean_ux) * scale


def params(**kw):
    return pltpu.CompilerParams(vmem_limit_bytes=vmem_bytes, **kw)


def whole(a):
    zero = (0,) * a.ndim
    return pl.BlockSpec(a.shape, lambda *_: zero)


MESH = pl.DeviceIdType.MESH
BITS = {"c": ("lo", 1), "x": ("lo", 2), "y": ("fsdp", 1), "z0": ("up", 1), "z1": ("up", 2)}
PEERS = (("c",), ("x",), ("y",), ("c", "x"), ("c", "y"), ("x", "y"), ("c", "x", "y"))
SAMPLE_ORDER = (("x",), ("y",), ("x", "y"), ("c", "x"), ("c", "y"), ("c", "x", "y"), ("c",), ())
SUM_ORDERS = (("c", "x", "y", "z0", "z1"), ("c", "y", "z0", "x", "z1"), ("c", "z0", "x", "y", "z1"))
COPY_ORDERS = (("z1", "z0", "x", "c"), ("x", "z1", "z0", "c"))


def coords():
    return {a: lax.axis_index(a) for a in ("up", "lo", "fsdp")}


def bit_of(where, name):
    axis, value = BITS[name]
    return lax.rem(where[axis] // value, 2)


def across(where, *names):
    other = dict(where)
    for name in names:
        axis, value = BITS[name]
        other[axis] = other[axis] + value * (1 - 2 * bit_of(where, name))
    return other


def device(where):
    return (where["up"], where["lo"], where["fsdp"])


def place(where):
    return where["lo"] * 2 + where["fsdp"]


def greet(devices):
    barrier = pltpu.get_barrier_semaphore()
    for other in devices:
        pl.semaphore_signal(barrier, inc=1, device_id=device(other), device_id_type=MESH)
    pl.semaphore_wait(barrier, len(devices))


def remote(src, dst, send_sem, recv_sem, other):
    copy = pltpu.make_async_remote_copy(
        src_ref=src, dst_ref=dst, send_sem=send_sem, recv_sem=recv_sem, device_id=device(other), device_id_type=MESH
    )
    copy.start()
    return copy


def lane_means(values):
    total = values.shape[-1]
    group = lax.broadcasted_iota(jnp.int32, (total, total), 0) // 128 == lax.broadcasted_iota(jnp.int32, (total, total), 1) // 128
    return dot(values, jnp.where(group, 1.0 / 128, 0.0).astype(bf16))


def pair_norm(*blocks):
    x = jnp.concatenate(blocks, axis=-1)
    centered = x.astype(f32) - lane_means(x)
    variance = lane_means((centered * centered).astype(bf16))
    scale = lax.rsqrt(variance + norm_eps)
    return centered * scale, scale


def pair_fwd_kernel(rows, counts_ref, x_ref, pw_ref, gain_ref, out_ref, scr_ref):
    step = pl.program_id(0)
    steps_each = pl.num_programs(0) // 2
    limit = counts_ref[step // steps_each]
    heads, length = scr_ref.shape[0], scr_ref.shape[2]
    valid = lax.broadcasted_iota(jnp.int32, (heads, length), 1) < limit
    pw = pw_ref[...]
    gain = gain_ref[...]
    for r in range(rows):
        low = (pair_norm(x_ref[0, r])[0] * gain).astype(bf16)
        bias = dot_nt(pw, low)
        scr_ref[:, r, :] = jnp.where(valid, bias * log2e, mask_fill)
    out_ref[:, 0] = scr_ref[...].astype(bf16)


def pair_fwd(counts, pair, pw_t, gain):
    _, total, length, width = pair.shape
    rows = 8 if total % 8 == 0 else total
    steps = total // rows
    heads = pw_t.shape[0]
    return pl.pallas_call(
        functools.partial(pair_fwd_kernel, rows),
        grid_spec=pltpu.PrefetchScalarGridSpec(
            num_scalar_prefetch=1,
            grid=(2 * steps,),
            in_specs=[
                pl.BlockSpec((1, rows, length, width), lambda i, _: (i // steps, i % steps, 0, 0)),
                whole(pw_t),
                whole(gain),
            ],
            out_specs=pl.BlockSpec((heads, 1, rows, length), lambda i, _: (0, i // steps, i % steps, 0)),
            scratch_shapes=[pltpu.VMEM((heads, rows, length), f32)],
        ),
        out_shape=jax.ShapeDtypeStruct((heads, 2, total, length), bf16),
        compiler_params=params(),
        cost_estimate=pl.CostEstimate(flops=2 * pair.size * 300, bytes_accessed=pair.size * 2, transcendentals=pair.size),
        name="pair_fwd",
    )(counts, pair, pw_t, gain)


def pair_bwd_kernel(rows, x_ref, bg_ref, a_ref, out_ref, q_ref, low_buf):
    @pl.when(pl.program_id(0) == 0)
    def _():
        q_ref[...] = jnp.zeros_like(q_ref)

    width = out_ref.shape[-1]
    heads, _, _, length = bg_ref.shape
    grads = bg_ref[:, 0].astype(f32).reshape(heads * rows, length)
    turned = grads.T.astype(bf16)
    u_all = dot(jnp.concatenate([turned, turned], axis=1), a_ref[...])
    step = 2 - rows % 2
    for r in range(0, rows, step):
        x_hat, scale = pair_norm(*(x_ref[0, r + t] for t in range(step)))
        low_buf[:, r * width : (r + step) * width] = x_hat.astype(bf16)
        u = u_all[:, r * width : (r + step) * width]
        grad = (u - x_hat * lane_means((u * x_hat).astype(bf16))) * scale
        for t in range(step):
            out_ref[0, r + t] = grad[:, t * width : (t + 1) * width]
    q_ref[...] += dot(grads.astype(bf16), low_buf[...])


def pair_bwd(pair, bias_grad, high, low):
    _, total, length, width = pair.shape
    rows = 8 if total % 8 == 0 else total
    steps = total // rows
    heads = bias_grad.shape[0]
    eye = jnp.eye(rows, dtype=bf16)
    both = jnp.stack([high, low])
    weights = (both[:, :, None, None, :] * eye[None, None, :, :, None]).reshape(2 * heads * rows, rows * width)
    grad, moments = pl.pallas_call(
        functools.partial(pair_bwd_kernel, rows),
        grid=(2 * steps,),
        in_specs=[
            pl.BlockSpec((1, rows, length, width), lambda i: (i // steps, i % steps, 0, 0)),
            pl.BlockSpec((heads, 1, rows, length), lambda i: (0, i // steps, i % steps, 0)),
            whole(weights),
        ],
        out_specs=[
            pl.BlockSpec((1, rows, length, width), lambda i: (i // steps, i % steps, 0, 0)),
            pl.BlockSpec((heads * rows, rows * width), lambda i: (0, 0)),
        ],
        out_shape=[
            jax.ShapeDtypeStruct(pair.shape, f32),
            jax.ShapeDtypeStruct((heads * rows, rows * width), f32),
        ],
        scratch_shapes=[pltpu.VMEM((length, rows * width), bf16)],
        compiler_params=params(),
        cost_estimate=pl.CostEstimate(flops=2 * pair.size * 500, bytes_accessed=pair.size * 6, transcendentals=pair.size),
        name="pair_bwd",
    )(pair, bias_grad, weights)
    moments = moments.reshape(heads, rows, rows, width)
    return grad, sum(moments[:, r, r] for r in range(rows))


class Mover:
    def __init__(self, where, order, own, full, stage, send, recv, keep):
        self.where, self.order, self.own, self.full, self.send, self.recv = where, order, own, full, send, recv
        self.half = own.shape[0]
        self.piece = self.half >> len(order)
        self.mine = sum(bit_of(where, name) << j for j, name in enumerate(order))
        self.copies = []
        self.kept = [
            pltpu.make_async_copy(own, stage, keep.at[0]),
            pltpu.make_async_copy(stage, full.at[pl.ds(where["fsdp"] * self.half, self.half)], keep.at[1]),
        ]

    def stage(self, k):
        if k:
            self.kept[k - 1].wait()
        if k < 2:
            self.kept[k].start()

    def advance(self, k):
        if k:
            self.copies[k - 1].wait_recv()
        if k == 0:
            name, src_at = "y", self.mine * self.piece
            at, size = self.where["fsdp"] * self.half + src_at, self.piece
            src = self.own.at[pl.ds(src_at, size)]
        elif k <= len(self.order):
            name, size = self.order[k - 1], self.piece << (k - 1)
            at = (1 - self.where["fsdp"]) * self.half + self.mine * self.piece // size * size
            src = self.full.at[pl.ds(at, size)]
        else:
            return
        dst = self.full.at[pl.ds(at, size)]
        self.copies.append(remote(src, dst, self.send.at[k], self.recv.at[k], across(self.where, name)))

    def finish(self):
        self.stage(2)
        for copy in self.copies:
            copy.wait_send()


MOVES = (("x", "c"), ("x", "z0", "c"), ("x", "z0", "c"), ("z0", "x", "c"), ("x", "z0", "c"))


def start_kernel(n_w, counts, pw, gain, pair, *refs):
    owns, others, spread = refs[:n_w], refs[n_w : 2 * n_w], refs[2 * n_w]
    *stages, x_buf, low_buf, bias_f, bias_v, x_sems, w_send, w_recv, w_keep, b_send, b_recv, b_sem = refs[2 * n_w + 1 :]
    where = coords()
    peers = [across(where, *names) for names in PEERS]
    total = pair.shape[1]
    length, width = pair.shape[2:]
    heads = bias_f.shape[0]
    groups = 2 * total // 8

    def fetch(g, slot):
        return pltpu.make_async_copy(
            pair.at[(g * 8) // total, pl.ds(lax.rem(g * 8, total), 8)], x_buf.at[slot], x_sems.at[slot]
        )

    fetch(0, 0).start()
    greet(peers + [across(where, "z0")])
    movers = [Mover(where, MOVES[i], owns[i], others[i], stages[i], w_send.at[i], w_recv.at[i], w_keep.at[i]) for i in range(n_w)]
    for m in movers:
        m.advance(0)
    for m in movers:
        m.stage(0)

    def group(g, _):
        slot = lax.rem(g, 2)

        @pl.when(g + 1 < groups)
        def _():
            fetch(g + 1, 1 - slot).start()

        fetch(g, slot).wait()
        for r in range(0, 8, 2):
            x_hat, _ = pair_norm(x_buf[slot, r], x_buf[slot, r + 1])
            low_buf[:, r * width : (r + 2) * width] = (x_hat * gain[...]).astype(bf16)
        bias = dot(low_buf[...], pw[...]).T
        limit = counts[(g * 8) // total]
        valid = lax.broadcasted_iota(jnp.int32, bias.shape, 1) < limit
        bias = jnp.where(valid, bias * log2e, mask_fill)
        bias_f[:, pl.ds(pl.multiple_of(g * 8, 8), 8), :] = bias.reshape(heads, 8, length)
        return 0

    third = groups // 3
    for k in range(3):
        lax.fori_loop(k * third, (k + 1) * third, group, 0)
        movers[k].advance(1)
    for m in movers:
        m.stage(1)
    bias_v[...] = bias_f[...].astype(bf16).reshape(bias_v.shape)

    keep = pltpu.make_async_copy(bias_v.at[place(where)], spread.at[place(where)], b_sem)
    keep.start()
    sent = []

    def send_bias():
        for k, peer in enumerate(peers):
            sent.append(remote(bias_v.at[place(peer)], spread.at[place(where)], b_send.at[k], b_recv.at[k], peer))

    for m in movers[3:]:
        m.advance(1)
    send_bias()
    for k in range(2, 5):
        for m in movers:
            if k <= len(m.order) + 1:
                m.advance(k)
    keep.wait()
    for copy in sent:
        copy.wait()
    for m in movers:
        m.finish()


def start(counts, pair, pw_big, gain, owns):
    heads, length, width = 16, pair.shape[2], pair.shape[3]
    rows = 2 * pair.shape[1]
    n = len(owns)
    any_spec = pl.BlockSpec(memory_space=pl.ANY)
    vm = pl.BlockSpec(memory_space=pltpu.VMEM)
    return pl.pallas_call(
        functools.partial(start_kernel, n),
        in_specs=[pl.BlockSpec(memory_space=pltpu.SMEM), vm, vm, any_spec] + [any_spec] * n,
        out_specs=[any_spec] * (n + 1),
        out_shape=[jax.ShapeDtypeStruct((2 * w.shape[0], w.shape[1]), bf16) for w in owns]
        + [jax.ShapeDtypeStruct((8, heads // 8, rows, length), bf16)],
        scratch_shapes=[pltpu.VMEM(w.shape, bf16) for w in owns]
        + [
            pltpu.VMEM((2, 8, length, width), bf16),
            pltpu.VMEM((length, 8 * width), bf16),
            pltpu.VMEM((heads, rows, length), f32),
            pltpu.VMEM((8, heads // 8, rows, length), bf16),
            pltpu.SemaphoreType.DMA((2,)),
            pltpu.SemaphoreType.DMA((n, 4)),
            pltpu.SemaphoreType.DMA((n, 4)),
            pltpu.SemaphoreType.DMA((n, 2)),
            pltpu.SemaphoreType.DMA((7,)),
            pltpu.SemaphoreType.DMA((7,)),
            pltpu.SemaphoreType.DMA,
        ],
        compiler_params=pltpu.CompilerParams(vmem_limit_bytes=vmem_bytes, collective_id=2, has_side_effects=True),
        name="start",
    )(counts, pw_big, gain, pair, *owns)


def big_weights(pw):
    width, heads = pw.shape
    eye = jnp.eye(8, dtype=pw.dtype)
    return (eye[:, None, None, :] * pw[None, :, :, None]).reshape(8 * width, heads * 8)


def attend(rb, c, x_ref, y_ref, bias_ref, add):
    length, hd = x_ref.shape[-1], x_ref.shape[-2]
    bz = bias_ref.shape[2]
    k_t, v_t = x_ref[1], x_ref[2]
    v_ext = jnp.concatenate([v_t, jnp.ones((16, length), bf16)], axis=0)
    dv = dk = 0.0
    for r in range(length // rb):
        sl = slice(r * rb, (r + 1) * rb)
        q_t = x_ref[0, :, sl]
        q = q_t.T
        dm = x_ref[3, :, sl].astype(f32).T
        z0 = r * rb // bz
        bias = jnp.concatenate([bias_ref[z0 + t, c].astype(f32) for t in range(rb // bz)], axis=0)
        s = dot(q, k_t) + bias
        e = jnp.exp2(s - jnp.max(s, axis=-1, keepdims=True))
        eb = e.astype(bf16)
        mx = dot_nt(eb, v_ext)
        inv = 1.0 / mx[:, hd : hd + 1]
        mixed = mx[:, :hd] * inv
        d = jnp.sum(mixed * dm, axis=-1, keepdims=True) * inv
        dms = (dm * inv).astype(bf16)
        ds = e * (dot(dms, v_t) - d)
        dsb = ds.astype(bf16)
        add(sl, ds)
        dq = dot_nt(dsb, k_t)
        dv = dv + dot(dms.T, eb)
        dk = dk + dot(q_t, dsb)
        y_ref[0, :, sl] = mixed.T.astype(bf16)
        y_ref[1, :, sl] = (dq * hd**-0.5).T.astype(bf16)
    y_ref[2] = (dk * ln2).astype(bf16)
    y_ref[3] = dv.astype(bf16)


def attn_kernel(rb, owner_ref, x_ref, bias_ref, y_ref, bg_ref, acc_ref):
    n = pl.program_id(0)
    c = owner_ref[n]
    up, bz = bias_ref.shape[0], bias_ref.shape[2]

    @pl.when(n == 0)
    def _():
        acc_ref[...] = jnp.zeros_like(acc_ref)

    def add(sl, ds):
        acc_ref[c, sl, :] += ds

    attend(rb, c, x_ref.at[0], y_ref.at[0], bias_ref, add)

    @pl.when(n == pl.num_programs(0) - 1)
    def _():
        for z in range(up):
            for cc in range(2):
                bg_ref[z, cc] = acc_ref[cc, z * bz : (z + 1) * bz, :].astype(bf16)


def sending_attn_kernel(
    rb, slot, owner_ref, x_ref, bias_ref, y_ref, bg_ref, both, second, x_buf, y_buf, x_sems, y_send, y_recv, y_keep
):
    step = pl.program_id(0)
    steps = pl.num_programs(0)
    where = coords()
    up, bz = bias_ref.shape[0], bias_ref.shape[2]

    def partner(k):
        other = dict(where)
        for name in ("c", "x", "y"):
            axis, value = BITS[name]
            flip = sum(jnp.where(k == i, 1, 0) for i, names in enumerate(SAMPLE_ORDER) if name in names)
            other[axis] = other[axis] + flip * value * (1 - 2 * bit_of(where, name))
        return other

    def fetch(k):
        return pltpu.make_async_copy(
            x_ref.at[place(partner(k)), pl.ds(slot * 4, 4)], x_buf.at[lax.rem(k, 2)], x_sems.at[lax.rem(k, 2)]
        )

    def sent(k, to):
        return pltpu.make_async_remote_copy(
            src_ref=y_buf.at[k],
            dst_ref=y_ref.at[place(to)],
            send_sem=y_send.at[k],
            recv_sem=y_recv.at[k],
            device_id=device(partner(k)),
            device_id_type=MESH,
        )

    keep = pltpu.make_async_copy(y_buf.at[len(PEERS)], y_ref.at[place(where)], y_keep)

    @pl.when(step == 0)
    def _():
        fetch(0).start()
        both[...] = jnp.zeros_like(both)
        second[...] = jnp.zeros_like(second)
        greet([across(where, *names) for names in PEERS])

    @pl.when(step + 1 < steps)
    def _():
        fetch(step + 1).start()

    fetch(step).wait()
    c = owner_ref[place(partner(step))]
    weight = c.astype(f32)

    def add(sl, ds):
        both[sl, :] += ds
        second[sl, :] += ds * weight

    attend(rb, c, x_buf.at[lax.rem(step, 2)], y_buf.at[step], bias_ref, add)

    @pl.when(step < steps - 1)
    def _():
        sent(step, where).start()

    @pl.when(step == steps - 1)
    def _():
        keep.start()
        for z in range(up):
            sl = slice(z * bz, (z + 1) * bz)
            bg_ref[z, 0] = (both[sl, :] - second[sl, :]).astype(bf16)
            bg_ref[z, 1] = second[sl, :].astype(bf16)
        keep.wait()
        for k in range(len(PEERS)):
            sent(k, partner(k)).wait_recv()
            sent(k, where).wait_send()


def sending_attention(owner, x, bias, slot):
    n, _, hd, length = x.shape
    any_spec = pl.BlockSpec(memory_space=pl.ANY)
    vm = pl.BlockSpec(memory_space=pltpu.VMEM)
    return pl.pallas_call(
        functools.partial(sending_attn_kernel, length // 2, slot),
        grid=(n,),
        in_specs=[pl.BlockSpec(memory_space=pltpu.SMEM), any_spec, vm],
        out_specs=[any_spec, vm],
        out_shape=[jax.ShapeDtypeStruct((n, 4, hd, length), bf16), jax.ShapeDtypeStruct(bias.shape, bf16)],
        scratch_shapes=[
            pltpu.VMEM((length, length), f32),
            pltpu.VMEM((length, length), f32),
            pltpu.VMEM((2, 4, hd, length), bf16),
            pltpu.VMEM((n, 4, hd, length), bf16),
            pltpu.SemaphoreType.DMA((2,)),
            pltpu.SemaphoreType.DMA((n,)),
            pltpu.SemaphoreType.DMA((n,)),
            pltpu.SemaphoreType.DMA,
        ],
        compiler_params=params(collective_id=3 + slot, has_side_effects=True),
        cost_estimate=pl.CostEstimate(
            flops=12 * n * length * length * 256, bytes_accessed=x.size * 2 + bias.size * 4, transcendentals=n * length * length
        ),
        name="attention_and_send",
    )(owner, x, bias)


def attention(owner, x, bias, slot):
    n, _, hd, length = x.shape
    four = 4
    return pl.pallas_call(
        functools.partial(attn_kernel, length // 2),
        grid_spec=pltpu.PrefetchScalarGridSpec(
            num_scalar_prefetch=1,
            grid=(n,),
            in_specs=[
                pl.BlockSpec((1, four, hd, length), lambda i, _: (i, slot, 0, 0)),
                pl.BlockSpec(bias.shape, lambda i, _: (0, 0, 0, 0)),
            ],
            out_specs=[
                pl.BlockSpec((1, four, hd, length), lambda i, _: (i, 0, 0, 0)),
                pl.BlockSpec(bias.shape, lambda i, _: (0, 0, 0, 0)),
            ],
            scratch_shapes=[pltpu.VMEM((2, length, length), f32)],
        ),
        out_shape=[jax.ShapeDtypeStruct((n, four, hd, length), bf16), jax.ShapeDtypeStruct(bias.shape, bf16)],
        compiler_params=params(),
        cost_estimate=pl.CostEstimate(
            flops=12 * n * length * length * 256, bytes_accessed=x.size * 2 + bias.size * 4, transcendentals=n * length * length
        ),
        name="attention",
    )(owner, x, bias)


def front_kernel(
    tok, cond, og, cgain, wc, cb, wq, qb, wo,
    *outs,
):
    x_o, sg_o, gg_o, s1_o, g1_o, first_o = outs
    width = tok.shape[-1]
    hd = width // head_count
    peers = x_o.shape[0]
    slots = head_count // peers
    cond_low = (norm_parts(cond[...].astype(f32))[0] * cgain[...]).astype(bf16)
    modul = dot(cond_low, wc[...]) + cb[...]
    s1 = jax.nn.sigmoid(modul[:, :width])
    g1 = jax.nn.sigmoid(modul[:, 2 * width :])
    tn, _ = norm_parts(tok[...].astype(f32))
    first = (s1 * tn + modul[:, width : 2 * width]).astype(bf16)
    proj = dot(first, wq[...])
    q = (proj[:, :width] + qb[...]) * (hd**-0.5 * log2e)
    sg = jax.nn.sigmoid(proj[:, 3 * width :])
    ga = (og[...].astype(f32) * g1).astype(bf16)
    gg = dot_nt(ga, wo[...])
    dm = sg * gg
    sg_o[...] = sg.astype(bf16)
    gg_o[...] = gg.astype(bf16)
    s1_o[...] = s1.astype(bf16)
    g1_o[...] = g1.astype(bf16)
    first_o[...] = first
    for i, part in enumerate((q, proj[:, width : 2 * width], proj[:, 2 * width : 3 * width], dm)):
        turned = part.T.astype(bf16).reshape(peers, slots, hd, part.shape[0])
        for t in range(slots):
            x_o[:, t * 4 + i] = turned[:, t]


def half_spec(a, h):
    return pl.BlockSpec((a.shape[0], a.shape[1] // 2), lambda *_: (0, h))


def row_spec(a, rb):
    return pl.BlockSpec((rb, a.shape[1]), lambda i, *_: (i, 0))


def front(tok, cond, og, cgain, wc, cb, wq, qb, wo, slots):
    length, width = tok.shape
    rb = 256
    peers, hd = head_count // slots, width // head_count
    small = jax.ShapeDtypeStruct((length, width), bf16)
    payload = jax.ShapeDtypeStruct((peers, 4 * slots, hd, length), bf16)
    return pl.pallas_call(
        front_kernel,
        grid_spec=pl.GridSpec(
            grid=(length // rb,),
            in_specs=[row_spec(tok, rb), row_spec(cond, rb), row_spec(og, rb)]
            + [whole(cgain)]
            + [half_spec(wc, 0)]
            + [whole(a) for a in (cb, wq, qb, wo)],
            out_specs=[pl.BlockSpec((peers, 4 * slots, hd, rb), lambda i: (0, 0, 0, i))] + [row_spec(tok, rb)] * 5,
        ),
        out_shape=[payload] + [small] * 5,
        compiler_params=params(),
        cost_estimate=pl.CostEstimate(flops=2 * length * width * width * 7, bytes_accessed=20 << 20, transcendentals=length * width * 4),
        name="front",
    )(tok, cond, og, cgain, wc, cb, wq, qb, wo)


def trans_kernel(
    tok, cond, og, cgain, wc, cb, wu, wd,
    part_o, u2_o, dcond_o, ml_o, cn_o, second_o, hid_o, act_o, gt_o, cbg_o,
):
    width = tok.shape[-1]
    cond_low = (norm_parts(cond[...].astype(f32))[0] * cgain[...]).astype(bf16)
    cn_o[...] = cond_low
    modul = dot(cond_low, wc[...]) + cb[...]
    s2 = jax.nn.sigmoid(modul[:, :width])
    g2 = jax.nn.sigmoid(modul[:, 2 * width :])
    tokens = tok[...].astype(f32)
    tn, _ = norm_parts(tokens)
    second = (s2 * tn + modul[:, width : 2 * width]).astype(bf16)
    second_o[...] = second
    hidden = dot(second, wu[...])
    ff = hidden.shape[1] // 2
    h_gate, h_up = hidden[:, :ff], hidden[:, ff:]
    sig = jax.nn.sigmoid(h_gate)
    silu = h_gate * sig
    act = (silu * h_up).astype(bf16)
    act_o[...] = act
    trans_out = dot(act, wd[...])
    part_o[...] = tokens + g2 * trans_out
    g = og[...].astype(f32)
    gt = (g * g2).astype(bf16)
    gt_o[...] = gt
    grad_act = dot_nt(gt, wd[...])
    hid = jnp.concatenate(
        [(grad_act * h_up * (sig * (1.0 + h_gate * (1.0 - sig)))).astype(bf16), (grad_act * silu).astype(bf16)], axis=-1
    )
    hid_o[...] = hid
    grad_second = dot_nt(hid, wu[...])
    u2_o[...] = (grad_second * s2).astype(bf16)
    grads = jnp.concatenate(
        [grad_second * tn * (s2 * (1.0 - s2)), grad_second, g * trans_out * (g2 * (1.0 - g2))], axis=-1
    )
    low = grads.astype(bf16)
    ml_o[...] = low

    @pl.when(pl.program_id(0) == 0)
    def _():
        cbg_o[...] = jnp.zeros_like(cbg_o)

    cbg_o[...] += jnp.sum(grads, axis=0, keepdims=True)
    dcond_o[...] = dot_nt(low, wc[...])


def transition(tok, cond, og, cgain, wc, cb, wu, wd):
    length, width = tok.shape
    rb = 256
    cs, mw = cond.shape[1], cb.shape[1]
    ff2 = wu.shape[1]

    def out(w, dtype):
        return jax.ShapeDtypeStruct((length, w), dtype)

    shapes = [
        out(width, f32), out(width, bf16), out(cs, f32), out(mw, bf16), out(cs, bf16), out(width, bf16),
        out(ff2, bf16), out(ff2 // 2, bf16), out(width, bf16),
    ]
    return pl.pallas_call(
        trans_kernel,
        grid_spec=pl.GridSpec(
            grid=(length // rb,),
            in_specs=[row_spec(tok, rb), row_spec(cond, rb), row_spec(og, rb)]
            + [whole(cgain)]
            + [half_spec(wc, 1)]
            + [whole(a) for a in (cb, wu, wd)],
            out_specs=[row_spec(s, rb) for s in shapes] + [pl.BlockSpec((1, mw), lambda i: (0, 0))],
        ),
        out_shape=shapes + [jax.ShapeDtypeStruct((1, mw), f32)],
        compiler_params=params(),
        cost_estimate=pl.CostEstimate(flops=2 * length * width * width * 15, bytes_accessed=40 << 20, transcendentals=length * width * 6),
        name="transition",
    )(tok, cond, og, cgain, wc, cb, wu, wd)


def back_kernel(slots, *refs):
    ys = refs[:slots]
    (
        sg, gg, s1, g1, part, u2, dcond2, tok, cond, og, cgain, wc, wq, wo,
        out_o, tg_o, cg_o, gated_o, ga_o, gp_o, ml_o, qbg_o, cbg_o, cgg_o,
    ) = refs[slots:]
    rb, width = tok.shape
    hd = width // head_count
    peers = head_count // slots

    def heads(i):
        stacked = jnp.stack([y[:, i] for y in ys], axis=1)
        return stacked.reshape(width, rb).astype(f32).T

    mixed = heads(0)
    sgv = sg[...].astype(f32)
    g1v = g1[...].astype(f32)
    gated = (sgv * mixed).astype(bf16)
    gated_o[...] = gated
    attn_out = dot(gated, wo[...])
    out_o[...] = part[...] + g1v * attn_out
    g = og[...].astype(f32)
    ga_o[...] = (g * g1v).astype(bf16)
    dg = gg[...].astype(f32) * mixed * (sgv * (1.0 - sgv))
    dq = heads(1)
    grad_proj = jnp.concatenate([dq.astype(bf16), heads(2).astype(bf16), heads(3).astype(bf16), dg.astype(bf16)], axis=-1)
    gp_o[...] = grad_proj
    grad_first = dot_nt(grad_proj, wq[...])
    s1v = s1[...].astype(f32)
    tn, tscale = norm_parts(tok[...].astype(f32))
    grads = jnp.concatenate(
        [grad_first * tn * (s1v * (1.0 - s1v)), grad_first, g * attn_out * (g1v * (1.0 - g1v))], axis=-1
    )
    low = grads.astype(bf16)
    ml_o[...] = low
    tg_o[...] = g + norm_back(tn, grad_first * s1v + u2[...].astype(f32), tscale)
    dcond = dot_nt(low, wc[...]) + dcond2[...]
    cx, cscale = norm_parts(cond[...].astype(f32))
    cg_o[...] = norm_back(cx, dcond * cgain[...], cscale)

    @pl.when(pl.program_id(0) == 0)
    def _():
        qbg_o[...] = jnp.zeros_like(qbg_o)
        cbg_o[...] = jnp.zeros_like(cbg_o)
        cgg_o[...] = jnp.zeros_like(cgg_o)

    qbg_o[...] += jnp.sum(dq, axis=0, keepdims=True)
    cbg_o[...] += jnp.sum(grads, axis=0, keepdims=True)
    cgg_o[...] += jnp.sum(dcond * cx, axis=0, keepdims=True)


def back(ys, sg, gg, s1, g1, part, u2, dcond2, tok, cond, og, cgain, wc, wq, wo):
    length, width = tok.shape
    rb = 256
    cs, mw = cond.shape[1], wc.shape[1] // 2
    rows = (sg, gg, s1, g1, part, u2, dcond2, tok, cond, og)
    consts = (wq, wo)

    def out(w, dtype):
        return jax.ShapeDtypeStruct((length, w), dtype)

    shapes = [
        out(width, f32), out(width, f32), out(cs, f32), out(width, bf16), out(width, bf16), out(wq.shape[1], bf16), out(mw, bf16),
    ]
    small = [jax.ShapeDtypeStruct((1, w), f32) for w in (width, mw, cs)]
    return pl.pallas_call(
        functools.partial(back_kernel, len(ys)),
        grid_spec=pl.GridSpec(
            grid=(length // rb,),
            in_specs=[pl.BlockSpec(y.shape[:3] + (rb,), lambda i: (0, 0, 0, i)) for y in ys]
            + [row_spec(a, rb) for a in rows]
            + [whole(cgain)]
            + [half_spec(wc, 0)]
            + [whole(a) for a in consts],
            out_specs=[row_spec(s, rb) for s in shapes] + [pl.BlockSpec(s.shape, lambda i: (0, 0)) for s in small],
        ),
        out_shape=shapes + small,
        compiler_params=params(),
        cost_estimate=pl.CostEstimate(flops=2 * length * width * width * 7, bytes_accessed=40 << 20, transcendentals=length * width),
        name="back",
    )(*ys, *rows, cgain, wc, *consts)


def wgrad_kernel(steps, lhs, *refs):
    *rhs, out_ref, turned = refs
    step = pl.program_id(0)

    @pl.when(step == 0)
    def _():
        turned[...] = lhs[...].T

    for k, r in enumerate(rhs):

        @pl.when(step // steps == k)
        def _():
            out_ref[...] = dot(turned[...], r[...]).astype(bf16).reshape(out_ref.shape)


def wgrad(lhs, *rhs):
    length, k = lhs.shape
    n = sum(r.shape[1] for r in rhs)
    row_groups = k // 96
    col_groups = 16 // row_groups
    piece = n // col_groups
    cols = piece if piece <= 1536 else piece // 2
    steps = n // cols
    each = steps // len(rhs)
    per = piece // cols

    def rhs_spec(t):
        return pl.BlockSpec((length, cols), lambda i: (0, jnp.clip(i - t * each, 0, each - 1)))

    return pl.pallas_call(
        functools.partial(wgrad_kernel, each),
        grid=(steps,),
        in_specs=[whole(lhs)] + [rhs_spec(t) for t in range(len(rhs))],
        out_specs=pl.BlockSpec((2, row_groups, 48, cols), lambda i: (0, i // per, 0, i % per)),
        out_shape=jax.ShapeDtypeStruct((2, 16, 48, piece), bf16),
        scratch_shapes=[pltpu.VMEM((k, length), bf16)],
        compiler_params=params(),
        cost_estimate=pl.CostEstimate(flops=2 * length * k * n, bytes_accessed=2 * (length * (k + n) + k * n), transcendentals=0),
        name="wgrad",
    )(lhs, *rhs)


def laid_out(pieces, rows):
    cols = pieces.shape[-1]
    row_groups = rows // 48
    blocks = pieces.reshape(16 // row_groups, rows, cols).astype(f32)
    return jnp.concatenate([blocks[t] for t in range(blocks.shape[0])], axis=1)


class Reducer:
    stages = 10

    def __init__(self, where, plan, ins, outs, xs, rs, load_sems, send_sems, recv_sems, keep_sems):
        self.where, self.plan, self.ins, self.outs, self.xs, self.rs = where, plan, ins, outs, xs, rs
        self.load_sems, self.send_sems, self.recv_sems, self.keep_sems = load_sems, send_sems, recv_sems, keep_sems
        n = len(plan)
        self.base, self.size, self.off, self.pending = [0] * n, [32] * n, [0] * n, [None] * n
        self.sends = []
        self.loads = [self.load(i) if ins else [] for i in range(n)]

    @staticmethod
    def scratch(plan):
        n = len(plan)
        return (
            [pltpu.VMEM((32, 48, w), bf16) for _, _, w, _, _ in plan]
            + [pltpu.VMEM((31, 48, w), bf16) for _, _, w, _, _ in plan]
            + [pltpu.SemaphoreType.DMA((n, 16))]
            + [pltpu.SemaphoreType.DMA((n, 9))] * 2
            + [pltpu.SemaphoreType.DMA((n,))]
        )

    def load(self, i):
        a, c0, w, order, _ = self.plan[i]
        at = SUM_ORDERS[order].index("y")
        run = 32 >> (at + 1)
        copies = []
        for b in range(1 << at):
            for f in range(2):
                copy = pltpu.make_async_copy(
                    self.ins[a].at[f, pl.ds(b * run, run), :, pl.ds(c0, w)],
                    self.xs[i].at[pl.ds((b * 2 + f) * run, run)],
                    self.load_sems.at[i, b * 2 + f],
                )
                copy.start()
                copies.append(copy)
        return copies

    def store(self, i, first_piece, rows):
        order = self.plan[i][3]
        low = 4 - SUM_ORDERS[order].index("y")
        row_groups = rows.shape[0] // 96
        for f in range(2):
            for g in range(row_groups):
                p = first_piece + g
                at = ((p >> low) * 2 + f) << low | p & ((1 << low) - 1)
                r0 = (f * row_groups + g) * 48
                self.xs[i][at] = rows[r0 : r0 + 48, :]

    def send(self, i, k, src, dst, name):
        copy = remote(src, dst, self.send_sems.at[i, k], self.recv_sems.at[i, k], across(self.where, name))
        self.sends.append(copy)
        self.pending[i] = copy

    def sum_start(self, i, k):
        name = SUM_ORDERS[self.plan[i][3]][k]
        half = self.size[i] // 2
        b = bit_of(self.where, name)
        src = self.xs[i].at[pl.ds(self.base[i] + (1 - b) * half, half)]
        self.send(i, k, src, self.rs[i].at[pl.ds(self.off[i], half)], name)
        self.base[i] = self.base[i] + b * half
        self.size[i] = half

    def sum_finish(self, i):
        self.pending[i].wait_recv()
        half, b0, r0 = self.size[i], self.base[i], self.off[i]
        x, r = self.xs[i], self.rs[i]

        def body(j, _):
            x[b0 + j] = (x[b0 + j].astype(f32) + r[r0 + j].astype(f32)).astype(bf16)
            return 0

        lax.fori_loop(0, half, body, 0)
        self.off[i] = r0 + half

    def block(self, i, done):
        a, c0, w, order, _ = self.plan[i]
        at = [
            slice(None) if name in done else bit_of(self.where, name) for name in SUM_ORDERS[order] if name != "y"
        ]
        return self.outs[a].at[(*at, slice(None), pl.ds(c0, w))]

    def copy_start(self, i, j):
        names = COPY_ORDERS[self.plan[i][4]]
        ref = self.block(i, names[:j])
        self.send(i, 5 + j, ref, ref, names[j])

    def advance(self, i, k):
        if k == 0:
            for copy in self.loads[i]:
                copy.wait()
            self.sum_start(i, 0)
        elif k < 5:
            self.sum_finish(i)
            self.sum_start(i, k)
        elif k == 5:
            self.sum_finish(i)
            keep = pltpu.make_async_copy(self.xs[i].at[self.base[i]], self.block(i, ()), self.keep_sems.at[i])
            keep.start()
            keep.wait()
            self.copy_start(i, 0)
        else:
            self.pending[i].wait_recv()
            if k < 9:
                self.copy_start(i, k - 5)

    def finish(self):
        for copy in self.sends:
            copy.wait_send()


class SmallSum:
    def __init__(self, where, buf, send_sems, recv_sems):
        self.where, self.buf, self.send_sems, self.recv_sems = where, buf, send_sems, recv_sems
        self.copies = []

    def advance(self, k):
        if k > 0:
            self.copies[k - 1].wait_recv()
            self.buf[2 * k] = self.buf[2 * k - 2] + self.buf[2 * k - 1]
        if k < 5:
            src, dst = self.buf.at[2 * k], self.buf.at[2 * k + 1]
            self.copies.append(
                remote(src, dst, self.send_sems.at[k], self.recv_sems.at[k], across(self.where, list(BITS)[k]))
            )


def reduce_kernel(n_left, *refs):
    refs = list(refs)

    def take(n):
        out, refs[:] = refs[:n], refs[n:]
        return out

    early_in, acts, (small, small_o) = take(2), take(7), take(2)
    late_out, early_out = take(3), take(2)
    n_late, n_early = len(late_plan), len(early_plan)
    late_scratch, early_scratch = take(2 * n_late + 4), take(2 * n_early + 4)
    bufs, (sbuf, s_send, s_recv, a_sems) = take(7), take(4)
    where = coords()
    loads = [pltpu.make_async_copy(src, dst, a_sems.at[i]) for i, (src, dst) in enumerate(zip(acts, bufs))]

    def reducer(plan, ins, outs, scratch):
        n = len(plan)
        return Reducer(where, plan, ins, outs, scratch[:n], scratch[n : 2 * n], *scratch[2 * n :])

    early = reducer(early_plan, early_in, early_out, early_scratch)
    for copy in loads:
        copy.start()
    late = reducer(late_plan, None, late_out, late_scratch)
    sbuf[0] = small[...]
    greet([across(where, name) for name in BITS])
    small_sum = SmallSum(where, sbuf, s_send, s_recv)
    small_sum.advance(0)
    for i in range(n_early):
        early.advance(i, 0)

    first, gp, cn, ml1, ml2, gated, ga = bufs
    sides = ((first, (gp,)), (cn, (ml1, ml2)), (gated, (ga,)))
    turned = {}
    waited = set()

    def ready(k):
        if k not in waited:
            loads[k].wait()
            waited.add(k)

    for i, (a, c0, w, _, _) in enumerate(late_plan):
        lhs, rhs = sides[a]
        k0 = (0, 2, 5)[a]
        for k in range(k0, k0 + 1 + len(rhs)):
            ready(k)
        if a not in turned:
            turned[a] = lhs[...].T
        row_groups = turned[a].shape[0] // 96
        total = sum(r.shape[1] for r in rhs)
        piece = total * row_groups // 16
        for g in range(16 // row_groups):
            c = g * piece
            r = rhs[c // rhs[0].shape[1]]
            c = c % rhs[0].shape[1] + c0
            late.store(i, g * row_groups, dot(turned[a], r[:, c : c + w]).astype(bf16))
        late.advance(i, 0)
        if i in (1, 4):
            for e in range(n_early):
                early.advance(e, 1 + i // 4)
    for k in range(1, Reducer.stages):
        for i in range(n_late):
            late.advance(i, k)
        if k + 2 < Reducer.stages:
            for i in range(n_early):
                early.advance(i, k + 2)
        if k < 6:
            small_sum.advance(k)
    small_o[...] = sbuf[10]
    for copy in late.sends + early.sends + small_sum.copies:
        copy.wait_send()


def reduce_all(early, acts, small):
    widths = (1536, 1152, 384, 1536, 768)
    shapes = [jax.ShapeDtypeStruct((2, 2, 2, 2, 48, w), bf16) for w in widths]
    any_spec = pl.BlockSpec(memory_space=pl.ANY)
    vm = pl.BlockSpec(memory_space=pltpu.VMEM)
    return pl.pallas_call(
        functools.partial(reduce_kernel, None),
        out_shape=[jax.ShapeDtypeStruct(small.shape, f32)] + shapes,
        in_specs=[any_spec] * (len(early) + len(acts)) + [vm],
        out_specs=[vm] + [any_spec] * len(shapes),
        scratch_shapes=Reducer.scratch(late_plan)
        + Reducer.scratch(early_plan)
        + [pltpu.VMEM(a.shape, bf16) for a in acts]
        + [
            pltpu.VMEM((11,) + small.shape, f32),
            pltpu.SemaphoreType.DMA((5,)),
            pltpu.SemaphoreType.DMA((5,)),
            pltpu.SemaphoreType.DMA((len(acts),)),
        ],
        compiler_params=params(collective_id=1, has_side_effects=True),
        name="reduce_grads",
    )(*early, *acts, small)


def small_kernel(x, out, buf, send_sems, recv_sems):
    where = coords()
    buf[0] = x[...]
    greet([across(where, name) for name in BITS])
    total = SmallSum(where, buf, send_sems, recv_sems)
    for k in range(6):
        total.advance(k)
    out[...] = buf[10]
    for copy in total.copies:
        copy.wait_send()


def small_sum(x):
    return pl.pallas_call(
        small_kernel,
        out_shape=jax.ShapeDtypeStruct(x.shape, f32),
        in_specs=[pl.BlockSpec(memory_space=pltpu.VMEM)],
        out_specs=pl.BlockSpec(memory_space=pltpu.VMEM),
        scratch_shapes=[
            pltpu.VMEM((11,) + x.shape, f32),
            pltpu.SemaphoreType.DMA((5,)),
            pltpu.SemaphoreType.DMA((5,)),
        ],
        compiler_params=params(collective_id=5, has_side_effects=True),
        name="small_sum",
    )(x)


late_plan = (
    (0, 0, 1024, 0, 0),
    (0, 1024, 512, 1, 1),
    (1, 0, 512, 1, 1),
    (1, 512, 640, 2, 0),
    (2, 0, 384, 2, 1),
)
early_plan = ((0, 0, 768, 0, 0), (0, 768, 768, 1, 1), (1, 0, 768, 2, 0))


def on_device(
    tokens, cond, pair, counts, owner, out_grad, cond_gain, cond_weight, cond_bias, qkvg_weight, query_bias,
    out_weight, pair_gain, pair_weight, up_weight, down_weight,
):
    ups, los, ffs = lax.axis_size("up"), lax.axis_size("lo"), lax.axis_size("fsdp")
    plane = ("lo", "fsdp")
    members = los * ffs
    slots = head_count // members
    length, width = tokens.shape[1:]
    rows = pair.shape[1]
    direct = ffs == 2 and los == 4 and ups == 4

    wide = 3 * width

    def spread(got):
        mine = got.reshape(members, 2, rows, length).transpose(1, 0, 2, 3).reshape(2, members * rows, length)
        return lax.all_gather(mine, "up", axis=0, tiled=False)

    matrices = (cond_weight, qkvg_weight, out_weight, up_weight, down_weight)
    if direct:
        wc, wq, wo, wu, wd, spreads = start(
            counts, pair, big_weights(pair_weight), jnp.tile(pair_gain, 2)[None], matrices
        )
    else:
        bias = pair_fwd(counts, pair, pair_weight.T, pair_gain[None])
        bias = bias.reshape(members, slots, 2 * rows, length)
        spreads = lax.all_to_all(bias, plane, 0, 0, tiled=True)
        wc, wq, wo, wu, wd = [lax.all_gather(w, "fsdp", axis=0, tiled=True) for w in matrices]
    biases = [spread(spreads[:, t]) for t in range(slots)]

    tok, cnd, og = tokens[0], cond[0], out_grad[0]
    cgain = cond_gain[None]
    x, sg, gg, s1, g1, first = front(
        tok, cnd, og, cgain, wc, cond_bias[None, :wide], wq, query_bias[None], wo, slots
    )
    x = lax.all_to_all(x, plane, 0, 0, tiled=True)
    part, u2, dcond2, ml2, cn, second, hid, act, gt, cbg2 = transition(
        tok, cnd, og, cgain, wc, cond_bias[None, wide:], wu, wd
    )
    def fold(g):
        k, n = g.shape
        if k == width:
            return g
        if k > width:
            times = k // width
            parts = g.reshape(ffs, times, width // ffs, n)
            return jnp.concatenate([parts[:, t] for t in range(times)], axis=-1).reshape(width, n * times)
        times = width // k
        parts = g.reshape(ffs, k // ffs, times, n // times)
        return jnp.concatenate([parts[:, :, t] for t in range(times)], axis=1).reshape(width, n // times)

    def unfold(h, k, n):
        rows_each = width // ffs
        if k == width:
            return h
        if k > width:
            times = k // width
            return jnp.concatenate([h[:, t * n : (t + 1) * n] for t in range(times)], axis=0)
        times = width // k
        step = rows_each // times
        return jnp.concatenate([h[t * step : (t + 1) * step] for t in range(times)], axis=1)

    def reduced(grads):
        folded = [fold(g) for g in grads]
        mine = lax.psum_scatter(
            jnp.concatenate(folded, axis=1), ("fsdp", "up", "lo"), scatter_dimension=0, tiled=True
        )
        full = lax.all_gather(mine, ("up", "lo"), axis=0, tiled=True)
        outs, at = [], 0
        for g, h in zip(grads, folded):
            outs.append(unfold(full[:, at : at + h.shape[1]], *g.shape).astype(f32))
            at += h.shape[1]
        return outs

    if direct:
        early = [wgrad(second, hid), wgrad(act, gt)]
        x, *early = lax.optimization_barrier((x, *early))
    else:
        up_total, down_total = reduced([dot_tn(second, hid).astype(bf16), dot_tn(act, gt).astype(bf16)])

    owners = lax.dynamic_slice_in_dim(owner, lax.axis_index("up") * members, members)
    ys, bias_grads = [], []
    for t in range(slots):
        if direct:
            y, bg = sending_attention(owners, x, biases[t], t)
        else:
            y, bg = attention(owners, x, biases[t], t)
            y = lax.all_to_all(y, plane, 0, 0, tiled=True)
        ys.append(y)
        mine = lax.psum_scatter(bg, "up", scatter_dimension=0, tiled=True)
        bias_grads.append(mine.reshape(2, members, rows, length).transpose(1, 0, 2, 3))

    block_out, tokens_grad, cond_grad, gated, ga, gp, ml1, qbg, cbg1, cgg = back(
        ys, sg, gg, s1, g1, part, u2, dcond2, tok, cnd, og, cgain, wc, wq, wo
    )
    if not direct:
        ml = jnp.concatenate([ml1, ml2], axis=1)
        qkvg_total, out_total, cond_total = reduced(
            [dot_tn(first, gp).astype(bf16), dot_tn(gated, ga).astype(bf16), dot_tn(cn, ml).astype(bf16)]
        )

    pieces = [cgg, cbg1, cbg2, qbg]
    stacked = jnp.concatenate([p.reshape(-1, 128) for p in pieces], axis=0)
    if direct:
        height = -(-stacked.shape[0] // 8) * 8
        stacked = jnp.pad(stacked, ((0, height - stacked.shape[0]), (0, 0)))
        stacked, *totals = reduce_all(early, (first, gp, cn, ml1, ml2, gated, ga), stacked)
        *bias_grads, stacked = lax.optimization_barrier((*bias_grads, stacked))
        qkvg_total, cond_total, out_total, up_total, down_total = [
            laid_out(p, w.shape[0]) for p, w in zip(totals, (qkvg_weight, cond_weight, out_weight, up_weight, down_weight))
        ]
    else:
        stacked = lax.psum(stacked, ("up", "lo", "fsdp"))
    bias_grad = lax.all_to_all(jnp.stack(bias_grads, axis=1), plane, 0, 0, tiled=True)
    bias_grad = bias_grad.reshape(head_count, 2, rows, length)
    pw = pair_weight.astype(f32).T
    scaled = pw * pair_gain
    centered = scaled - jnp.mean(scaled, axis=-1, keepdims=True)
    high = centered.astype(bf16)
    low = (centered - high.astype(f32)).astype(bf16)
    pair_grad, moments = pair_bwd(pair, bias_grad, high, low)
    moments = small_sum(moments) if direct else lax.psum(moments, ("up", "lo", "fsdp"))
    small = stacked.reshape(-1)
    ends = [0]
    for p in pieces:
        ends.append(ends[-1] + p.size)
    small = [small[a:b] for a, b in zip(ends[:-1], ends[1:])]
    return (
        block_out[None],
        tokens_grad[None],
        cond_grad[None],
        pair_grad,
        small[0],
        cond_total,
        jnp.concatenate([small[1], small[2]]),
        qkvg_total,
        small[3],
        out_total,
        jnp.sum(pw * moments, axis=0),
        (moments * pair_gain).T,
        up_total,
        down_total,
    )


def solution(mesh):
    dp, fsdp = mesh.shape["dp"], mesh.shape["fsdp"]
    lo = max(1, group_size // fsdp)
    fine = Mesh(mesh.devices.reshape(dp // lo, lo, fsdp), ("up", "lo", "fsdp"))
    every = ("up", "lo", "fsdp")
    in_specs = (
        P(every, None, None),
        P(every, None, None),
        P(None, every, None, None),
        P(),
        P(),
        P(every, None, None),
        P(),
        P("fsdp", None),
        P(),
        P("fsdp", None),
        P(),
        P("fsdp", None),
        P(),
        P(),
        P("fsdp", None),
        P("fsdp", None),
    )
    out_specs = (
        P(every, None, None),
        P(every, None, None),
        P(every, None, None),
        P(None, every, None, None),
        P(),
        P("fsdp", None),
        P(),
        P("fsdp", None),
        P(),
        P("fsdp", None),
        P(),
        P(),
        P("fsdp", None),
        P("fsdp", None),
    )
    return jax.shard_map(on_device, mesh=fine, in_specs=in_specs, out_specs=out_specs, check_vma=False)
```

time: 571 us -> 498 us (0.87)
  blocking collectives: 32.6 us -> 0 us
  Pallas kernels: 417 us -> 405 us
  starting transfers between devices: 20.1 us -> 8.52 us
  local copies, waits for them, and re-layouts: 24.5 us -> 17.6 us
    all_to_all x1 -> x0, blocking collectives: 32.6 us -> none  [on_device(): xs = [xs[0]] + [lax.all_to_all(x, plane, 0, 0, tiled=True) for x in xs[1:]]]
    pallas_call x1, Pallas kernels: 81.5 us -> 67.5 us  [start(): pl.pallas_call(functools.partial(start_kernel, n), in_specs=[pl.BlockSpec...]
    all_to_all x5 -> x2, starting transfers between devices: 19.7 us -> 8.19 us  [the longest x1 4.62 us: on_device(): x = lax.all_to_all(x, plane, 0, 0, tiled=True)]
    all_to_all x5 -> x2, waiting for transfers between devices: 29.6 us -> 24.1 us  [the longest x1 12.4 us: on_device(): lax.all_to_all(jnp.stack(bias_grads, axis=1), plane, 0, 0, tiled=True)]
    pallas_call x11 -> x9, Pallas kernels: 318 us -> 320 us  [the longest x1 156 us: reduce_all(): pl.pallas_call(functools.partial(reduce_kernel, None), out_shape=[jax.Sha...]
  transfers between devices with their start and end apart: 9 -> 6, of which waited for: 2 -> 2; matrix products, arithmetic and copies ran while one was open for 3% -> 5% of each run, Pallas kernels for 28% -> 62%
where the time goes in v3:
time: 498 us; the launch traced here: 491 us
  Pallas kernels  405 us (81%)
  waiting for transfers between devices  24.2 us (5%)
  other arithmetic  20.7 us (4%)
  local copies, waits for them, and re-layouts  17.6 us (4%)
  between operations  14.5 us (3%)
  starting transfers between devices  8.52 us (2%)
    pallas_call x1, Pallas kernels, reduce_all(): pl.pallas_call(functools.partial(reduce_kernel, None), out_shape=[jax.Sha...  156 us
    pallas_call x2, Pallas kernels, sending_attention(): pl.pallas_call(functools.partial(sending_attn_kernel, length // 2, slot),...  77.1 us
    pallas_call x1, Pallas kernels, start(): pl.pallas_call(functools.partial(start_kernel, n), in_specs=[pl.BlockSpec...  67.5 us
    pallas_call x1, Pallas kernels, transition(): pl.pallas_call(trans_kernel, grid_spec=pl.GridSpec(grid=(length // rb,),...  26.6 us
    pallas_call x1, Pallas kernels, back(): pl.pallas_call(functools.partial(back_kernel, len(ys)), grid_spec=pl.Grid...  20.4 us
    pallas_call x1, Pallas kernels, pair_bwd(): pl.pallas_call(functools.partial(pair_bwd_kernel, rows), grid=(2 * steps,...  17.8 us
    pallas_call x1, Pallas kernels, small_sum(): pl.pallas_call(small_kernel, out_shape=jax.ShapeDtypeStruct(x.shape, f32)...  14 us
    pallas_call x2, Pallas kernels, wgrad(): pl.pallas_call(functools.partial(wgrad_kernel, each), grid=(steps,), in_s...  13.2 us
  transfers between devices with their start and end apart: 6, of which 2 were waited for; matrix products, arithmetic and copies ran while one was open for 5% of the time, Pallas kernels for 62%

profile of v3, /device:TPU:0, one launch (start us, length us, event | category | flops | bytes accessed | tf_op | source)
XLA Modules:
  0.0 490.9 jit_solution(2848604251574360465)
XLA Ops:
  8.9 1.2 tile.2
  10.1 67.5 %start.1 = (bf16[384,4608]{1,0:T(8,128)(2,1)}, bf16[768,3072]{1,0:T(8,128)(2,1)}, bf16[768,768]{1,0:T(8,128)(2,1)}, bf16[768,3072]{1,0:T(8,128)(2,1)}, bf16[1536...) custom-call(s32[2]{0:T(128)} %counts.1, bf16[1024,128]{1,0:T(8,128)(2,1)} %copy.49.pw, f32[1,256]{1,0:T(1,128)} %bitcast.148, ...), custom_call_target="tpu_custom_call" | custom-call | tf_op jit(solution)/shard_map/start/pallas_call | solution.py:331
  77.7 1.3 fusion.11
  81.7 12.8 %front.1 = (bf16[8,8,48,768]{3,2,1,0:T(8,128)(2,1)}, bf16[768,768]{1,0:T(8,128)(2,1)}, bf16[768,768]{1,0:T(8,128)(2,1)}, bf16[768,768]{1,0:T(8,128)(2,1)}, bf16[...) custom-call(bf16[768,768]{1,0:T(8,128)(2,1)} %bitcast.121, bf16[768,384]{1,0:T(8,128)(2,1)} %bitcast.129, ...), custom_call_target="tpu_custom_call" | custom-call | flops 6341787648 | bytes 20971520 | tf_op jit(solution)/shard_map/front/pallas_call | solution.py:588
  94.5 4.6 all-to-all-start
  99.2 0.9 copy.50
  101.5 26.6 %transition.1 = (f32[768,768]{1,0:T(8,128)}, bf16[768,768]{1,0:T(8,128)(2,1)}, f32[768,384]{1,0:T(8,128)}, bf16[768,2304]{1,0:T(8,128)(2,1)}, bf16[768,384]{1,0:...) custom-call(bf16[768,768]{1,0:T(8,128)(2,1)} %bitcast.122, ...), custom_call_target="tpu_custom_call" | custom-call | flops 13589544960 | bytes 41943040 | tf_op jit(solution)/shard_map/transition/pallas_call | solution.py:665
  128.2 5.4 %wgrad.3.refs_1_ = bf16[2,16,48,768]{3,2,1,0:T(8,128)(2,1)} custom-call(bf16[768,1536]{1,0:T(8,128)(2,1)} %get-tuple-element.72.lhs, bf16[768,768]{1,0:T(8,128)(2,1)} %get-tuple-element.73.refs_0_), custom_call_target="tpu_custom_call" | custom-call | flops 1811939328 | bytes 5898240 | tf_op jit(solution)/shard_map/wgrad/pallas_call | solution.py:794
  133.6 7.8 %wgrad.2.refs_0_ = bf16[2,16,48,1536]{3,2,1,0:T(8,128)(2,1)} custom-call(bf16[768,768]{1,0:T(8,128)(2,1)} %get-tuple-element.70.lhs, bf16[768,3072]{1,0:T(8,128)(2,1)} %get-tuple-element.71.refs_0_), custom_call_target="tpu_custom_call" | custom-call | flops 3623878656 | bytes 10616832 | tf_op jit(solution)/shard_map/wgrad/pallas_call | solution.py:794
  141.4 11.7 %all-to-all-done.x_ref = bf16[8,8,48,768]{3,2,1,0:T(8,128)(2,1)} async-done(((bf16[8,8,48,768]{3,2,1,0:T(8,128)(2,1)}), bf16[8,8,48,768]{3,2,1,0:T(8,128)(2,1)}, u32[]{:S(2)}, u32[]{:S(2)}) %all-to-all-start) | async-done | bytes 4718624 | tf_op jit(solution)/shard_map/all_to_all | solution.py:1110
  153.0 38.7 %attention_and_send.3 = (bf16[8,4,48,768]{3,2,1,0:T(8,128)(2,1)}, bf16[4,2,192,768]{3,2,1,0:T(8,128)(2,1)}) custom-call(s32[8]{0:T(128)} %dynamic_slice.3.owner_ref, bf16[8,8,48,768]{3,2,1,0:T(8,128)(2,1)} %all-to-all-done.x_ref, bf16[4,2,192,768]{3,2,1,0:T(8,128)(2,1)} %all-gather.5.cloned.1.call-done.bias_ref), custom_call_target="tpu_custom_call" | custom-call | flops 14495514624 | bytes 9437184 | tf_op jit(solution)/shard_map/attention_and_send/pallas_call | solution.py:491
  192.6 38.4 %attention_and_send.2 = (bf16[8,4,48,768]{3,2,1,0:T(8,128)(2,1)}, bf16[4,2,192,768]{3,2,1,0:T(8,128)(2,1)}) custom-call(s32[8]{0:T(128)} %dynamic_slice.3.owner_ref, bf16[8,8,48,768]{3,2,1,0:T(8,128)(2,1)} %all-to-all-done.x_ref, bf16[4,2,192,768]{3,2,1,0:T(8,128)(2,1)} %all-gather.3.cloned.1.call-done.bias_ref), custom_call_target="tpu_custom_call" | custom-call | flops 14495514624 | bytes 9437184 | tf_op jit(solution)/shard_map/attention_and_send/pallas_call | solution.py:491
  231.2 0.9 broadcast_multiply_fusion
  232.1 20.4 %back.1 = (f32[768,768]{1,0:T(8,128)}, f32[768,768]{1,0:T(8,128)}, f32[768,384]{1,0:T(8,128)}, bf16[768,768]{1,0:T(8,128)(2,1)}, bf16[768,768]{1,0:T(8,128)(2,1)...) custom-call(bf16[8,4,48,768]{3,2,1,0:T(8,128)(2,1)} %get-tuple-eleme, ...), custom_call_target="tpu_custom_call" | custom-call | flops 6341787648 | bytes 41943040 | tf_op jit(solution)/shard_map/back/pallas_call | solution.py:747
  255.3 155.9 %reduce_grads.1 = (f32[48,128]{1,0:T(8,128)}, bf16[2,2,2,2,48,1536]{5,4,3,2,1,0:T(8,128)(2,1)}, bf16[2,2,2,2,48,1152]{5,4,3,2,1,0:T(8,128)(2,1)}, bf16[2,2,2,2,4...) custom-call(bf16[2,16,48,1536]{3,2,1,0:T(8,128)(2,1)} %wgrad.2.refs_0_, ...), custom_call_target="tpu_custom_call" | custom-call | tf_op jit(solution)/shard_map/reduce_grads/pallas_call | solution.py:1018
  411.2 1.8 convert.3
  413.1 1.1 pad_maximum_fusion.4
  415.8 1.3 fusion.9
  417.1 2.6 pad_maximum_fusion.1
  419.7 2.6 pad_maximum_fusion
  422.5 2.2 pad_maximum_fusion.2
  424.7 1.1 copy.76
  425.8 1.1 copy.77
  427.0 1.1 pad_maximum_fusion.3
  428.1 3.6 all-to-all-start.1
  431.7 1.7 bitcast_convert_fusion
  435.1 12.4 %all-to-all-done.1 = bf16[8,2,2,24,768]{4,3,2,1,0:T(8,128)(2,1)S(1)} async-done(((bf16[8,2,2,24,768]{4,3,2,1,0:T(8,128)(2,1)}), bf16[8,2,2,24,768]{4,3,2,1,0:T(8,128)(2,1)S(1)}, u32[]{:S(2)}, u32[]{:S(2)}) %all-to-all-start.1) | async-done | bytes 1179680 | tf_op jit(solution)/shard_map/all_to_all | solution.py:1188
  447.5 1.0 copy-done.4
  448.6 17.8 %pair_bwd.1 = (f32[2,24,768,128]{3,2,1,0:T(8,128)}, f32[128,1024]{1,0:T(8,128)}) custom-call(bf16[2,24,768,128]{3,2,1,0:T(8,128)(2,1)} %x_ref.1, bf16[16,2,24,768]{3,2,1,0:T(8,128)(2,1)} %bitcast.127, bf16[256,1024]{1,0:T(8,128)(2,1)} %bitcast.134), custom_call_target="tpu_custom_call" | custom-call | flops 4718592000 | bytes 28311552 | tf_op jit(solution)/shard_map/pair_bwd/pallas_call | solution.py:186
  466.3 1.1 copy.78
  468.2 14.0 %small_sum.1 = f32[16,128]{1,0:T(8,128)} custom-call(f32[16,128]{1,0:T(8,128)} %add_bitcast_fusion.x), custom_call_target="tpu_custom_call" | custom-call | tf_op jit(solution)/shard_map/small_sum/pallas_call | solution.py:1050
  482.2 1.8 multiply_bitcast_fusion.1
  (65 shorter events, 13.9 us)
Async XLA Ops:
  7.2 145.9 %all-gather.5.cloned.1.call-start = ((), (), s32[]{:S(2)}) async-start(), calls=%async_computation.5 | async-start | bytes 2949120 | tf_op jit(solution)/shard_map/all_gather | solution.py:1091
  77.6 2.3 copy-start.11
  77.6 2.8 copy-start.7
  77.7 3.4 copy-start.10
  94.5 6.4 %copy-start.12 = (s32[32]{0:T(128)S(1)}, s32[32]{0:T(128)}, u32[]{:S(2)}) copy-start(s32[32]{0:T(128)} %param.20) | copy-start | bytes 388
  94.5 58.5 %all-to-all-start = ((bf16[8,8,48,768]{3,2,1,0:T(8,128)(2,1)}), bf16[8,8,48,768]{3,2,1,0:T(8,128)(2,1)}, u32[]{:S(2)}, u32[]{:S(2)}) async-start(bf16[8,8,48,768]{3,2,1,0:T(8,128)(2,1)} %get-tuple-element.67), calls=%async_computation | async-start | bytes 9437184 | tf_op jit(solution)/shard_map/all_to_all | solution.py:1110
  99.2 93.4 %all-gather.3.cloned.1.call-start = ((), (), s32[]{:S(2)}) async-start(), calls=%async_computation.4 | async-start | bytes 2949120 | tf_op jit(solution)/shard_map/all_gather | solution.py:1091
  100.1 324.6 %reduce-scatter.5.cloned.1.call-start = ((), (), s32[]{:S(2)}) async-start(), calls=%async_computation.7 | async-start | bytes 2949120 | tf_op jit(solution)/shard_map/reduce_scatter | solution.py:1164
  191.7 0.7 copy-start.8
  191.7 0.7 copy-start.5
  191.7 0.7 copy-start.9
  191.8 234.1 %reduce-scatter.3.cloned.1.call-start = ((), (), s32[]{:S(2)}) async-start(), calls=%async_computation.6 | async-start | bytes 2949120 | tf_op jit(solution)/shard_map/reduce_scatter | solution.py:1164
  411.2 1.8 copy-start.2
  413.0 2.1 copy-start
  413.0 2.8 copy-start.1
  427.0 4.7 copy-start.3
  428.1 19.4 %all-to-all-start.1 = ((bf16[8,2,2,24,768]{4,3,2,1,0:T(8,128)(2,1)}), bf16[8,2,2,24,768]{4,3,2,1,0:T(8,128)(2,1)S(1)}, u32[]{:S(2)}, u32[]{:S(2)}) async-start(bf16[8,2,2,24,768]{4,3,2,1,0:T(8,128)(2,1)} %pad_maximum_fusion.3), calls=%async_computation.3 | async-start | bytes 2359296 | tf_op jit(solution)/shard_map/all_to_all | solution.py:1188
  431.7 1.7 copy-start.6
  447.5 1.0 copy-start.4
Sparse Core Ops, SparseCore 0:
  80.0 51.9 all-gather.4
  133.6 49.2 all-gather.2
  191.9 48.6 reduce-scatter.4
  242.7 62.2 reduce-scatter.2

commit v4 on v3

--- a/solution.py
+++ b/solution.py
@@ -56,8 +56,18 @@
 BITS = {"c": ("lo", 1), "x": ("lo", 2), "y": ("fsdp", 1), "z0": ("up", 1), "z1": ("up", 2)}
 PEERS = (("c",), ("x",), ("y",), ("c", "x"), ("c", "y"), ("x", "y"), ("c", "x", "y"))
 SAMPLE_ORDER = (("x",), ("y",), ("x", "y"), ("c", "x"), ("c", "y"), ("c", "x", "y"), ("c",), ())
-SUM_ORDERS = (("c", "x", "y", "z0", "z1"), ("c", "y", "z0", "x", "z1"), ("c", "z0", "x", "y", "z1"))
-COPY_ORDERS = (("z1", "z0", "x", "c"), ("x", "z1", "z0", "c"))
+SUM_ORDERS = (
+    ("c", "x", "y", "z0", "z1"),
+    ("c", "x", "z0", "y", "z1"),
+    ("c", "y", "x", "z0", "z1"),
+    ("c", "z0", "y", "z1", "x"),
+)
+COPY_ORDERS = (
+    ("x", "z0", "z1", "c"),
+    ("z0", "z1", "x", "c"),
+    ("z1", "x", "z0", "c"),
+    ("z1", "z0", "x", "c"),
+)
 
 
 def coords():
@@ -154,10 +164,13 @@
     )(counts, pair, pw_t, gain)
 
 
-def pair_bwd_kernel(rows, x_ref, bg_ref, a_ref, out_ref, q_ref, low_buf):
-    @pl.when(pl.program_id(0) == 0)
-    def _():
-        q_ref[...] = jnp.zeros_like(q_ref)
+def pair_bwd_kernel(rows, x_ref, bg_ref, a_ref, out_ref, *sums):
+    if sums:
+        q_ref, low_buf = sums
+
+        @pl.when(pl.program_id(0) == 0)
+        def _():
+            q_ref[...] = jnp.zeros_like(q_ref)
 
     width = out_ref.shape[-1]
     heads, _, _, length = bg_ref.shape
@@ -167,15 +180,17 @@
     step = 2 - rows % 2
     for r in range(0, rows, step):
         x_hat, scale = pair_norm(*(x_ref[0, r + t] for t in range(step)))
-        low_buf[:, r * width : (r + step) * width] = x_hat.astype(bf16)
+        if sums:
+            low_buf[:, r * width : (r + step) * width] = x_hat.astype(bf16)
         u = u_all[:, r * width : (r + step) * width]
         grad = (u - x_hat * lane_means((u * x_hat).astype(bf16))) * scale
         for t in range(step):
             out_ref[0, r + t] = grad[:, t * width : (t + 1) * width]
-    q_ref[...] += dot(grads.astype(bf16), low_buf[...])
-
-
-def pair_bwd(pair, bias_grad, high, low):
+    if sums:
+        q_ref[...] += dot(grads.astype(bf16), low_buf[...])
+
+
+def pair_bwd(pair, bias_grad, high, low, with_sums):
     _, total, length, width = pair.shape
     rows = 8 if total % 8 == 0 else total
     steps = total // rows
@@ -183,7 +198,7 @@
     eye = jnp.eye(rows, dtype=bf16)
     both = jnp.stack([high, low])
     weights = (both[:, :, None, None, :] * eye[None, None, :, :, None]).reshape(2 * heads * rows, rows * width)
-    grad, moments = pl.pallas_call(
+    grad, *moments = pl.pallas_call(
         functools.partial(pair_bwd_kernel, rows),
         grid=(2 * steps,),
         in_specs=[
@@ -194,17 +209,19 @@
         out_specs=[
             pl.BlockSpec((1, rows, length, width), lambda i: (i // steps, i % steps, 0, 0)),
             pl.BlockSpec((heads * rows, rows * width), lambda i: (0, 0)),
-        ],
+        ][: 1 + with_sums],
         out_shape=[
             jax.ShapeDtypeStruct(pair.shape, f32),
             jax.ShapeDtypeStruct((heads * rows, rows * width), f32),
-        ],
-        scratch_shapes=[pltpu.VMEM((length, rows * width), bf16)],
+        ][: 1 + with_sums],
+        scratch_shapes=[pltpu.VMEM((length, rows * width), bf16)][:with_sums],
         compiler_params=params(),
         cost_estimate=pl.CostEstimate(flops=2 * pair.size * 500, bytes_accessed=pair.size * 6, transcendentals=pair.size),
         name="pair_bwd",
     )(pair, bias_grad, weights)
-    moments = moments.reshape(heads, rows, rows, width)
+    if not moments:
+        return grad, None
+    moments = moments[0].reshape(heads, rows, rows, width)
     return grad, sum(moments[:, r, r] for r in range(rows))
 
 
@@ -938,6 +955,69 @@
             )
 
 
+class BiasHome:
+    def __init__(self, where, raw, done, home_out, home, kept, got, last, done_v, out, load_sems, send_sems, recv_sems):
+        self.where, self.raw, self.home, self.kept, self.got, self.last = where, raw, home, kept, got, last
+        self.done_v, self.out, self.send_sems, self.recv_sems = done_v, out, send_sems, recv_sems
+        self.z0, self.z1 = bit_of(where, "z0"), bit_of(where, "z1")
+        self.loads = [
+            pltpu.make_async_copy(raw.at[:, self.z0], kept, load_sems.at[0]),
+            pltpu.make_async_copy(done, done_v, load_sems.at[1]),
+        ]
+        self.keep = pltpu.make_async_copy(out.at[place(where)], home.at[place(where)], load_sems.at[2])
+        self.written = pltpu.make_async_copy(home, home_out, load_sems.at[3])
+        self.copies = []
+
+    @staticmethod
+    def scratch(block, members):
+        plane, length = block[1], block[2]
+        rows = pltpu.VMEM((members, 2, 2 * plane // members, length), bf16)
+        return [
+            rows,
+            pltpu.VMEM((2,) + block, bf16),
+            pltpu.VMEM((2,) + block, bf16),
+            pltpu.VMEM(block, bf16),
+            pltpu.VMEM(block, bf16),
+            rows,
+            pltpu.SemaphoreType.DMA((4,)),
+            pltpu.SemaphoreType.DMA((2 + len(PEERS),)),
+            pltpu.SemaphoreType.DMA((2 + len(PEERS),)),
+        ]
+
+    def send(self, k, src, dst, other):
+        self.copies.append(remote(src, dst, self.send_sems.at[k], self.recv_sems.at[k], other))
+
+    def lay(self, slot, value):
+        members, _, rows, _ = self.out.shape
+        each = rows // 2
+        for m in range(members):
+            part = [value[c, m * each : (m + 1) * each, :] for c in range(2)]
+            self.out[m, slot] = jnp.concatenate(part, axis=0).astype(bf16)
+
+    def advance(self, k):
+        if k == 0:
+            self.send(0, self.raw.at[:, 1 - self.z0], self.got, across(self.where, "z0"))
+        elif k == 1:
+            self.loads[0].wait()
+            self.copies[0].wait_recv()
+            self.kept[...] = (self.kept[...].astype(f32) + self.got[...].astype(f32)).astype(bf16)
+            self.send(1, self.kept.at[1 - self.z1], self.last, across(self.where, "z1"))
+            self.loads[1].wait()
+            self.lay(0, self.done_v[...].astype(f32))
+        elif k == 2:
+            self.copies[1].wait_recv()
+            self.lay(1, self.kept[self.z1].astype(f32) + self.last[...].astype(f32))
+            for j, names in enumerate(PEERS):
+                peer = across(self.where, *names)
+                self.send(2 + j, self.out.at[place(peer)], self.home.at[place(self.where)], peer)
+            self.keep.start()
+        elif k == 3:
+            self.keep.wait()
+            for copy in self.copies[2:]:
+                copy.wait_recv()
+            self.written.start()
+
+
 def reduce_kernel(n_left, *refs):
     refs = list(refs)
 
@@ -945,12 +1025,14 @@
         out, refs[:] = refs[:n], refs[n:]
         return out
 
-    early_in, acts, (small, small_o) = take(2), take(7), take(2)
-    late_out, early_out = take(3), take(2)
+    early_in, acts, (raw, done, pair), (small, small_o) = take(2), take(7), take(3), take(2)
+    late_out, early_out, (home,) = take(3), take(2), take(1)
     n_late, n_early = len(late_plan), len(early_plan)
     late_scratch, early_scratch = take(2 * n_late + 4), take(2 * n_early + 4)
     bufs, (sbuf, s_send, s_recv, a_sems) = take(7), take(4)
     where = coords()
+    bias = BiasHome(where, raw, done, home, *take(9))
+    (moment_buf, p_sems) = take(2)
     loads = [pltpu.make_async_copy(src, dst, a_sems.at[i]) for i, (src, dst) in enumerate(zip(acts, bufs))]
 
     def reducer(plan, ins, outs, scratch):
@@ -961,12 +1043,12 @@
     for copy in loads:
         copy.start()
     late = reducer(late_plan, None, late_out, late_scratch)
+    for copy in bias.loads:
+        copy.start()
     sbuf[0] = small[...]
-    greet([across(where, name) for name in BITS])
+    greet([across(where, *names) for names in PEERS + (("z0",), ("z1",))])
     small_sum = SmallSum(where, sbuf, s_send, s_recv)
-    small_sum.advance(0)
-    for i in range(n_early):
-        early.advance(i, 0)
+    bias.advance(0)
 
     first, gp, cn, ml1, ml2, gated, ga = bufs
     sides = ((first, (gp,)), (cn, (ml1, ml2)), (gated, (ga,)))
@@ -978,7 +1060,8 @@
             loads[k].wait()
             waited.add(k)
 
-    for i, (a, c0, w, _, _) in enumerate(late_plan):
+    def multiply(i):
+        a, c0, w, _, _ = late_plan[i]
         lhs, rhs = sides[a]
         k0 = (0, 2, 5)[a]
         for k in range(k0, k0 + 1 + len(rhs)):
@@ -993,33 +1076,75 @@
             r = rhs[c // rhs[0].shape[1]]
             c = c % rhs[0].shape[1] + c0
             late.store(i, g * row_groups, dot(turned[a], r[:, c : c + w]).astype(bf16))
-        late.advance(i, 0)
-        if i in (1, 4):
-            for e in range(n_early):
-                early.advance(e, 1 + i // 4)
-    for k in range(1, Reducer.stages):
-        for i in range(n_late):
-            late.advance(i, k)
-        if k + 2 < Reducer.stages:
-            for i in range(n_early):
-                early.advance(i, k + 2)
-        if k < 6:
+
+    pair_rows, length, width = pair.shape[1:]
+    heads = bias.home.shape[0] * bias.home.shape[1]
+
+    def pair_copy(c, r):
+        return pltpu.make_async_copy(pair.at[c, r], gp.at[:, pl.ds(r * width, width)], p_sems.at[r])
+
+    def moments(c):
+        for r in range(pair_rows):
+            pair_copy(c, r).wait()
+        for r in range(0, pair_rows, 2):
+            cols = slice(r * width, (r + 2) * width)
+            gp[:, cols] = pair_norm(gp[:, cols])[0].astype(bf16)
+        total = 0.0
+        for g in range(0, pair_rows, 8):
+            grads = bias.home[...].astype(f32)[:, :, c * pair_rows + g : c * pair_rows + g + 8, :]
+            total += dot(grads.reshape(heads * 8, length).astype(bf16), gp[:, g * width : (g + 8) * width])
+        if c == 0:
+            for r in range(pair_rows):
+                pair_copy(1, r).start()
+            moment_buf[...] = total
+        else:
+            total = total + moment_buf[...]
+            row = lax.rem(lax.broadcasted_iota(jnp.int32, (heads * 8, width), 0), 8)
+            own = sum(jnp.where(row == r, total[:, r * width : (r + 1) * width], 0.0) for r in range(8))
+            sbuf[0, small.shape[0] - heads :, :] = jnp.sum(own.reshape(heads, 8, width), axis=1)
+
+    stage = {}
+    multiplied = 0
+    for at, s in enumerate(schedule):
+        k = stage.get(s, 0)
+        stage[s] = k + 1
+        if s == -2:
             small_sum.advance(k)
+        elif s == -1:
+            bias.advance(k + 1)
+            if k > 1:
+                moments(k - 2)
+        elif s < n_late:
+            if k == 0:
+                multiply(s)
+                multiplied += late_plan[s][0] == 0
+                if late_plan[s][0] == 0 and multiplied == sum(p[0] == 0 for p in late_plan):
+                    for r in range(pair_rows):
+                        pair_copy(0, r).start()
+            late.advance(s, k)
+        else:
+            early.advance(s - n_late, k)
+    bias.written.wait()
     small_o[...] = sbuf[10]
-    for copy in late.sends + early.sends + small_sum.copies:
+    for copy in late.sends + early.sends + small_sum.copies + bias.copies:
         copy.wait_send()
 
 
-def reduce_all(early, acts, small):
+def reduce_all(early, acts, raw, done, pair, small):
+    raw = raw.reshape((2, 2) + raw.shape[1:])
+    block = done.shape
+    members = group_size
     widths = (1536, 1152, 384, 1536, 768)
     shapes = [jax.ShapeDtypeStruct((2, 2, 2, 2, 48, w), bf16) for w in widths]
     any_spec = pl.BlockSpec(memory_space=pl.ANY)
     vm = pl.BlockSpec(memory_space=pltpu.VMEM)
     return pl.pallas_call(
         functools.partial(reduce_kernel, None),
-        out_shape=[jax.ShapeDtypeStruct(small.shape, f32)] + shapes,
-        in_specs=[any_spec] * (len(early) + len(acts)) + [vm],
-        out_specs=[vm] + [any_spec] * len(shapes),
+        out_shape=[jax.ShapeDtypeStruct(small.shape, f32)]
+        + shapes
+        + [jax.ShapeDtypeStruct((members, 2, 2 * block[1] // members, block[2]), bf16)],
+        in_specs=[any_spec] * (len(early) + len(acts) + 3) + [vm],
+        out_specs=[vm] + [any_spec] * (len(shapes) + 1),
         scratch_shapes=Reducer.scratch(late_plan)
         + Reducer.scratch(early_plan)
         + [pltpu.VMEM(a.shape, bf16) for a in acts]
@@ -1028,48 +1153,34 @@
             pltpu.SemaphoreType.DMA((5,)),
             pltpu.SemaphoreType.DMA((5,)),
             pltpu.SemaphoreType.DMA((len(acts),)),
-        ],
+        ]
+        + BiasHome.scratch(block, members)
+        + [pltpu.VMEM((2 * members * 8, 8 * pair.shape[3]), f32), pltpu.SemaphoreType.DMA((pair.shape[1],))],
         compiler_params=params(collective_id=1, has_side_effects=True),
         name="reduce_grads",
-    )(*early, *acts, small)
-
-
-def small_kernel(x, out, buf, send_sems, recv_sems):
-    where = coords()
-    buf[0] = x[...]
-    greet([across(where, name) for name in BITS])
-    total = SmallSum(where, buf, send_sems, recv_sems)
-    for k in range(6):
-        total.advance(k)
-    out[...] = buf[10]
-    for copy in total.copies:
-        copy.wait_send()
-
-
-def small_sum(x):
-    return pl.pallas_call(
-        small_kernel,
-        out_shape=jax.ShapeDtypeStruct(x.shape, f32),
-        in_specs=[pl.BlockSpec(memory_space=pltpu.VMEM)],
-        out_specs=pl.BlockSpec(memory_space=pltpu.VMEM),
-        scratch_shapes=[
-            pltpu.VMEM((11,) + x.shape, f32),
-            pltpu.SemaphoreType.DMA((5,)),
-            pltpu.SemaphoreType.DMA((5,)),
-        ],
-        compiler_params=params(collective_id=5, has_side_effects=True),
-        name="small_sum",
-    )(x)
+    )(*early, *acts, raw, done, pair, small)
 
 
 late_plan = (
-    (0, 0, 1024, 0, 0),
-    (0, 1024, 512, 1, 1),
-    (1, 0, 512, 1, 1),
-    (1, 512, 640, 2, 0),
-    (2, 0, 384, 2, 1),
+    (0, 0, 768, 2, 3),
+    (0, 768, 768, 2, 0),
+    (1, 0, 640, 0, 2),
+    (1, 640, 512, 3, 3),
+    (2, 0, 384, 2, 3),
 )
-early_plan = ((0, 0, 768, 0, 0), (0, 768, 768, 1, 1), (1, 0, 768, 2, 0))
+early_plan = (
+    (0, 0, 768, 1, 3),
+    (0, 768, 768, 0, 3),
+    (1, 0, 384, 0, 2),
+    (1, 384, 384, 2, 1),
+)
+schedule = (
+    8, 6, 3, 8, 4, 6, 1, 4, 5, 5, 7, 1, 4, 3, 0, -1, 2, 0, 4, 6, 1, 2, 8, 5,
+    7, 3, 8, 3, 6, 1, 5, 4, 7, 8, 5, 0, 2, 8, 3, 4, 7, 3, -1, 4, 6, 3, 1, 0,
+    7, 6, 2, 3, 5, 6, 1, 7, -1, 8, 5, 6, 1, 2, 0, 7, -1, 4, 2, -2, 0, 7, 8, -2,
+    2, 4, 5, 6, 1, 0, 3, 0, 2, 8, 4, 5, 7, 6, -2, 7, 5, 8, 1, -2, 3, 0, -2, 2,
+    -2, 1, 0, 2,
+)
 
 
 def on_device(
@@ -1161,8 +1272,11 @@
             y, bg = attention(owners, x, biases[t], t)
             y = lax.all_to_all(y, plane, 0, 0, tiled=True)
         ys.append(y)
+        if direct and t == slots - 1:
+            bias_grads.append(bg)
+            continue
         mine = lax.psum_scatter(bg, "up", scatter_dimension=0, tiled=True)
-        bias_grads.append(mine.reshape(2, members, rows, length).transpose(1, 0, 2, 3))
+        bias_grads.append(mine.reshape(2, members * rows, length))
 
     block_out, tokens_grad, cond_grad, gated, ga, gp, ml1, qbg, cbg1, cgg = back(
         ys, sg, gg, s1, g1, part, u2, dcond2, tok, cnd, og, cgain, wc, wq, wo
@@ -1176,24 +1290,26 @@
     pieces = [cgg, cbg1, cbg2, qbg]
     stacked = jnp.concatenate([p.reshape(-1, 128) for p in pieces], axis=0)
     if direct:
-        height = -(-stacked.shape[0] // 8) * 8
+        height = -(-stacked.shape[0] // 8) * 8 + head_count
         stacked = jnp.pad(stacked, ((0, height - stacked.shape[0]), (0, 0)))
-        stacked, *totals = reduce_all(early, (first, gp, cn, ml1, ml2, gated, ga), stacked)
-        *bias_grads, stacked = lax.optimization_barrier((*bias_grads, stacked))
+        stacked, *totals, bias_grad = reduce_all(
+            early, (first, gp, cn, ml1, ml2, gated, ga), bias_grads[1], bias_grads[0], pair, stacked
+        )
         qkvg_total, cond_total, out_total, up_total, down_total = [
             laid_out(p, w.shape[0]) for p, w in zip(totals, (qkvg_weight, cond_weight, out_weight, up_weight, down_weight))
         ]
     else:
         stacked = lax.psum(stacked, ("up", "lo", "fsdp"))
-    bias_grad = lax.all_to_all(jnp.stack(bias_grads, axis=1), plane, 0, 0, tiled=True)
+        split = [b.reshape(2, members, rows, length).transpose(1, 0, 2, 3) for b in bias_grads]
+        bias_grad = lax.all_to_all(jnp.stack(split, axis=1), plane, 0, 0, tiled=True)
     bias_grad = bias_grad.reshape(head_count, 2, rows, length)
     pw = pair_weight.astype(f32).T
     scaled = pw * pair_gain
     centered = scaled - jnp.mean(scaled, axis=-1, keepdims=True)
     high = centered.astype(bf16)
     low = (centered - high.astype(f32)).astype(bf16)
-    pair_grad, moments = pair_bwd(pair, bias_grad, high, low)
-    moments = small_sum(moments) if direct else lax.psum(moments, ("up", "lo", "fsdp"))
+    pair_grad, moments = pair_bwd(pair, bias_grad, high, low, not direct)
+    moments = stacked[-head_count:] if direct else lax.psum(moments, ("up", "lo", "fsdp"))
     small = stacked.reshape(-1)
     ends = [0]
     for p in pieces:

time: 498 us -> 459 us (0.922)
  Pallas kernels: 405 us -> 387 us
  waiting for transfers between devices: 24.2 us -> 11.4 us
    pallas_call x1 -> x0, Pallas kernels: 14 us -> none  [small_sum(): pl.pallas_call(small_kernel, out_shape=jax.ShapeDtypeStruct(x.shape, f32)...]
    all_to_all x1 -> x0, waiting for transfers between devices: 12.4 us -> none  [on_device(): lax.all_to_all(jnp.stack(bias_grads, axis=1), plane, 0, 0, tiled=True)]
  transfers between devices with their start and end apart: 6 -> 4, of which waited for: 2 -> 1; matrix products, arithmetic and copies ran while one was open for 5% -> 1% of each run, Pallas kernels for 62% -> 33%
where the time goes in v4:
time: 459 us; the launch traced here: 451 us
  Pallas kernels  387 us (84%)
  other arithmetic  17.3 us (4%)
  local copies, waits for them, and re-layouts  15.9 us (3%)
  between operations  14.4 us (3%)
  waiting for transfers between devices  11.4 us (2%)
  starting transfers between devices  5.2 us (1%)
    pallas_call x1, Pallas kernels, reduce_all(): pl.pallas_call(functools.partial(reduce_kernel, None), out_shape=[jax.Sha...  152 us
    pallas_call x2, Pallas kernels, sending_attention(): pl.pallas_call(functools.partial(sending_attn_kernel, length // 2, slot),...  77 us
    pallas_call x1, Pallas kernels, start(): pl.pallas_call(functools.partial(start_kernel, n), in_specs=[pl.BlockSpec...  67.5 us
    pallas_call x1, Pallas kernels, transition(): pl.pallas_call(trans_kernel, grid_spec=pl.GridSpec(grid=(length // rb,),...  26.6 us
    pallas_call x1, Pallas kernels, back(): pl.pallas_call(functools.partial(back_kernel, len(ys)), grid_spec=pl.Grid...  20.5 us
    pallas_call x1, Pallas kernels, pair_bwd(): pl.pallas_call(functools.partial(pair_bwd_kernel, rows), grid=(2 * steps,...  17.1 us
    pallas_call x2, Pallas kernels, wgrad(): pl.pallas_call(functools.partial(wgrad_kernel, each), grid=(steps,), in_s...  13.2 us
    pallas_call x1, Pallas kernels, front(): pl.pallas_call(front_kernel, grid_spec=pl.GridSpec(grid=(length // rb,),...  12.8 us
  transfers between devices with their start and end apart: 4, of which 1 were waited for; matrix products, arithmetic and copies ran while one was open for 1% of the time, Pallas kernels for 33%

profile of v4, /device:TPU:0, one launch (start us, length us, event | category | flops | bytes accessed | tf_op | source)
XLA Modules:
  0.0 451.2 jit_solution(13059871211000199562)
XLA Ops:
  7.2 0.8 multiply_bitcast_fusion
  8.1 0.8 copy.37.pw
  8.9 1.2 tile.2
  10.1 67.5 %start.1 = (bf16[384,4608]{1,0:T(8,128)(2,1)}, bf16[768,3072]{1,0:T(8,128)(2,1)}, bf16[768,768]{1,0:T(8,128)(2,1)}, bf16[768,3072]{1,0:T(8,128)(2,1)}, bf16[1536...) custom-call(s32[2]{0:T(128)} %counts.1, bf16[1024,128]{1,0:T(8,128)(2,1)} %copy.37.pw, f32[1,256]{1,0:T(1,128)} %bitcast.114, ...), custom_call_target="tpu_custom_call" | custom-call | tf_op jit(solution)/shard_map/start/pallas_call | solution.py:348
  77.7 1.3 fusion.11
  79.0 0.9 copy.38
  81.7 12.8 %front.1 = (bf16[8,8,48,768]{3,2,1,0:T(8,128)(2,1)}, bf16[768,768]{1,0:T(8,128)(2,1)}, bf16[768,768]{1,0:T(8,128)(2,1)}, bf16[768,768]{1,0:T(8,128)(2,1)}, bf16[...) custom-call(bf16[768,768]{1,0:T(8,128)(2,1)} %bitcast.98, bf16[768,384]{1,0:T(8,128)(2,1)} %bitcast.106, ...), custom_call_target="tpu_custom_call" | custom-call | flops 6341787648 | bytes 20971520 | tf_op jit(solution)/shard_map/front/pallas_call | solution.py:605
  94.5 4.6 %all-to-all-start = ((bf16[8,8,48,768]{3,2,1,0:T(8,128)(2,1)}), bf16[8,8,48,768]{3,2,1,0:T(8,128)(2,1)}, u32[]{:S(2)}, u32[]{:S(2)}) async-start(bf16[8,8,48,768]{3,2,1,0:T(8,128)(2,1)} %get-tuple-element.63), calls=%async_computation | async-start | bytes 9437184 | tf_op jit(solution)/shard_map/all_to_all | solution.py:1221
  99.2 0.9 copy.39
  101.8 26.6 %transition.1 = (f32[768,768]{1,0:T(8,128)}, bf16[768,768]{1,0:T(8,128)(2,1)}, f32[768,384]{1,0:T(8,128)}, bf16[768,2304]{1,0:T(8,128)(2,1)}, bf16[768,384]{1,0:...) custom-call(bf16[768,768]{1,0:T(8,128)(2,1)} %bitcast.99, ...), custom_call_target="tpu_custom_call" | custom-call | flops 13589544960 | bytes 41943040 | tf_op jit(solution)/shard_map/transition/pallas_call | solution.py:682
  128.5 5.4 %wgrad.3.refs_1_ = bf16[2,16,48,768]{3,2,1,0:T(8,128)(2,1)} custom-call(bf16[768,1536]{1,0:T(8,128)(2,1)} %get-tuple-element.68.lhs, bf16[768,768]{1,0:T(8,128)(2,1)} %get-tuple-element.69.refs_0_), custom_call_target="tpu_custom_call" | custom-call | flops 1811939328 | bytes 5898240 | tf_op jit(solution)/shard_map/wgrad/pallas_call | solution.py:811
  133.9 7.8 %wgrad.2.refs_0_ = bf16[2,16,48,1536]{3,2,1,0:T(8,128)(2,1)} custom-call(bf16[768,768]{1,0:T(8,128)(2,1)} %get-tuple-element.66.lhs, bf16[768,3072]{1,0:T(8,128)(2,1)} %get-tuple-element.67.refs_0_), custom_call_target="tpu_custom_call" | custom-call | flops 3623878656 | bytes 10616832 | tf_op jit(solution)/shard_map/wgrad/pallas_call | solution.py:811
  141.7 11.3 %all-to-all-done.x_ref = bf16[8,8,48,768]{3,2,1,0:T(8,128)(2,1)} async-done(((bf16[8,8,48,768]{3,2,1,0:T(8,128)(2,1)}), bf16[8,8,48,768]{3,2,1,0:T(8,128)(2,1)}, u32[]{:S(2)}, u32[]{:S(2)}) %all-to-all-start) | async-done | bytes 4718624 | tf_op jit(solution)/shard_map/all_to_all | solution.py:1221
  153.0 38.8 %attention_and_send.2 = (bf16[8,4,48,768]{3,2,1,0:T(8,128)(2,1)}, bf16[4,2,192,768]{3,2,1,0:T(8,128)(2,1)}) custom-call(s32[8]{0:T(128)} %dynamic_slice.3.owner_ref, bf16[8,8,48,768]{3,2,1,0:T(8,128)(2,1)} %all-to-all-done.x_ref, bf16[4,2,192,768]{3,2,1,0:T(8,128)(2,1)} %all-gather.3.cloned.1.call-done.bias_ref), custom_call_target="tpu_custom_call" | custom-call | flops 14495514624 | bytes 9437184 | tf_op jit(solution)/shard_map/attention_and_send/pallas_call | solution.py:508
  192.6 38.2 %attention_and_send.3 = (bf16[8,4,48,768]{3,2,1,0:T(8,128)(2,1)}, bf16[4,2,192,768]{3,2,1,0:T(8,128)(2,1)}) custom-call(s32[8]{0:T(128)} %dynamic_slice.3.owner_ref, bf16[8,8,48,768]{3,2,1,0:T(8,128)(2,1)} %all-to-all-done.x_ref, bf16[4,2,192,768]{3,2,1,0:T(8,128)(2,1)} %all-gather.5.cloned.1.call-done.bias_ref), custom_call_target="tpu_custom_call" | custom-call | flops 14495514624 | bytes 9437184 | tf_op jit(solution)/shard_map/attention_and_send/pallas_call | solution.py:508
  230.8 20.5 %back.1 = (f32[768,768]{1,0:T(8,128)}, f32[768,768]{1,0:T(8,128)}, f32[768,384]{1,0:T(8,128)}, bf16[768,768]{1,0:T(8,128)(2,1)}, bf16[768,768]{1,0:T(8,128)(2,1)...) custom-call(bf16[8,4,48,768]{3,2,1,0:T(8,128)(2,1)} %get-tuple-eleme, ...), custom_call_target="tpu_custom_call" | custom-call | flops 6341787648 | bytes 41943040 | tf_op jit(solution)/shard_map/back/pallas_call | solution.py:764
  251.2 0.7 reduce.1
  254.0 152.3 %reduce_grads.1 = (f32[64,128]{1,0:T(8,128)}, bf16[2,2,2,2,48,1536]{5,4,3,2,1,0:T(8,128)(2,1)}, bf16[2,2,2,2,48,1152]{5,4,3,2,1,0:T(8,128)(2,1)}, bf16[2,2,2,2,4...) custom-call(bf16[2,16,48,1536]{3,2,1,0:T(8,128)(2,1)} %wgrad.2.refs_, ...), custom_call_target="tpu_custom_call" | custom-call | tf_op jit(solution)/shard_map/reduce_grads/pallas_call | solution.py:1141
  406.3 0.9 slice_bitcast_fusion.5
  407.2 1.8 fusion.5
  409.0 1.3 slice_bitcast_fusion.6
  410.3 1.3 slice_bitcast_fusion.7
  411.6 1.1 fusion.12
  413.3 0.9 broadcast_multiply_fusion
  414.2 1.7 bitcast_convert_fusion
  415.9 0.9 copy-done
  416.8 1.3 fusion.9
  418.1 2.6 pad_maximum_fusion.1
  420.7 1.1 pad_maximum_fusion.3
  421.8 2.6 pad_maximum_fusion
  425.0 17.1 %pair_bwd.1 = f32[2,24,768,128]{3,2,1,0:T(8,128)} custom-call(bf16[2,24,768,128]{3,2,1,0:T(8,128)(2,1)} %x_ref.1, bf16[16,2,24,768]{3,2,1,0:T(8,128)(2,1)} %bitcast.104, bf16[256,1024]{1,0:T(8,128)(2,1)} %bitcast.96), custom_call_target="tpu_custom_call" | custom-call | flops 4718592000 | bytes 28311552 | tf_op jit(solution)/shard_map/pair_bwd/pallas_call | solution.py:201
  442.1 2.2 pad_maximum_fusion.2
  (48 shorter events, 7.6 us)
Async XLA Ops:
  7.2 145.8 %all-gather.3.cloned.1.call-start = ((), (), s32[]{:S(2)}) async-start(), calls=%async_computation.2 | async-start | bytes 2949120 | tf_op jit(solution)/shard_map/all_gather | solution.py:1202
  77.6 2.3 copy-start.8
  77.6 2.8 copy-start.5
  77.7 3.4 copy-start.7
  94.5 6.7 %copy-start.10 = (s32[32]{0:T(128)S(1)}, s32[32]{0:T(128)}, u32[]{:S(2)}) copy-start(s32[32]{0:T(128)} %param.20) | copy-start | bytes 388
  94.5 58.5 %all-to-all-start = ((bf16[8,8,48,768]{3,2,1,0:T(8,128)(2,1)}), bf16[8,8,48,768]{3,2,1,0:T(8,128)(2,1)}, u32[]{:S(2)}, u32[]{:S(2)}) async-start(bf16[8,8,48,768]{3,2,1,0:T(8,128)(2,1)} %get-tuple-element.63), calls=%async_computation | async-start | bytes 9437184 | tf_op jit(solution)/shard_map/all_to_all | solution.py:1221
  99.1 93.4 %all-gather.5.cloned.1.call-start = ((), (), s32[]{:S(2)}) async-start(), calls=%async_computation.3 | async-start | bytes 2949120 | tf_op jit(solution)/shard_map/all_gather | solution.py:1202
  100.1 153.9 %reduce-scatter.2.cloned.1.call-start = ((), (), s32[]{:S(2)}) async-start(), calls=%async_computation.4 | async-start | bytes 2949120 | tf_op jit(solution)/shard_map/reduce_scatter | solution.py:1278
  191.8 0.7 copy-start.6
  254.0 153.2 %copy-start.4 = (bf16[128,16]{0,1:T(8,128)(2,1)S(1)}, bf16[128,16]{0,1:T(8,128)(2,1)}, u32[]{:S(2)}) copy-start(bf16[128,16]{0,1:T(8,128)(2,1)} %param.29) | copy-start | bytes 12292
  254.0 153.2 %copy-start.9 = (f32[128]{0:T(128)S(1)}, f32[128]{0:T(128)}, u32[]{:S(2)}) copy-start(f32[128]{0:T(128)} %param.28) | copy-start | bytes 1540
  406.3 6.4 %copy-start.2 = (bf16[2,2,2,2,48,1152]{5,4,3,2,1,0:T(8,128)(2,1)S(1)}, bf16[2,2,2,2,48,1152]{5,4,3,2,1,0:T(8,128)(2,1)}, u32[]{:S(2)}) copy-start(bf16[2,2,2,2,48,1152]{5,4,3,2,1,0:T(8,128)(2,1)} %get-tuple-element.101) | copy-start | bytes 5308420
  413.0 1.3 copy-start.3
  413.0 2.9 copy-start.1
  413.2 3.6 copy-start
Sparse Core Ops, SparseCore 0:
  80.0 51.9 all-gather.2
  133.6 49.2 all-gather.4
  192.0 48.6 reduce-scatter.1

commit v5 on v4

--- a/solution.py
+++ b/solution.py
@@ -164,13 +164,44 @@
     )(counts, pair, pw_t, gain)
 
 
-def pair_bwd_kernel(rows, x_ref, bg_ref, a_ref, out_ref, *sums):
+def small_outputs(stacked, pw, gain, _, cond_gain_o, cond_bias_o, query_bias_o, pair_gain_o, pair_weight_o):
+    row = 0
+    for out in (cond_gain_o, cond_bias_o, query_bias_o):
+        for k in range(out.shape[0] // 128):
+            out[k * 128 : (k + 1) * 128] = stacked[row, :]
+            row += 1
+    moments = stacked[stacked.shape[0] - head_count :, :]
+    pair_gain_o[...] = jnp.sum(pw[...] * moments, axis=0)
+    pair_weight_o[...] = moments * gain[...]
+
+
+def pair_bwd_kernel(rows, n_pieces, x_ref, bg_ref, a_ref, *refs):
+    n_small = 4 if n_pieces else 0
+    smalls, refs = refs[:n_small], refs[n_small:]
+    pieces, (out_ref, *refs) = refs[:n_pieces], refs[n_pieces:]
+    laid, sums = refs[:n_pieces], refs[n_pieces:]
+    if n_pieces:
+        vectors, sums = sums, ()
+
+        @pl.when(pl.program_id(0) == 0)
+        def _():
+            small_outputs(*smalls, *vectors)
+
     if sums:
         q_ref, low_buf = sums
 
         @pl.when(pl.program_id(0) == 0)
         def _():
             q_ref[...] = jnp.zeros_like(q_ref)
+
+    if n_pieces:
+
+        @pl.when(lax.rem(pl.program_id(0), 2) == 0)
+        def _():
+            for piece, full in zip(pieces, laid):
+                groups, _, cols = piece.shape[0] // full.shape[0], piece.shape[1], piece.shape[2]
+                for g in range(groups):
+                    full[:, :, g * cols : (g + 1) * cols] = piece[g * full.shape[0] : (g + 1) * full.shape[0]].astype(f32)
 
     width = out_ref.shape[-1]
     heads, _, _, length = bg_ref.shape
@@ -190,37 +221,54 @@
         q_ref[...] += dot(grads.astype(bf16), low_buf[...])
 
 
-def pair_bwd(pair, bias_grad, high, low, with_sums):
+def pair_bwd_weights(rows, pw, gain):
+    rows = 8 if rows % 8 == 0 else rows
+    heads, width = pw.shape
+    scaled = pw * gain
+    centered = scaled - jnp.mean(scaled, axis=-1, keepdims=True)
+    high = centered.astype(bf16)
+    low = (centered - high.astype(f32)).astype(bf16)
+    eye = jnp.eye(rows, dtype=bf16)
+    both = jnp.stack([high, low])
+    weights = (both[:, :, None, None, :] * eye[None, None, :, :, None]).reshape(2 * heads * rows, rows * width)
+    return weights
+
+
+def pair_bwd(pair, bias_grad, weights, totals=(), heights=(), smalls=(), sizes=()):
+    with_sums = not totals
+    totals = [t.reshape(16, 48, t.shape[-1]) for t in totals]
+    vectors = [jax.ShapeDtypeStruct(shape, f32) for shape in sizes]
+    laid = [jax.ShapeDtypeStruct((h // 48, 48, 16 * 48 // h * t.shape[2]), f32) for t, h in zip(totals, heights)]
+
     _, total, length, width = pair.shape
     rows = 8 if total % 8 == 0 else total
     steps = total // rows
     heads = bias_grad.shape[0]
-    eye = jnp.eye(rows, dtype=bf16)
-    both = jnp.stack([high, low])
-    weights = (both[:, :, None, None, :] * eye[None, None, :, :, None]).reshape(2 * heads * rows, rows * width)
     grad, *moments = pl.pallas_call(
-        functools.partial(pair_bwd_kernel, rows),
+        functools.partial(pair_bwd_kernel, rows, len(totals)),
         grid=(2 * steps,),
         in_specs=[
             pl.BlockSpec((1, rows, length, width), lambda i: (i // steps, i % steps, 0, 0)),
             pl.BlockSpec((heads, 1, rows, length), lambda i: (0, i // steps, i % steps, 0)),
             whole(weights),
-        ],
-        out_specs=[
-            pl.BlockSpec((1, rows, length, width), lambda i: (i // steps, i % steps, 0, 0)),
-            pl.BlockSpec((heads * rows, rows * width), lambda i: (0, 0)),
-        ][: 1 + with_sums],
-        out_shape=[
-            jax.ShapeDtypeStruct(pair.shape, f32),
-            jax.ShapeDtypeStruct((heads * rows, rows * width), f32),
-        ][: 1 + with_sums],
+        ]
+        + [whole(a) for a in smalls]
+        + [pl.BlockSpec((16, 16, t.shape[2]), lambda i: (0, i // 2, 0)) for t in totals],
+        out_specs=[pl.BlockSpec((1, rows, length, width), lambda i: (i // steps, i % steps, 0, 0))]
+        + [pl.BlockSpec((t.shape[0], 16, t.shape[2]), lambda i: (0, i // 2, 0)) for t in laid]
+        + [whole(a) for a in vectors]
+        + [pl.BlockSpec((heads * rows, rows * width), lambda i: (0, 0))] * with_sums,
+        out_shape=[jax.ShapeDtypeStruct(pair.shape, f32)]
+        + laid
+        + vectors
+        + [jax.ShapeDtypeStruct((heads * rows, rows * width), f32)] * with_sums,
         scratch_shapes=[pltpu.VMEM((length, rows * width), bf16)][:with_sums],
         compiler_params=params(),
         cost_estimate=pl.CostEstimate(flops=2 * pair.size * 500, bytes_accessed=pair.size * 6, transcendentals=pair.size),
         name="pair_bwd",
-    )(pair, bias_grad, weights)
-    if not moments:
-        return grad, None
+    )(pair, bias_grad, weights, *smalls, *totals)
+    if totals:
+        return grad, [m.reshape(-1, m.shape[2]) for m in moments[: len(totals)]], moments[len(totals) :]
     moments = moments[0].reshape(heads, rows, rows, width)
     return grad, sum(moments[:, r, r] for r in range(rows))
 
@@ -327,11 +375,12 @@
 
     for m in movers[3:]:
         m.advance(1)
-    send_bias()
     for k in range(2, 5):
         for m in movers:
             if k <= len(m.order) + 1:
                 m.advance(k)
+        if k == 2:
+            send_bias()
     keep.wait()
     for copy in sent:
         copy.wait()
@@ -598,7 +647,7 @@
 
 def front(tok, cond, og, cgain, wc, cb, wq, qb, wo, slots):
     length, width = tok.shape
-    rb = 256
+    rb = 384
     peers, hd = head_count // slots, width // head_count
     small = jax.ShapeDtypeStruct((length, width), bf16)
     payload = jax.ShapeDtypeStruct((peers, 4 * slots, hd, length), bf16)
@@ -668,7 +717,7 @@
 
 def transition(tok, cond, og, cgain, wc, cb, wu, wd):
     length, width = tok.shape
-    rb = 256
+    rb = 384
     cs, mw = cond.shape[1], cb.shape[1]
     ff2 = wu.shape[1]
 
@@ -699,8 +748,8 @@
 def back_kernel(slots, *refs):
     ys = refs[:slots]
     (
-        sg, gg, s1, g1, part, u2, dcond2, tok, cond, og, cgain, wc, wq, wo,
-        out_o, tg_o, cg_o, gated_o, ga_o, gp_o, ml_o, qbg_o, cbg_o, cgg_o,
+        sg, gg, s1, g1, part, u2, dcond2, tok, cond, og, cbg2, cgain, wc, wq, wo,
+        out_o, tg_o, cg_o, gated_o, ga_o, gp_o, ml_o, small_o,
     ) = refs[slots:]
     rb, width = tok.shape
     hd = width // head_count
@@ -736,20 +785,28 @@
     cx, cscale = norm_parts(cond[...].astype(f32))
     cg_o[...] = norm_back(cx, dcond * cgain[...], cscale)
 
-    @pl.when(pl.program_id(0) == 0)
+    step = pl.program_id(0)
+
+    @pl.when(step == 0)
     def _():
-        qbg_o[...] = jnp.zeros_like(qbg_o)
-        cbg_o[...] = jnp.zeros_like(cbg_o)
-        cgg_o[...] = jnp.zeros_like(cgg_o)
-
-    qbg_o[...] += jnp.sum(dq, axis=0, keepdims=True)
-    cbg_o[...] += jnp.sum(grads, axis=0, keepdims=True)
-    cgg_o[...] += jnp.sum(dcond * cx, axis=0, keepdims=True)
-
-
-def back(ys, sg, gg, s1, g1, part, u2, dcond2, tok, cond, og, cgain, wc, wq, wo):
+        small_o[...] = jnp.zeros_like(small_o)
+
+    row = 0
+    last = jnp.where(step == pl.num_programs(0) - 1, 1.0, 0.0)
+    for values in (
+        jnp.sum(dcond * cx, axis=0, keepdims=True),
+        jnp.sum(grads, axis=0, keepdims=True),
+        cbg2[...] * last,
+        jnp.sum(dq, axis=0, keepdims=True),
+    ):
+        for k in range(values.shape[1] // 128):
+            small_o[row : row + 1, :] += values[:, k * 128 : (k + 1) * 128]
+            row += 1
+
+
+def back(ys, sg, gg, s1, g1, part, u2, dcond2, tok, cond, og, cbg2, cgain, wc, wq, wo):
     length, width = tok.shape
-    rb = 256
+    rb = 384
     cs, mw = cond.shape[1], wc.shape[1] // 2
     rows = (sg, gg, s1, g1, part, u2, dcond2, tok, cond, og)
     consts = (wq, wo)
@@ -760,14 +817,15 @@
     shapes = [
         out(width, f32), out(width, f32), out(cs, f32), out(width, bf16), out(width, bf16), out(wq.shape[1], bf16), out(mw, bf16),
     ]
-    small = [jax.ShapeDtypeStruct((1, w), f32) for w in (width, mw, cs)]
+    used = (width + 2 * mw + cs) // 128
+    small = [jax.ShapeDtypeStruct((-(-used // 8) * 8 + head_count, 128), f32)]
     return pl.pallas_call(
         functools.partial(back_kernel, len(ys)),
         grid_spec=pl.GridSpec(
             grid=(length // rb,),
             in_specs=[pl.BlockSpec(y.shape[:3] + (rb,), lambda i: (0, 0, 0, i)) for y in ys]
             + [row_spec(a, rb) for a in rows]
-            + [whole(cgain)]
+            + [whole(cbg2), whole(cgain)]
             + [half_spec(wc, 0)]
             + [whole(a) for a in consts],
             out_specs=[row_spec(s, rb) for s in shapes] + [pl.BlockSpec(s.shape, lambda i: (0, 0)) for s in small],
@@ -776,7 +834,7 @@
         compiler_params=params(),
         cost_estimate=pl.CostEstimate(flops=2 * length * width * width * 7, bytes_accessed=40 << 20, transcendentals=length * width),
         name="back",
-    )(*ys, *rows, cgain, wc, *consts)
+    )(*ys, *rows, cbg2, cgain, wc, *consts)
 
 
 def wgrad_kernel(steps, lhs, *refs):
@@ -819,13 +877,6 @@
         cost_estimate=pl.CostEstimate(flops=2 * length * k * n, bytes_accessed=2 * (length * (k + n) + k * n), transcendentals=0),
         name="wgrad",
     )(lhs, *rhs)
-
-
-def laid_out(pieces, rows):
-    cols = pieces.shape[-1]
-    row_groups = rows // 48
-    blocks = pieces.reshape(16 // row_groups, rows, cols).astype(f32)
-    return jnp.concatenate([blocks[t] for t in range(blocks.shape[0])], axis=1)
 
 
 class Reducer:
@@ -1213,6 +1264,8 @@
         wc, wq, wo, wu, wd = [lax.all_gather(w, "fsdp", axis=0, tiled=True) for w in matrices]
     biases = [spread(spreads[:, t]) for t in range(slots)]
 
+    pw = pair_weight.astype(f32).T
+    bwd_weights = pair_bwd_weights(rows, pw, pair_gain)
     tok, cnd, og = tokens[0], cond[0], out_grad[0]
     cgain = cond_gain[None]
     x, sg, gg, s1, g1, first = front(
@@ -1259,7 +1312,7 @@
 
     if direct:
         early = [wgrad(second, hid), wgrad(act, gt)]
-        x, *early = lax.optimization_barrier((x, *early))
+        x, bwd_weights, *early = lax.optimization_barrier((x, bwd_weights, *early))
     else:
         up_total, down_total = reduced([dot_tn(second, hid).astype(bf16), dot_tn(act, gt).astype(bf16)])
 
@@ -1278,8 +1331,8 @@
         mine = lax.psum_scatter(bg, "up", scatter_dimension=0, tiled=True)
         bias_grads.append(mine.reshape(2, members * rows, length))
 
-    block_out, tokens_grad, cond_grad, gated, ga, gp, ml1, qbg, cbg1, cgg = back(
-        ys, sg, gg, s1, g1, part, u2, dcond2, tok, cnd, og, cgain, wc, wq, wo
+    block_out, tokens_grad, cond_grad, gated, ga, gp, ml1, stacked = back(
+        ys, sg, gg, s1, g1, part, u2, dcond2, tok, cnd, og, cbg2, cgain, wc, wq, wo
     )
     if not direct:
         ml = jnp.concatenate([ml1, ml2], axis=1)
@@ -1287,47 +1340,43 @@
             [dot_tn(first, gp).astype(bf16), dot_tn(gated, ga).astype(bf16), dot_tn(cn, ml).astype(bf16)]
         )
 
-    pieces = [cgg, cbg1, cbg2, qbg]
-    stacked = jnp.concatenate([p.reshape(-1, 128) for p in pieces], axis=0)
     if direct:
-        height = -(-stacked.shape[0] // 8) * 8 + head_count
-        stacked = jnp.pad(stacked, ((0, height - stacked.shape[0]), (0, 0)))
         stacked, *totals, bias_grad = reduce_all(
             early, (first, gp, cn, ml1, ml2, gated, ga), bias_grads[1], bias_grads[0], pair, stacked
         )
-        qkvg_total, cond_total, out_total, up_total, down_total = [
-            laid_out(p, w.shape[0]) for p, w in zip(totals, (qkvg_weight, cond_weight, out_weight, up_weight, down_weight))
-        ]
     else:
         stacked = lax.psum(stacked, ("up", "lo", "fsdp"))
         split = [b.reshape(2, members, rows, length).transpose(1, 0, 2, 3) for b in bias_grads]
         bias_grad = lax.all_to_all(jnp.stack(split, axis=1), plane, 0, 0, tiled=True)
     bias_grad = bias_grad.reshape(head_count, 2, rows, length)
-    pw = pair_weight.astype(f32).T
-    scaled = pw * pair_gain
-    centered = scaled - jnp.mean(scaled, axis=-1, keepdims=True)
-    high = centered.astype(bf16)
-    low = (centered - high.astype(f32)).astype(bf16)
-    pair_grad, moments = pair_bwd(pair, bias_grad, high, low, not direct)
+    if direct:
+        heights = [w.shape[0] for w in (qkvg_weight, cond_weight, out_weight, up_weight, down_weight)]
+        smalls = (stacked, pw, pair_gain[None], pair_gain[None])
+        sizes = (cond_gain.shape, cond_bias.shape, query_bias.shape, pair_gain.shape, pw.shape)
+        pair_grad, laid, vectors = pair_bwd(pair, bias_grad, bwd_weights, totals, heights, smalls, sizes)
+        vectors[4] = vectors[4].T
+        qkvg_total, cond_total, out_total, up_total, down_total = laid
+    else:
+        pair_grad, moments = pair_bwd(pair, bias_grad, bwd_weights)
     moments = stacked[-head_count:] if direct else lax.psum(moments, ("up", "lo", "fsdp"))
-    small = stacked.reshape(-1)
-    ends = [0]
-    for p in pieces:
-        ends.append(ends[-1] + p.size)
-    small = [small[a:b] for a, b in zip(ends[:-1], ends[1:])]
+    if not direct:
+        small = stacked.reshape(-1)
+        ends = [0, cond_gain.size, cond_gain.size + cond_bias.size, cond_gain.size + cond_bias.size + query_bias.size]
+        vectors = [small[a:b] for a, b in zip(ends[:-1], ends[1:])]
+        vectors += [jnp.sum(pw * moments, axis=0), (moments * pair_gain).T]
     return (
         block_out[None],
         tokens_grad[None],
         cond_grad[None],
         pair_grad,
-        small[0],
+        vectors[0],
         cond_total,
-        jnp.concatenate([small[1], small[2]]),
+        vectors[1],
         qkvg_total,
-        small[3],
+        vectors[2],
         out_total,
-        jnp.sum(pw * moments, axis=0),
-        (moments * pair_gain).T,
+        vectors[3],
+        vectors[4],
         up_total,
         down_total,
     )

time: 459 us -> 437 us (0.952)
  other arithmetic: 17.3 us -> 2.51 us
  local copies, waits for them, and re-layouts: 15.9 us -> 8.17 us
    concatenate x6 -> x0, other arithmetic: 9.72 us -> none  [the longest x4 8.49 us: laid_out(): return jnp.concatenate([blocks[t] for t in range(blocks.shape[0])], axis=1)]
    pallas_call x1, Pallas kernels: 17.1 us -> 23.5 us  [pair_bwd(): pl.pallas_call(functools.partial(pair_bwd_kernel, rows, len(totals)), gri...]
    slice x5 -> x0, local copies, waits for them, and re-layouts: 5.84 us -> none  [the longest x3 3.41 us: on_device(): small = [small[a:b] for a, b in zip(ends[:-1], ends[1:])]]
  transfers between devices with their start and end apart: 4 -> 4, of which waited for: 1 -> 1; matrix products, arithmetic and copies ran while one was open for 1% -> 1% of each run, Pallas kernels for 33% -> 35%
where the time goes in v5:
time: 437 us; the launch traced here: 429 us
  Pallas kernels  388 us (89%)
  between operations  14.4 us (3%)
  waiting for transfers between devices  10.9 us (2%)
  local copies, waits for them, and re-layouts  8.17 us (2%)
  starting transfers between devices  5.34 us (1%)
    pallas_call x1, Pallas kernels, reduce_all(): pl.pallas_call(functools.partial(reduce_kernel, None), out_shape=[jax.Sha...  149 us
    pallas_call x2, Pallas kernels, sending_attention(): pl.pallas_call(functools.partial(sending_attn_kernel, length // 2, slot),...  76.9 us
    pallas_call x1, Pallas kernels, start(): pl.pallas_call(functools.partial(start_kernel, n), in_specs=[pl.BlockSpec...  64.7 us
    pallas_call x1, Pallas kernels, transition(): pl.pallas_call(trans_kernel, grid_spec=pl.GridSpec(grid=(length // rb,),...  26.4 us
    pallas_call x1, Pallas kernels, pair_bwd(): pl.pallas_call(functools.partial(pair_bwd_kernel, rows, len(totals)), gri...  23.5 us
    pallas_call x1, Pallas kernels, back(): pl.pallas_call(functools.partial(back_kernel, len(ys)), grid_spec=pl.Grid...  20.8 us
    pallas_call x2, Pallas kernels, wgrad(): pl.pallas_call(functools.partial(wgrad_kernel, each), grid=(steps,), in_s...  13.2 us
    pallas_call x1, Pallas kernels, front(): pl.pallas_call(front_kernel, grid_spec=pl.GridSpec(grid=(length // rb,),...  13.1 us
  transfers between devices with their start and end apart: 4, of which 1 were waited for; matrix products, arithmetic and copies ran while one was open for 1% of the time, Pallas kernels for 35%

profile of v5, /device:TPU:0, one launch (start us, length us, event | category | flops | bytes accessed | tf_op | source)
XLA Modules:
  0.0 429.0 jit_solution(9100077615930117859)
XLA Ops:
  7.2 0.0 all-gather.3.cloned.1.call-start
  7.2 0.8 multiply_bitcast_fusion
  8.1 0.8 copy.37.pw
  8.9 1.2 tile.8
  10.1 64.7 %start.1 = (bf16[384,4608]{1,0:T(8,128)(2,1)}, bf16[768,3072]{1,0:T(8,128)(2,1)}, bf16[768,768]{1,0:T(8,128)(2,1)}, bf16[768,3072]{1,0:T(8,128)(2,1)}, bf16[1536...) custom-call(s32[2]{0:T(128)} %counts.1, bf16[1024,128]{1,0:T(8,128)(2,1)} %copy.37.pw, f32[1,256]{1,0:T(1,128)} %bitcast.82, ...), custom_call_target="tpu_custom_call" | custom-call | tf_op jit(solution)/shard_map/start/pallas_call | solution.py:397
  74.8 1.3 fusion.3
  76.2 0.9 copy.38
  77.1 0.6 broadcast_in_dim.14.cgain.refs_13_
  77.6 0.6 broadcast_in_dim.30.cb
  78.3 0.6 broadcast_in_dim.31.qb
  78.8 13.1 %front.1 = (bf16[8,8,48,768]{3,2,1,0:T(8,128)(2,1)}, bf16[768,768]{1,0:T(8,128)(2,1)}, bf16[768,768]{1,0:T(8,128)(2,1)}, bf16[768,768]{1,0:T(8,128)(2,1)}, bf16[...) custom-call(bf16[768,768]{1,0:T(8,128)(2,1)} %bitcast.66, bf16[768,384]{1,0:T(8,128)(2,1)} %bitcast.75, ...), custom_call_target="tpu_custom_call" | custom-call | flops 6341787648 | bytes 20971520 | tf_op jit(solution)/shard_map/front/pallas_call | solution.py:654
  91.9 4.8 %all-to-all-start = ((bf16[8,8,48,768]{3,2,1,0:T(8,128)(2,1)}), bf16[8,8,48,768]{3,2,1,0:T(8,128)(2,1)}, u32[]{:S(2)}, u32[]{:S(2)}) async-start(bf16[8,8,48,768]{3,2,1,0:T(8,128)(2,1)} %get-tuple-element.73), calls=%async_computation | async-start | bytes 9437184 | tf_op jit(solution)/shard_map/all_to_all | solution.py:1274
  96.7 0.0 all-gather.5.cloned.1.call-start
  96.8 0.9 copy.39
  97.7 0.5 reduce-scatter.2.cloned.1.call-start
  98.2 0.1 multiply_reduce_fusion
  98.3 0.1 fusion
  98.4 0.6 broadcast_in_dim.32.cb
  99.0 0.6 dynamic_slice.3.owner_ref
  99.6 26.4 %transition.1 = (f32[768,768]{1,0:T(8,128)}, bf16[768,768]{1,0:T(8,128)(2,1)}, f32[768,384]{1,0:T(8,128)}, bf16[768,2304]{1,0:T(8,128)(2,1)}, bf16[768,384]{1,0:...) custom-call(bf16[768,768]{1,0:T(8,128)(2,1)} %bitcast.67, ...), custom_call_target="tpu_custom_call" | custom-call | flops 13589544960 | bytes 41943040 | tf_op jit(solution)/shard_map/transition/pallas_call | solution.py:731
  126.0 5.4 %wgrad.3.refs_1_ = bf16[2,16,48,768]{3,2,1,0:T(8,128)(2,1)} custom-call(bf16[768,1536]{1,0:T(8,128)(2,1)} %get-tuple-element.78.lhs, bf16[768,768]{1,0:T(8,128)(2,1)} %get-tuple-element.79.refs_0_), custom_call_target="tpu_custom_call" | custom-call | flops 1811939328 | bytes 5898240 | tf_op jit(solution)/shard_map/wgrad/pallas_call | solution.py:869
  131.4 0.9 broadcast_multiply_fusion
  132.3 7.8 %wgrad.2.refs_0_ = bf16[2,16,48,1536]{3,2,1,0:T(8,128)(2,1)} custom-call(bf16[768,768]{1,0:T(8,128)(2,1)} %get-tuple-element.76.lhs, bf16[768,3072]{1,0:T(8,128)(2,1)} %get-tuple-element.77.refs_0_), custom_call_target="tpu_custom_call" | custom-call | flops 3623878656 | bytes 10616832 | tf_op jit(solution)/shard_map/wgrad/pallas_call | solution.py:869
  140.1 10.8 %all-to-all-done.x_ref = bf16[8,8,48,768]{3,2,1,0:T(8,128)(2,1)} async-done(((bf16[8,8,48,768]{3,2,1,0:T(8,128)(2,1)}), bf16[8,8,48,768]{3,2,1,0:T(8,128)(2,1)}, u32[]{:S(2)}, u32[]{:S(2)}) %all-to-all-start) | async-done | bytes 4718624 | tf_op jit(solution)/shard_map/all_to_all | solution.py:1274
  150.9 38.5 %attention_and_send.2 = (bf16[8,4,48,768]{3,2,1,0:T(8,128)(2,1)}, bf16[4,2,192,768]{3,2,1,0:T(8,128)(2,1)}) custom-call(s32[8]{0:T(128)} %dynamic_slice.3.owner_ref, bf16[8,8,48,768]{3,2,1,0:T(8,128)(2,1)} %all-to-all-done.x_ref, bf16[4,2,192,768]{3,2,1,0:T(8,128)(2,1)} %all-gather.3.cloned.1.call-done.bias_ref), custom_call_target="tpu_custom_call" | custom-call | flops 14495514624 | bytes 9437184 | tf_op jit(solution)/shard_map/attention_and_send/pallas_call | solution.py:557
  189.4 0.0 reduce-scatter.2.cloned.1.call-update
  189.4 0.6 convert_bitcast_fusion.refs_1_
  190.0 38.4 %attention_and_send.3 = (bf16[8,4,48,768]{3,2,1,0:T(8,128)(2,1)}, bf16[4,2,192,768]{3,2,1,0:T(8,128)(2,1)}) custom-call(s32[8]{0:T(128)} %dynamic_slice.3.owner_ref, bf16[8,8,48,768]{3,2,1,0:T(8,128)(2,1)} %all-to-all-done.x_ref, bf16[4,2,192,768]{3,2,1,0:T(8,128)(2,1)} %all-gather.5.cloned.1.call-done.bias_ref), custom_call_target="tpu_custom_call" | custom-call | flops 14495514624 | bytes 9437184 | tf_op jit(solution)/shard_map/attention_and_send/pallas_call | solution.py:557
  228.5 20.8 %back.1 = (f32[768,768]{1,0:T(8,128)}, f32[768,768]{1,0:T(8,128)}, f32[768,384]{1,0:T(8,128)}, bf16[768,768]{1,0:T(8,128)(2,1)}, bf16[768,768]{1,0:T(8,128)(2,1)...) custom-call(bf16[8,4,48,768]{3,2,1,0:T(8,128)(2,1)} %get-tuple-element.82.refs_0_, ...), custom_call_target="tpu_custom_call" | custom-call | flops 6341787648 | bytes 41943040 | tf_op jit(solution)/shard_map/back/pallas_call | solution.py:822
  249.3 0.0 reduce-scatter.2.cloned.1.call-done
  249.3 149.2 %reduce_grads.1 = (f32[64,128]{1,0:T(8,128)}, bf16[2,2,2,2,48,1536]{5,4,3,2,1,0:T(8,128)(2,1)}, bf16[2,2,2,2,48,1152]{5,4,3,2,1,0:T(8,128)(2,1)}, bf16[2,2,2,2,4...) custom-call(bf16[2,16,48,1536]{3,2,1,0:T(8,128)(2,1)} %wgrad.2.refs_, ...), custom_call_target="tpu_custom_call" | custom-call | tf_op jit(solution)/shard_map/reduce_grads/pallas_call | solution.py:1192
  398.5 23.5 %pair_bwd.1 = (f32[2,24,768,128]{3,2,1,0:T(8,128)}, f32[8,48,3072]{2,1,0:T(8,128)}, f32[4,48,4608]{2,1,0:T(8,128)}, f32[8,48,768]{2,1,0:T(8,128)}, f32[8,48,3072...) custom-call(bf16[2,24,768,128]{3,2,1,0:T(8,128)(2,1)} %x_ref.1, ...), custom_call_target="tpu_custom_call" | custom-call | flops 4718592000 | bytes 28311552 | tf_op jit(solution)/shard_map/pair_bwd/pallas_call | solution.py:247
  (21 shorter events, 0.1 us)
Async XLA Ops:
  7.2 143.7 %all-gather.3.cloned.1.call-start = ((), (), s32[]{:S(2)}) async-start(), calls=%async_computation.2 | async-start | bytes 2949120 | tf_op jit(solution)/shard_map/all_gather | solution.py:1253
  74.8 2.3 copy-start.4
  74.8 2.8 copy-start.1
  74.8 3.4 copy-start.3
  91.9 6.3 %copy-start = (bf16[128,16]{0,1:T(8,128)(2,1)S(1)}, bf16[128,16]{0,1:T(8,128)(2,1)}, u32[]{:S(2)}) copy-start(bf16[128,16]{0,1:T(8,128)(2,1)} %param.29) | copy-start | bytes 12292
  91.9 6.3 %copy-start.2 = (f32[128]{0:T(128)S(1)}, f32[128]{0:T(128)}, u32[]{:S(2)}) copy-start(f32[128]{0:T(128)} %param.28) | copy-start | bytes 1540
  91.9 7.1 %copy-start.5 = (s32[32]{0:T(128)S(1)}, s32[32]{0:T(128)}, u32[]{:S(2)}) copy-start(s32[32]{0:T(128)} %param.20) | copy-start | bytes 388
  91.9 59.0 %all-to-all-start = ((bf16[8,8,48,768]{3,2,1,0:T(8,128)(2,1)}), bf16[8,8,48,768]{3,2,1,0:T(8,128)(2,1)}, u32[]{:S(2)}, u32[]{:S(2)}) async-start(bf16[8,8,48,768]{3,2,1,0:T(8,128)(2,1)} %get-tuple-element.73), calls=%async_computation | async-start | bytes 9437184 | tf_op jit(solution)/shard_map/all_to_all | solution.py:1274
  96.7 93.3 %all-gather.5.cloned.1.call-start = ((), (), s32[]{:S(2)}) async-start(), calls=%async_computation.3 | async-start | bytes 2949120 | tf_op jit(solution)/shard_map/all_gather | solution.py:1253
  97.7 151.7 %reduce-scatter.2.cloned.1.call-start = ((), (), s32[]{:S(2)}) async-start(), calls=%async_computation.4 | async-start | bytes 2949120 | tf_op jit(solution)/shard_map/reduce_scatter | solution.py:1331
Sparse Core Ops, SparseCore 0:
  77.2 50.7 all-gather.2
  129.6 49.2 all-gather.4
  189.5 47.4 reduce-scatter.1

commit v6 on v5

--- a/solution.py
+++ b/solution.py
@@ -58,12 +58,12 @@
 SAMPLE_ORDER = (("x",), ("y",), ("x", "y"), ("c", "x"), ("c", "y"), ("c", "x", "y"), ("c",), ())
 SUM_ORDERS = (
     ("c", "x", "y", "z0", "z1"),
-    ("c", "x", "z0", "y", "z1"),
+    ("c", "x", "y", "z1", "z0"),
     ("c", "y", "x", "z0", "z1"),
-    ("c", "z0", "y", "z1", "x"),
+    ("c", "z0", "x", "y", "z1"),
 )
 COPY_ORDERS = (
-    ("x", "z0", "z1", "c"),
+    ("z0", "x", "z1", "c"),
     ("z0", "z1", "x", "c"),
     ("z1", "x", "z0", "c"),
     ("z1", "z0", "x", "c"),
@@ -194,14 +194,10 @@
         def _():
             q_ref[...] = jnp.zeros_like(q_ref)
 
-    if n_pieces:
-
-        @pl.when(lax.rem(pl.program_id(0), 2) == 0)
-        def _():
-            for piece, full in zip(pieces, laid):
-                groups, _, cols = piece.shape[0] // full.shape[0], piece.shape[1], piece.shape[2]
-                for g in range(groups):
-                    full[:, :, g * cols : (g + 1) * cols] = piece[g * full.shape[0] : (g + 1) * full.shape[0]].astype(f32)
+    for piece, full in zip(pieces, laid):
+        groups, cols = piece.shape[0] // full.shape[0], piece.shape[2]
+        for g in range(groups):
+            full[:, :, g * cols : (g + 1) * cols] = piece[g * full.shape[0] : (g + 1) * full.shape[0]].astype(f32)
 
     width = out_ref.shape[-1]
     heads, _, _, length = bg_ref.shape
@@ -253,9 +249,9 @@
             whole(weights),
         ]
         + [whole(a) for a in smalls]
-        + [pl.BlockSpec((16, 16, t.shape[2]), lambda i: (0, i // 2, 0)) for t in totals],
+        + [pl.BlockSpec((16, 8, t.shape[2]), lambda i: (0, i, 0)) for t in totals],
         out_specs=[pl.BlockSpec((1, rows, length, width), lambda i: (i // steps, i % steps, 0, 0))]
-        + [pl.BlockSpec((t.shape[0], 16, t.shape[2]), lambda i: (0, i // 2, 0)) for t in laid]
+        + [pl.BlockSpec((t.shape[0], 8, t.shape[2]), lambda i: (0, i, 0)) for t in laid]
         + [whole(a) for a in vectors]
         + [pl.BlockSpec((heads * rows, rows * width), lambda i: (0, 0))] * with_sums,
         out_shape=[jax.ShapeDtypeStruct(pair.shape, f32)]
@@ -1213,24 +1209,22 @@
 
 
 late_plan = (
-    (0, 0, 768, 2, 3),
-    (0, 768, 768, 2, 0),
-    (1, 0, 640, 0, 2),
-    (1, 640, 512, 3, 3),
-    (2, 0, 384, 2, 3),
+    (0, 0, 1024, 3, 1),
+    (0, 1024, 512, 0, 3),
+    (1, 0, 640, 0, 0),
+    (1, 640, 512, 2, 1),
+    (2, 0, 384, 2, 2),
 )
 early_plan = (
     (0, 0, 768, 1, 3),
-    (0, 768, 768, 0, 3),
-    (1, 0, 384, 0, 2),
-    (1, 384, 384, 2, 1),
+    (0, 768, 768, 0, 2),
+    (1, 0, 768, 2, 2),
 )
 schedule = (
-    8, 6, 3, 8, 4, 6, 1, 4, 5, 5, 7, 1, 4, 3, 0, -1, 2, 0, 4, 6, 1, 2, 8, 5,
-    7, 3, 8, 3, 6, 1, 5, 4, 7, 8, 5, 0, 2, 8, 3, 4, 7, 3, -1, 4, 6, 3, 1, 0,
-    7, 6, 2, 3, 5, 6, 1, 7, -1, 8, 5, 6, 1, 2, 0, 7, -1, 4, 2, -2, 0, 7, 8, -2,
-    2, 4, 5, 6, 1, 0, 3, 0, 2, 8, 4, 5, 7, 6, -2, 7, 5, 8, 1, -2, 3, 0, -2, 2,
-    -2, 1, 0, 2,
+    5, 2, 7, 5, 0, 2, 6, 7, 4, 1, 4, 0, 5, -1, 6, 3, 2, 3, 1, 2, 6, 7, 4, 5,
+    3, 4, 0, 2, 6, 5, 1, 4, 1, -1, 5, 6, 7, 3, 6, 1, 5, 7, 3, 2, 0, 6, 1, 3,
+    7, 1, 0, 5, 6, -1, 4, 0, 5, 3, 7, 2, -1, 4, -2, 0, 7, 3, -2, 1, 3, 0, -2, 2,
+    5, 6, 1, 4, 7, 6, 4, -2, 3, 0, -2, 2, -2, 2, 0, 4, 1, 7,
 )
 
 

time: 437 us -> 435 us (level)
  no operation moved by 1% of the time
where the time goes in v6:
time: 435 us; the launch traced here: 427 us
  Pallas kernels  386 us (89%)
  between operations  14.4 us (3%)
  waiting for transfers between devices  10.9 us (3%)
  local copies, waits for them, and re-layouts  8.17 us (2%)
  starting transfers between devices  5.34 us (1%)
    pallas_call x1, Pallas kernels, reduce_all(): pl.pallas_call(functools.partial(reduce_kernel, None), out_shape=[jax.Sha...  148 us
    pallas_call x2, Pallas kernels, sending_attention(): pl.pallas_call(functools.partial(sending_attn_kernel, length // 2, slot),...  76.9 us
    pallas_call x1, Pallas kernels, start(): pl.pallas_call(functools.partial(start_kernel, n), in_specs=[pl.BlockSpec...  64.7 us
    pallas_call x1, Pallas kernels, transition(): pl.pallas_call(trans_kernel, grid_spec=pl.GridSpec(grid=(length // rb,),...  26.4 us
    pallas_call x1, Pallas kernels, pair_bwd(): pl.pallas_call(functools.partial(pair_bwd_kernel, rows, len(totals)), gri...  22.8 us
    pallas_call x1, Pallas kernels, back(): pl.pallas_call(functools.partial(back_kernel, len(ys)), grid_spec=pl.Grid...  20.8 us
    pallas_call x2, Pallas kernels, wgrad(): pl.pallas_call(functools.partial(wgrad_kernel, each), grid=(steps,), in_s...  13.2 us
    pallas_call x1, Pallas kernels, front(): pl.pallas_call(front_kernel, grid_spec=pl.GridSpec(grid=(length // rb,),...  13.1 us
  transfers between devices with their start and end apart: 4, of which 1 were waited for; matrix products, arithmetic and copies ran while one was open for 1% of the time, Pallas kernels for 35%

profile of v6, /device:TPU:0, one launch (start us, length us, event | category | flops | bytes accessed | tf_op | source)
XLA Modules:
  0.0 427.0 jit_solution(1579412266216560932)
XLA Ops:
  7.2 0.0 all-gather.3.cloned.1.call-start
  7.2 0.8 multiply_bitcast_fusion
  8.1 0.8 copy.37.pw
  8.9 1.2 tile.8
  10.1 64.7 %start.1 = (bf16[384,4608]{1,0:T(8,128)(2,1)}, bf16[768,3072]{1,0:T(8,128)(2,1)}, bf16[768,768]{1,0:T(8,128)(2,1)}, bf16[768,3072]{1,0:T(8,128)(2,1)}, bf16[1536...) custom-call(s32[2]{0:T(128)} %counts.1, bf16[1024,128]{1,0:T(8,128)(2,1)} %copy.37.pw, f32[1,256]{1,0:T(1,128)} %bitcast.82, ...), custom_call_target="tpu_custom_call" | custom-call | tf_op jit(solution)/shard_map/start/pallas_call | solution.py:393
  74.8 1.3 fusion.3
  76.2 0.9 copy.38
  77.1 0.6 broadcast_in_dim.14.cgain.refs_13_
  77.6 0.6 broadcast_in_dim.30.cb
  78.3 0.6 broadcast_in_dim.31.qb
  78.8 13.1 %front.1 = (bf16[8,8,48,768]{3,2,1,0:T(8,128)(2,1)}, bf16[768,768]{1,0:T(8,128)(2,1)}, bf16[768,768]{1,0:T(8,128)(2,1)}, bf16[768,768]{1,0:T(8,128)(2,1)}, bf16[...) custom-call(bf16[768,768]{1,0:T(8,128)(2,1)} %bitcast.66, bf16[768,384]{1,0:T(8,128)(2,1)} %bitcast.75, ...), custom_call_target="tpu_custom_call" | custom-call | flops 6341787648 | bytes 20971520 | tf_op jit(solution)/shard_map/front/pallas_call | solution.py:650
  91.9 4.8 %all-to-all-start = ((bf16[8,8,48,768]{3,2,1,0:T(8,128)(2,1)}), bf16[8,8,48,768]{3,2,1,0:T(8,128)(2,1)}, u32[]{:S(2)}, u32[]{:S(2)}) async-start(bf16[8,8,48,768]{3,2,1,0:T(8,128)(2,1)} %get-tuple-element.73), calls=%async_computation | async-start | bytes 9437184 | tf_op jit(solution)/shard_map/all_to_all | solution.py:1268
  96.7 0.0 all-gather.5.cloned.1.call-start
  96.8 0.9 copy.39
  97.7 0.5 reduce-scatter.2.cloned.1.call-start
  98.2 0.1 multiply_reduce_fusion
  98.3 0.1 fusion
  98.4 0.6 broadcast_in_dim.32.cb
  99.0 0.6 dynamic_slice.3.owner_ref
  99.6 26.4 %transition.1 = (f32[768,768]{1,0:T(8,128)}, bf16[768,768]{1,0:T(8,128)(2,1)}, f32[768,384]{1,0:T(8,128)}, bf16[768,2304]{1,0:T(8,128)(2,1)}, bf16[768,384]{1,0:...) custom-call(bf16[768,768]{1,0:T(8,128)(2,1)} %bitcast.67, ...), custom_call_target="tpu_custom_call" | custom-call | flops 13589544960 | bytes 41943040 | tf_op jit(solution)/shard_map/transition/pallas_call | solution.py:727
  126.0 5.4 %wgrad.3.refs_1_ = bf16[2,16,48,768]{3,2,1,0:T(8,128)(2,1)} custom-call(bf16[768,1536]{1,0:T(8,128)(2,1)} %get-tuple-element.78.lhs, bf16[768,768]{1,0:T(8,128)(2,1)} %get-tuple-element.79.refs_0_), custom_call_target="tpu_custom_call" | custom-call | flops 1811939328 | bytes 5898240 | tf_op jit(solution)/shard_map/wgrad/pallas_call | solution.py:865
  131.4 0.9 broadcast_multiply_fusion
  132.3 7.8 %wgrad.2.refs_0_ = bf16[2,16,48,1536]{3,2,1,0:T(8,128)(2,1)} custom-call(bf16[768,768]{1,0:T(8,128)(2,1)} %get-tuple-element.76.lhs, bf16[768,3072]{1,0:T(8,128)(2,1)} %get-tuple-element.77.refs_0_), custom_call_target="tpu_custom_call" | custom-call | flops 3623878656 | bytes 10616832 | tf_op jit(solution)/shard_map/wgrad/pallas_call | solution.py:865
  140.1 10.8 %all-to-all-done.x_ref = bf16[8,8,48,768]{3,2,1,0:T(8,128)(2,1)} async-done(((bf16[8,8,48,768]{3,2,1,0:T(8,128)(2,1)}), bf16[8,8,48,768]{3,2,1,0:T(8,128)(2,1)}, u32[]{:S(2)}, u32[]{:S(2)}) %all-to-all-start) | async-done | bytes 4718624 | tf_op jit(solution)/shard_map/all_to_all | solution.py:1268
  150.9 38.5 %attention_and_send.2 = (bf16[8,4,48,768]{3,2,1,0:T(8,128)(2,1)}, bf16[4,2,192,768]{3,2,1,0:T(8,128)(2,1)}) custom-call(s32[8]{0:T(128)} %dynamic_slice.3.owner_ref, bf16[8,8,48,768]{3,2,1,0:T(8,128)(2,1)} %all-to-all-done.x_ref, bf16[4,2,192,768]{3,2,1,0:T(8,128)(2,1)} %all-gather.3.cloned.1.call-done.bias_ref), custom_call_target="tpu_custom_call" | custom-call | flops 14495514624 | bytes 9437184 | tf_op jit(solution)/shard_map/attention_and_send/pallas_call | solution.py:553
  189.4 0.0 reduce-scatter.2.cloned.1.call-update
  189.4 0.6 convert_bitcast_fusion.refs_1_
  190.0 38.4 %attention_and_send.3 = (bf16[8,4,48,768]{3,2,1,0:T(8,128)(2,1)}, bf16[4,2,192,768]{3,2,1,0:T(8,128)(2,1)}) custom-call(s32[8]{0:T(128)} %dynamic_slice.3.owner_ref, bf16[8,8,48,768]{3,2,1,0:T(8,128)(2,1)} %all-to-all-done.x_ref, bf16[4,2,192,768]{3,2,1,0:T(8,128)(2,1)} %all-gather.5.cloned.1.call-done.bias_ref), custom_call_target="tpu_custom_call" | custom-call | flops 14495514624 | bytes 9437184 | tf_op jit(solution)/shard_map/attention_and_send/pallas_call | solution.py:553
  228.5 20.8 %back.1 = (f32[768,768]{1,0:T(8,128)}, f32[768,768]{1,0:T(8,128)}, f32[768,384]{1,0:T(8,128)}, bf16[768,768]{1,0:T(8,128)(2,1)}, bf16[768,768]{1,0:T(8,128)(2,1)...) custom-call(bf16[8,4,48,768]{3,2,1,0:T(8,128)(2,1)} %get-tuple-element.82.refs_0_, ...), custom_call_target="tpu_custom_call" | custom-call | flops 6341787648 | bytes 41943040 | tf_op jit(solution)/shard_map/back/pallas_call | solution.py:818
  249.3 0.0 reduce-scatter.2.cloned.1.call-done
  249.3 147.8 %reduce_grads.1 = (f32[64,128]{1,0:T(8,128)}, bf16[2,2,2,2,48,1536]{5,4,3,2,1,0:T(8,128)(2,1)}, bf16[2,2,2,2,48,1152]{5,4,3,2,1,0:T(8,128)(2,1)}, bf16[2,2,2,2,4...) custom-call(bf16[2,16,48,1536]{3,2,1,0:T(8,128)(2,1)} %wgrad.2.refs_, ...), custom_call_target="tpu_custom_call" | custom-call | tf_op jit(solution)/shard_map/reduce_grads/pallas_call | solution.py:1188
  397.2 22.8 %pair_bwd.1 = (f32[2,24,768,128]{3,2,1,0:T(8,128)}, f32[8,48,3072]{2,1,0:T(8,128)}, f32[4,48,4608]{2,1,0:T(8,128)}, f32[8,48,768]{2,1,0:T(8,128)}, f32[8,48,3072...) custom-call(bf16[2,24,768,128]{3,2,1,0:T(8,128)(2,1)} %x_ref.1, ...), custom_call_target="tpu_custom_call" | custom-call | flops 4718592000 | bytes 28311552 | tf_op jit(solution)/shard_map/pair_bwd/pallas_call | solution.py:243
  (21 shorter events, 0.1 us)
Async XLA Ops:
  7.2 143.7 %all-gather.3.cloned.1.call-start = ((), (), s32[]{:S(2)}) async-start(), calls=%async_computation.2 | async-start | bytes 2949120 | tf_op jit(solution)/shard_map/all_gather | solution.py:1247
  74.8 2.3 copy-start.4
  74.8 2.8 copy-start.1
  74.8 3.4 copy-start.3
  91.9 6.3 %copy-start = (bf16[128,16]{0,1:T(8,128)(2,1)S(1)}, bf16[128,16]{0,1:T(8,128)(2,1)}, u32[]{:S(2)}) copy-start(bf16[128,16]{0,1:T(8,128)(2,1)} %param.29) | copy-start | bytes 12292
  91.9 6.3 %copy-start.2 = (f32[128]{0:T(128)S(1)}, f32[128]{0:T(128)}, u32[]{:S(2)}) copy-start(f32[128]{0:T(128)} %param.28) | copy-start | bytes 1540
  91.9 7.1 %copy-start.5 = (s32[32]{0:T(128)S(1)}, s32[32]{0:T(128)}, u32[]{:S(2)}) copy-start(s32[32]{0:T(128)} %param.20) | copy-start | bytes 388
  91.9 59.0 %all-to-all-start = ((bf16[8,8,48,768]{3,2,1,0:T(8,128)(2,1)}), bf16[8,8,48,768]{3,2,1,0:T(8,128)(2,1)}, u32[]{:S(2)}, u32[]{:S(2)}) async-start(bf16[8,8,48,768]{3,2,1,0:T(8,128)(2,1)} %get-tuple-element.73), calls=%async_computation | async-start | bytes 9437184 | tf_op jit(solution)/shard_map/all_to_all | solution.py:1268
  96.7 93.3 %all-gather.5.cloned.1.call-start = ((), (), s32[]{:S(2)}) async-start(), calls=%async_computation.3 | async-start | bytes 2949120 | tf_op jit(solution)/shard_map/all_gather | solution.py:1247
  97.7 151.7 %reduce-scatter.2.cloned.1.call-start = ((), (), s32[]{:S(2)}) async-start(), calls=%async_computation.4 | async-start | bytes 2949120 | tf_op jit(solution)/shard_map/reduce_scatter | solution.py:1325
Sparse Core Ops, SparseCore 0:
  77.2 50.7 all-gather.2
  129.6 49.2 all-gather.4
  189.5 47.4 reduce-scatter.1
